TPU v7x, 256 devices: a whole 4x4x8 slice. The times are simulated.
256 devices in a mesh: dp: 8 (over z), expert: 2 (over core), tensor: 16 (over y, x).
Axes of the slice: x: 4, y: 4, z: 8, core: 2. Of those that a mesh axis runs over, the one named last changes fastest.
Arguments:
- tokens: bfloat16 [8192, 6144], P(('dp', 'expert'), 'tensor'), parts along dimension 0, may hold values from -6 to 6
- route_ids: int32 [8192, 2], P(('dp', 'expert')), parts along dimension 0, may hold values from 0 to 7, as said below
- route_gates: float32 [8192, 2], P(('dp', 'expert')), parts along dimension 0, may hold values from 0.2 to 1
- w_gate: bfloat16 [2, 6144, 8192], P('expert', None, 'tensor'), may hold values from -0.078125 to 0.078125
- w_up: bfloat16 [2, 6144, 8192], P('expert', None, 'tensor'), may hold values from -0.078125 to 0.078125
- w_down: bfloat16 [2, 8192, 6144], P('expert', 'tensor'), may hold values from -0.0625 to 0.0625
Outputs:
- mixed: bfloat16 [8192, 6144], P(('dp', 'expert'), 'tensor'), parts along dimension 0
There are 8 independent parts, one for each index of `dp`. A program takes and returns all parts, laid end to end along the dimension named above; an argument that names none is the same for every part. Nothing has to cross between parts.
Inputs may be any that keep to these rules, and one draw needn't show every extreme that they name: `route_ids`: in each aligned block of 512 rows (the rows of one expert index) every expert is named at most 256 times, and one expert below 2, the same in all blocks of a replica, is named exactly 256 times in every block. The 2 experts of a row differ.
All inputs are finite; a program needn't handle non-finite values.
Results may differ from a plain program's by a relative error of at most 0.0057.
Values may be sent and summed in bfloat16 or wider, within the bound.
No kernel may reach another device: no remote copies, remote signals or barrier semaphores. Data moves between devices by JAX's collectives and lax.ppermute only.
A program may use at most 128 MiB of HBM per device.

v0:
```python
import jax
import jax.numpy as jnp
from jax import lax
from jax.sharding import PartitionSpec as P


def body(tokens, route_ids, route_gates, w_gate, w_up, w_down):
    tok_rows, width_dev = tokens.shape
    picks = route_ids.shape[1]
    n_source = lax.axis_size("expert")
    local_count = w_gate.shape[0]
    n_flight = n_source * local_count
    capacity = tok_rows // 2
    flat_ids = route_ids.reshape(-1)
    onehot = (flat_ids[:, None] == jnp.arange(n_flight, dtype=jnp.int32)[None, :]).astype(jnp.int32)
    earlier = jnp.cumsum(onehot, axis=0) - onehot
    position = jnp.sum(earlier * onehot, axis=1)
    in_window = flat_ids < n_flight
    slots = jnp.where(in_window, flat_ids * capacity + position, n_flight * capacity)
    repeated = jnp.repeat(tokens, picks, axis=0)
    buffer = (
        jnp.zeros((n_flight * capacity, width_dev), jnp.bfloat16)
        .at[slots]
        .set(repeated, mode="drop")
    )
    buffer = buffer.reshape(n_flight, capacity, width_dev)
    received = lax.all_to_all(buffer, "expert", split_axis=0, concat_axis=0, tiled=True)
    piece = lax.all_gather(received, "tensor", axis=2, tiled=True)
    columns = piece.shape[2]
    grouped = piece.reshape(n_source, local_count, capacity, columns)
    gate = jnp.einsum("secd,edf->secf", grouped, w_gate, preferred_element_type=jnp.float32)
    upper = jnp.einsum("secd,edf->secf", grouped, w_up, preferred_element_type=jnp.float32)
    gated = (jax.nn.silu(gate) * upper).astype(jnp.bfloat16)
    partial_out = jnp.einsum("secf,efd->secd", gated, w_down, preferred_element_type=jnp.float32)
    partial_out = partial_out.reshape(n_flight, capacity, partial_out.shape[3])
    summed = lax.psum_scatter(partial_out, "tensor", scatter_dimension=2, tiled=True)
    expert_out = summed.astype(jnp.bfloat16)
    back = lax.all_to_all(expert_out, "expert", split_axis=0, concat_axis=0, tiled=True)
    flat_back = back.reshape(n_flight * capacity, width_dev)
    picked = jnp.take(flat_back, slots, axis=0, mode="fill", fill_value=0).astype(jnp.float32)
    picked = picked.reshape(tok_rows, picks, width_dev)
    mixed = jnp.sum(picked * route_gates[:, :, None], axis=1)
    return mixed.astype(jnp.bfloat16)


def solution(mesh):
    placed = (
        P(("dp", "expert"), "tensor"),
        P(("dp", "expert"), None),
        P(("dp", "expert"), None),
        P("expert", None, "tensor"),
        P("expert", None, "tensor"),
        P("expert", "tensor", None),
    )
    return jax.shard_map(
        body, mesh=mesh, in_specs=placed, out_specs=P(("dp", "expert"), "tensor"), check_vma=False
    )
```

profile of v0, /device:TPU:1, one launch (start us, length us, event | category | flops | bytes accessed | tf_op | source)
XLA Modules:
  0.0 239.1 jit_solution(11714694738695395970)
XLA Ops:
  6.5 0.8 copy.9
  7.4 0.2 eq.26
  7.5 0.2 reshape.107
  7.7 0.6 reduce-window.6
  8.3 0.2 slice_reduce_fusion
  8.5 0.2 reduce-window.9
  8.8 0.2 reduce_sum.23
  9.2 0.2 lt.47
  9.4 0.2 mul.40
  9.6 1.4 broadcast_in_dim.29
  11.0 0.3 reshape.128
  11.3 5.1 %scatter_custom_fusion = bf16[512,384]{1,0:T(8,128)(2,1)S(1)} fusion(s32[1024]{0:T(1024)S(1)} %bitcast.73, bf16[1024,384]{1,0:T(8,128)(2,1)S(1)} %reshape.128, bf16[]{:T(256)} %constant.17.clone.1), kind=kCustom, calls=%fused_computation.17 | custom fusion | bytes 393218 | tf_op jit(solution)/shard_map/scatter | solution.py:24
  16.4 7.6 %all_to_all.10 = bf16[2,256,384]{2,1,0:T(8,128)(2,1)} all-to-all(bf16[2,256,384]{2,1,0:T(8,128)(2,1)S(1)} %bitcast.71), channel_id=1, replica_groups=mesh['dp'=8,'expert'=2,'tensor'=16] {'expert'}, dimensions={0} | all-to-all | bytes 786432 | tf_op jit(solution)/shard_map/all_to_all | solution.py:27
  24.1 73.0 %all-gather.2.cloned.1.call-done = bf16[2,256,6144]{2,1,0:T(8,128)(2,1)} async-done(((bf16[2,256,384]{2,1,0:T(8,128)(2,1)}), bf16[2,256,6144]{2,1,0:T(8,128)(2,1)}) %all-gather.2.cloned.1.call-update) | async-done | bytes 6291472 | tf_op jit(solution)/shard_map/all_gather | solution.py:28
  97.1 8.1 %fusion.6 = f32[2,1,256,512]{3,2,0,1:T(8,128)S(1)} fusion(bf16[2,256,6144]{2,1,0:T(8,128)(2,1)} %all-gather.2.cloned.1.call-done, bf16[1,6144,512]{2,1,0:T(8,128)(2,1)} %param.9), kind=kOutput, calls=%fused_computation.10 | convolution fusion | flops 3221225472 | bytes 13631488 | tf_op jit(solution)/shard_map/secd,edf->secf/dot_general | solution.py:31
  105.2 6.5 %fusion.18 = bf16[2,256,512]{2,1,0:T(8,128)(2,1)S(1)} fusion(bf16[2,256,6144]{2,1,0:T(8,128)(2,1)S(1)} %copy-done.1, bf16[1,6144,512]{2,1,0:T(8,128)(2,1)} %param.10, f32[2,1,256,512]{3,2,0,1:T(8,128)S(1)} %fusion.6), kind=kOutput, calls=%fused_computation.14 | convolution fusion | flops 3222798336 | bytes 14155776 | tf_op jit(solution)/shard_map/secd,edf->secf/dot_general | solution.py:32
  111.7 6.4 %fusion = f32[2,256,6144]{2,1,0:T(8,128)} fusion(bf16[2,256,512]{2,1,0:T(8,128)(2,1)S(1)} %fusion.18, bf16[1,512,6144]{2,1,0:T(8,128)(2,1)S(1)} %bitcast.70), kind=kOutput, calls=%fused_computation.2 | convolution fusion | flops 3221225472 | bytes 19398656 | tf_op jit(solution)/shard_map/secf,efd->secd/dot_general | solution.py:34
  118.1 0.7 copy-done
  118.9 99.0 %reduce-scatter.2.cloned.1.call-done = f32[2,256,384]{2,1,0:T(8,128)} async-done(((f32[2,256,6144]{2,1,0:T(8,128)}), f32[2,256,384]{2,1,0:T(8,128)}) %reduce-scatter.2.cloned.1.call-update) | async-done | bytes 786448 | tf_op jit(solution)/shard_map/reduce_scatter | solution.py:36
  217.9 1.2 convert_element_type.23
  219.1 4.6 %all_to_all.11 = bf16[2,256,384]{2,1,0:T(8,128)(2,1)S(1)} all-to-all(bf16[2,256,384]{2,1,0:T(8,128)(2,1)S(1)} %convert_element_type.23), channel_id=1, replica_groups=mesh['dp'=8,'expert'=2,'tensor'=16] {'expert'}, dimensions={0} | all-to-all | bytes 786432 | tf_op jit(solution)/shard_map/all_to_all | solution.py:38
  223.7 3.9 %gather_fusion = bf16[1024,384]{1,0:T(8,128)(2,1)S(1)} fusion(bf16[512,384]{1,0:T(8,128)(2,1)S(1)} %bitcast.68, s32[1024]{0:T(1024)S(1)} %broadcast_clamp_fusion), kind=kCustom, calls=%fused_computation | custom fusion | bytes 1576960 | tf_op jit(solution)/shard_map/jit(_take)/gather | solution.py:40
  227.6 0.3 gather.7
  227.9 4.4 %multiply_reduce_fusion = bf16[512,384]{1,0:T(8,128)(2,1)} fusion(bf16[512,2,384]{2,1,0:T(2,128)(2,1)S(1)} %gather.7, pred[512,2]{1,0:T(8,128)(4,1)S(1)} %get-tuple-element.5, f32[512,2]{1,0:T(8,128)S(1)} %copy.13), kind=kLoop, calls=%fused_computation.8 | loop fusion | flops 1376256 | bytes 1184768 | tf_op jit(solution)/shard_map/reduce_sum | solution.py:42
  (20 shorter events, 0.5 us)
Async XLA Ops:
  6.5 90.5 %all-gather.2.cloned.1.call-start = ((), (), s32[]{:S(2)}) async-start(), calls=%async_computation.3 | async-start | bytes 6684672 | tf_op jit(solution)/shard_map/all_gather | solution.py:28
  24.0 193.9 %reduce-scatter.2.cloned.1.call-start = ((), (), s32[]{:S(2)}) async-start(), calls=%async_computation.4 | async-start | bytes 13369344 | tf_op jit(solution)/shard_map/reduce_scatter | solution.py:36
  97.1 8.1 %copy-start.1 = (bf16[2,256,6144]{2,1,0:T(8,128)(2,1)S(1)}, bf16[2,256,6144]{2,1,0:T(8,128)(2,1)}, u32[]{:S(2)}) copy-start(bf16[2,256,6144]{2,1,0:T(8,128)(2,1)} %all-gather.2.cloned.1.call-done) | copy-start | bytes 18874372
  97.1 14.6 %slice-start = ((s8[6291456]{0:T(1024)(128)(4,1)}), s8[4194304]{0:T(1024)(128)(4,1)S(1)}, s32[]{:S(2)}) async-start(s8[6291456]{0:T(1024)(128)(4,1)} %bitcast.69), calls=%async_computation.5 | async-start | bytes 8388608
  105.1 6.5 %slice-start.1 = ((s8[6291456]{0:T(1024)(128)(4,1)}), s8[2097152]{0:T(1024)(128)(4,1)S(1)}, s32[]{:S(2)}) async-start(s8[6291456]{0:T(1024)(128)(4,1)} %bitcast.69), calls=%async_computation.6 | async-start | bytes 4194304
  118.1 0.7 copy-start
Sparse Core Ops, SparseCore 0:
  24.2 72.8 all-gather.1
  118.2 99.6 reduce-scatter.1
where the time goes:
time: 239 us
  waiting for transfers between devices  172 us (72%)
  matrix products  20.9 us (9%)
  local copies, waits for them, and re-layouts  13.7 us (6%)
  between operations  13.6 us (6%)
  blocking collectives  12.2 us (5%)
  other arithmetic  6.63 us (3%)
    reduce_scatter x1, waiting for transfers between devices, body(): lax.psum_scatter(partial_out, 'tensor', scatter_dimension=2, tiled=True)  99 us
    all_gather x1, waiting for transfers between devices, body(): piece = lax.all_gather(received, 'tensor', axis=2, tiled=True)  73 us
    dot_general x1, matrix products, body(): jnp.einsum('secd,edf->secf', grouped, w_gate, preferred_element_type=jnp....  8.05 us
    all_to_all x1, blocking collectives, body(): lax.all_to_all(buffer, 'expert', split_axis=0, concat_axis=0, tiled=True)  7.65 us
    dot_general x1, matrix products, body(): jnp.einsum('secd,edf->secf', grouped, w_up, preferred_element_type=jnp.fl...  6.47 us
    dot_general x1, matrix products, body(): jnp.einsum('secf,efd->secd', gated, w_down, preferred_element_type=jnp.fl...  6.42 us
    scatter x1, local copies, waits for them, and re-layouts, body(): buffer = jnp.zeros((n_flight * capacity, width_dev), jnp.bfloat16).at[slo...  5.06 us
  transfers between devices with their start and end apart: 2, of which 2 were waited for; matrix products, arithmetic and copies ran while one was open for 0% of the time, Pallas kernels for 0%

commit v1 on v0

v1 whole, which is shorter than its diff:
```python
import functools

import jax
import jax.numpy as jnp
import numpy as np
from jax import lax
from jax.experimental import pallas as pl
from jax.experimental.pallas import tpu as pltpu
from jax.sharding import PartitionSpec as P

TENSOR = 16
MASKS = (1, 3, 4, 12)
CHAINS = ((0, 2, 1, 3), (1, 3, 0, 2), (2, 0, 3, 1), (3, 1, 2, 0))
MIB = 1 << 20


def positions(masks):
    table = [0] * TENSOR
    for bits in range(TENSOR):
        r = 0
        for k in range(4):
            if bits >> k & 1:
                r ^= masks[k]
        table[r] = bits
    return table


GATHER_POS = [positions([MASKS[l] for l in order]) for order in CHAINS]
SCATTER_POS = [positions([MASKS[l] for l in order]) for order in CHAINS]


def linear(table, value):
    total = 0
    for bit in range(4):
        total = total ^ (((value >> bit) & 1) * table[1 << bit])
    return total


def exchange(value, link):
    pairs = [(t, t ^ MASKS[link]) for t in range(TENSOR)]
    return lax.ppermute(value, "tensor", pairs)


def dispatch_kernel(core_ref, ids_ref, tok_ref, own_ref, oth_ref, pos_ref):
    rows = tok_ref.shape[0]
    cap = own_ref.shape[0]
    core = core_ref[0]
    first, second = ids_ref[:, 0:1], ids_ref[:, 1:2]
    tri = (
        lax.broadcasted_iota(jnp.int32, (rows, rows), 0) > lax.broadcasted_iota(jnp.int32, (rows, rows), 1)
    ).astype(jnp.bfloat16)
    lane = lax.broadcasted_iota(jnp.int32, (rows, 128), 1)
    wanted = jnp.where(lane == 0, core, jnp.where(lane == 1, 1 - core, -1))
    match = ((first == wanted) | (second == wanted)).astype(jnp.bfloat16)
    earlier = jnp.dot(tri, match, preferred_element_type=jnp.float32).astype(jnp.int32)
    slot = jnp.where(match > 0, earlier, -1)
    pos_ref[...] = slot
    slots = lax.broadcasted_iota(jnp.int32, (rows, cap), 1)
    for k, out in enumerate((own_ref, oth_ref)):
        onehot = (slot[:, k : k + 1] == slots).astype(jnp.bfloat16)
        picked = lax.dot_general(
            onehot, tok_ref[...], (((0,), (0,)), ((), ())), preferred_element_type=jnp.float32
        )
        out[...] = picked.astype(jnp.bfloat16)


def dispatch(core, ids, tokens, cap):
    rows, width = tokens.shape
    vmem = pl.BlockSpec(memory_space=pltpu.VMEM)
    return pl.pallas_call(
        dispatch_kernel,
        in_specs=[pl.BlockSpec(memory_space=pltpu.SMEM), vmem, vmem],
        out_specs=[vmem, vmem, vmem],
        out_shape=[
            jax.ShapeDtypeStruct((cap, width), jnp.bfloat16),
            jax.ShapeDtypeStruct((cap, width), jnp.bfloat16),
            jax.ShapeDtypeStruct((rows, 128), jnp.int32),
        ],
        name="dispatch",
    )(core, ids, tokens)


def combine_kernel(core_ref, ids_ref, gates_ref, pos_ref, own_ref, oth_ref, out_ref):
    rows = ids_ref.shape[0]
    cap = own_ref.shape[0]
    core = core_ref[0]
    slots = lax.broadcasted_iota(jnp.int32, (rows, cap), 1)
    total = jnp.zeros(out_ref.shape, jnp.float32)
    for k, src in enumerate((own_ref, oth_ref)):
        expert = core if k == 0 else 1 - core
        weight = jnp.sum(jnp.where(ids_ref[...] == expert, gates_ref[...], 0.0), axis=1, keepdims=True)
        onehot = (pos_ref[:, k : k + 1] == slots).astype(jnp.bfloat16)
        total += weight * jnp.dot(onehot, src[...], preferred_element_type=jnp.float32)
    out_ref[...] = total.astype(jnp.bfloat16)


def combine(core, ids, gates, slot, own, oth):
    vmem = pl.BlockSpec(memory_space=pltpu.VMEM)
    return pl.pallas_call(
        combine_kernel,
        in_specs=[pl.BlockSpec(memory_space=pltpu.SMEM)] + [vmem] * 5,
        out_specs=vmem,
        out_shape=jax.ShapeDtypeStruct((ids.shape[0], own.shape[1]), jnp.bfloat16),
        name="combine",
    )(core, ids, gates, slot, own, oth)


def expert_kernel(me_ref, x0, x1, x2, x3, wg_ref, wu_ref, wd_ref, *rest):
    sends, keeps = rest[0:4], rest[4:8]
    acc_g, acc_u, gated, xs = rest[8:]
    step = pl.program_id(0)
    me = me_ref[0]
    part, width = x0.shape[1], x0.shape[2]

    @pl.when(step < 8)
    def _():
        for half in range(2):
            block = 2 * step + half
            for i, x in enumerate((x0, x1, x2, x3)):
                where = linear(GATHER_POS[i], block ^ me)
                xs[i * part : (i + 1) * part, half * width : (half + 1) * width] = x[where]
        g = jnp.dot(xs[...], wg_ref[...], preferred_element_type=jnp.float32)
        u = jnp.dot(xs[...], wu_ref[...], preferred_element_type=jnp.float32)

        @pl.when(step == 0)
        def _():
            acc_g[...] = g
            acc_u[...] = u

        @pl.when(step > 0)
        def _():
            acc_g[...] += g
            acc_u[...] += u

    @pl.when(step == 7)
    def _():
        v = acc_g[...]
        gated[...] = (v / (1.0 + jnp.exp(-v)) * acc_u[...]).astype(jnp.bfloat16)

    @pl.when(step >= 8)
    def _():
        y = jnp.dot(gated[...], wd_ref[...], preferred_element_type=jnp.float32)
        for half in range(2):
            block = 2 * (step - 8) + half
            for i in range(4):
                where = linear(SCATTER_POS[i], block ^ me)
                piece = y[i * part : (i + 1) * part, half * width : (half + 1) * width]

                @pl.when(where >= 8)
                def _():
                    sends[i][where - 8] = piece.astype(jnp.bfloat16)

                @pl.when(where < 8)
                def _():
                    keeps[i][where] = piece


def experts(me, xs, w_gate, w_up, w_down):
    blocks, part, width = xs[0].shape
    rows = 4 * part
    model, hidden = w_gate.shape
    pair = 2 * width
    vmem = pl.BlockSpec(memory_space=pltpu.VMEM)
    return pl.pallas_call(
        expert_kernel,
        grid=(16,),
        in_specs=[pl.BlockSpec(memory_space=pltpu.SMEM)]
        + [vmem] * 4
        + [
            pl.BlockSpec((pair, hidden), lambda s: (jnp.minimum(s, 7), 0)),
            pl.BlockSpec((pair, hidden), lambda s: (jnp.minimum(s, 7), 0)),
            pl.BlockSpec((hidden, pair), lambda s: (0, jnp.maximum(s - 8, 0))),
        ],
        out_specs=[vmem] * 8,
        out_shape=[jax.ShapeDtypeStruct((8, part, width), jnp.bfloat16)] * 4
        + [jax.ShapeDtypeStruct((8, part, width), jnp.float32)] * 4,
        scratch_shapes=[
            pltpu.VMEM((rows, hidden), jnp.float32),
            pltpu.VMEM((rows, hidden), jnp.float32),
            pltpu.VMEM((rows, hidden), jnp.bfloat16),
            pltpu.VMEM((rows, pair), jnp.bfloat16),
        ],
        compiler_params=pltpu.CompilerParams(vmem_limit_bytes=48 * MIB),
        cost_estimate=pl.CostEstimate(
            flops=6 * rows * model * hidden, bytes_accessed=6 * model * hidden, transcendentals=rows * hidden
        ),
        name="experts",
    )(me, *xs, w_gate, w_up, w_down)


def body(tokens, route_ids, route_gates, w_gate, w_up, w_down):
    rows, width = tokens.shape
    cap = rows // 2
    part = cap // 2
    swap = [(0, 1), (1, 0)]
    core = lax.axis_index("expert").astype(jnp.int32).reshape(1)
    me = lax.axis_index("tensor").astype(jnp.int32).reshape(1)

    own, oth, slot = dispatch(core, route_ids, tokens, cap)
    got = lax.ppermute(oth, "expert", swap)
    held = [own[None, :part], own[None, part:], got[None, :part], got[None, part:]]
    for phase in range(4):
        arrived = [exchange(held[i], CHAINS[i][phase]) for i in range(4)]
        held = [jnp.concatenate([held[i], arrived[i]]) for i in range(4)]

    results = experts(me, held, w_gate[0], w_up[0], w_down[0])
    sends, keeps = list(results[:4]), list(results[4:])
    for phase in range(4):
        link = [CHAINS[i][3 - phase] for i in range(4)]
        arrived = [exchange(sends[i], link[i]) for i in range(4)]
        sums = [keeps[i] + arrived[i].astype(jnp.float32) for i in range(4)]
        half = sums[0].shape[0] // 2
        if phase < 3:
            sends = [s[half:].astype(jnp.bfloat16) for s in sums]
            keeps = [s[:half] for s in sums]
    done = [s[0].astype(jnp.bfloat16) for s in sums]
    mine = jnp.concatenate(done[:2])
    theirs = jnp.concatenate(done[2:])
    back = lax.ppermute(theirs, "expert", swap)
    return combine(core, route_ids, route_gates, slot, mine, back)


def solution(mesh):
    placed = (
        P(("dp", "expert"), "tensor"),
        P(("dp", "expert"), None),
        P(("dp", "expert"), None),
        P("expert", None, "tensor"),
        P("expert", None, "tensor"),
        P("expert", "tensor", None),
    )
    return jax.shard_map(
        body, mesh=mesh, in_specs=placed, out_specs=P(("dp", "expert"), "tensor"), check_vma=False
    )
```

time: 239 us -> 144 us (0.60); the launches traced: 239 us -> 142 us
  waiting for transfers between devices: 172 us -> 50.4 us
  starting transfers between devices: 0.04 us -> 44.7 us
  Pallas kernels: 0 us -> 30.2 us
  matrix products: 20.9 us -> 0 us
  between operations: 13.6 us -> 0.48 us
  blocking collectives: 12.2 us -> 0 us
  local copies, waits for them, and re-layouts: 13.7 us -> 9.04 us
    reduce_scatter x1 -> x0, waiting for transfers between devices: 99 us -> none  [body(): lax.psum_scatter(partial_out, 'tensor', scatter_dimension=2, tiled=True)]
    all_gather x1 -> x0, waiting for transfers between devices: 73 us -> none  [body(): piece = lax.all_gather(received, 'tensor', axis=2, tiled=True)]
    ppermute x0 -> x34, waiting for transfers between devices: none -> 50.4 us  [the longest x32 50.1 us: exchange(): return lax.ppermute(value, 'tensor', pairs)]
    ppermute x0 -> x34, starting transfers between devices: none -> 44.7 us  [the longest x32 33.9 us: exchange(): return lax.ppermute(value, 'tensor', pairs)]
    pallas_call x0 -> x3, Pallas kernels: none -> 30.2 us  [the longest x1 24.7 us: experts(): pl.pallas_call(expert_kernel, grid=(16,), in_specs=[pl.BlockSpec(memory_s...]
    dot_general x3 -> x0, matrix products: 20.9 us -> none  [the longest x1 8.05 us: body(): jnp.einsum('secd,edf->secf', grouped, w_gate, preferred_element_type=jnp....]
    all_to_all x2 -> x0, blocking collectives: 12.2 us -> none  [the longest x1 7.65 us: body(): lax.all_to_all(buffer, 'expert', split_axis=0, concat_axis=0, tiled=True)]
    unnamed x10 -> x34, local copies, waits for them, and re-layouts: 1.64 us -> 7.13 us
  transfers between devices with their start and end apart: 2 -> 34, of which waited for: 2 -> 16; matrix products, arithmetic and copies ran while one was open for 0% -> 9% of each run, Pallas kernels for 0% -> 0%
where the time goes in v1:
time: 144 us; the launch traced here: 142 us
  waiting for transfers between devices  50.4 us (35%)
  starting transfers between devices  44.7 us (31%)
  Pallas kernels  30.2 us (21%)
  local copies, waits for them, and re-layouts  9.04 us (6%)
  other arithmetic  6.73 us (5%)
    ppermute x32, waiting for transfers between devices, exchange(): return lax.ppermute(value, 'tensor', pairs)  50.1 us
    ppermute x32, starting transfers between devices, exchange(): return lax.ppermute(value, 'tensor', pairs)  33.9 us
    pallas_call x1, Pallas kernels, experts(): pl.pallas_call(expert_kernel, grid=(16,), in_specs=[pl.BlockSpec(memory_s...  24.7 us
    ppermute x1, starting transfers between devices, body(): back = lax.ppermute(theirs, 'expert', swap)  7.61 us
    unnamed x34, local copies, waits for them, and re-layouts  7.13 us
    add x12, other arithmetic, body(): sums = [keeps[i] + arrived[i].astype(jnp.float32) for i in range(4)]  5.18 us
    ppermute x1, starting transfers between devices, body(): got = lax.ppermute(oth, 'expert', swap)  3.24 us
    pallas_call x1, Pallas kernels, dispatch(): pl.pallas_call(dispatch_kernel, in_specs=[pl.BlockSpec(memory_space=pltpu...  3.01 us
  transfers between devices with their start and end apart: 34, of which 16 were waited for; matrix products, arithmetic and copies ran while one was open for 9% of the time, Pallas kernels for 0%

profile of v1, /device:TPU:1, one launch (start us, length us, event | category | flops | bytes accessed | tf_op | source)
XLA Modules:
  0.0 141.5 jit_solution(696910434284873911)
XLA Ops:
  0.0 1.5 %copy.8.ids_ref = s32[512,2]{1,0:T(8,128)} copy(s32[512,2]{0,1:T(2,128)} %param.7) | data formatting | bytes 8192 | tf_op args[1]
  1.5 3.0 %dispatch.1 = (bf16[256,384]{1,0:T(8,128)(2,1)}, bf16[256,384]{1,0:T(8,128)(2,1)}, s32[512,128]{1,0:T(8,128)}) custom-call(s32[1]{0:T(128)} %bitcast.core_ref, s32[512,2]{1,0:T(8,128)} %copy.8.ids_ref, bf16[512,384]{1,0:T(8,128)(2,1)} %tok_ref.1), custom_call_target="tpu_custom_call" | custom-call | tf_op jit(solution)/shard_map/dispatch/pallas_call | solution.py:70
  4.6 3.2 %collective-permute-start.8 = (bf16[256,384]{1,0:T(8,128)(2,1)}, bf16[256,384]{1,0:T(8,128)(2,1)S(1)}, u32[]{:S(2)}, u32[]{:S(2)}) collective-permute-start(bf16[256,384]{1,0:T(8,128)(2,1)} %get-tuple-element.18), channel_id=1, source_target_pairs={{0,16},{16,0},{1,17},{17,1},{2,18},{18,2},{3,19},{19,3},{4,20},{20... | collective-permute-start | bytes 589832 | tf_op jit(solution)/shard_map/ppermute | solution.py:200
  9.6 1.6 %constant_dynamic-update-slice_fusion.9 = (bf16[16,128,384]{2,1,0:T(8,128)(2,1)}, bf16[16,128,384]{2,1,0:T(8,128)(2,1)S(1)}) fusion(bf16[256,384]{1,0:T(8,128)(2,1)} %get-tuple-element.17), kind=kLoop, calls=%fused_computation.63 | loop fusion | bytes 393216
  11.2 3.3 %collective-permute-done.4 = bf16[1,128,384]{2,1,0:T(8,128)(2,1)S(1)} collective-permute-done((bf16[1,128,384]{2,1,0:T(8,128)(2,1)S(1)}, bf16[1,128,384]{2,1,0:T(8,128)(2,1)S(1)}, u32[]{:S(2)}, u32[]{:S(2)}) %collective-permute-start.4) | collective-permute-done | bytes 98336 | tf_op jit(solution)/shard_map/ppermute | solution.py:41
  16.5 1.8 %collective-permute-start.13 = (bf16[1,128,384]{2,1,0:T(8,128)(2,1)S(1)}, bf16[1,128,384]{2,1,0:T(8,128)(2,1)S(1)}, u32[]{:S(2)}, u32[]{:S(2)}) collective-permute-start(bf16[1,128,384]{2,1,0:T(8,128)(2,1)S(1)} %get-tuple-element.27), channel_id=1, source_target_pairs={{0,12},{1,13},{2,14},{3,15},{4,8},{5,9},{6,10},{7,11},{8,4},{9,5},... | collective-permute-start | bytes 294920 | tf_op jit(solution)/shard_map/ppermute | solution.py:41
  19.1 4.5 %collective-permute-done.13 = bf16[1,128,384]{2,1,0:T(8,128)(2,1)S(1)} collective-permute-done((bf16[1,128,384]{2,1,0:T(8,128)(2,1)S(1)}, bf16[1,128,384]{2,1,0:T(8,128)(2,1)S(1)}, u32[]{:S(2)}, u32[]{:S(2)}) %collective-permute-start.13) | collective-permute-done | bytes 98336 | tf_op jit(solution)/shard_map/ppermute | solution.py:41
  24.6 1.5 %collective-permute-start.6 = (bf16[4,128,384]{2,1,0:T(8,128)(2,1)S(1)}, bf16[4,128,384]{2,1,0:T(8,128)(2,1)S(1)}, u32[]{:S(2)}, u32[]{:S(2)}) collective-permute-start(bf16[4,128,384]{2,1,0:T(8,128)(2,1)S(1)} %pad_maximum_fusion.5), channel_id=1, source_target_pairs={{0,1},{1,0},{2,3},{3,2},{4,5},{5,4},{6,7},{7,6},{8,9},{9,8},{10,11... | collective-permute-start | bytes 1179656 | tf_op jit(solution)/shard_map/ppermute | solution.py:41
  26.2 2.0 %collective-permute-start.2 = (bf16[4,128,384]{2,1,0:T(8,128)(2,1)S(1)}, bf16[4,128,384]{2,1,0:T(8,128)(2,1)S(1)}, u32[]{:S(2)}, u32[]{:S(2)}) collective-permute-start(bf16[4,128,384]{2,1,0:T(8,128)(2,1)S(1)} %pad_maximum_fusion.4), channel_id=1, source_target_pairs={{0,3},{1,2},{2,1},{3,0},{4,7},{5,6},{6,5},{7,4},{8,11},{9,10},{10,... | collective-permute-start | bytes 1179656 | tf_op jit(solution)/shard_map/ppermute | solution.py:41
  29.6 2.6 %collective-permute-start.11 = (bf16[4,128,384]{2,1,0:T(8,128)(2,1)S(1)}, bf16[4,128,384]{2,1,0:T(8,128)(2,1)S(1)}, u32[]{:S(2)}, u32[]{:S(2)}) collective-permute-start(bf16[4,128,384]{2,1,0:T(8,128)(2,1)S(1)} %pad_maximum_fusion.6), channel_id=1, source_target_pairs={{0,12},{1,13},{2,14},{3,15},{4,8},{5,9},{6,10},{7,11},{8,4},{9,5},... | collective-permute-start | bytes 1179656 | tf_op jit(solution)/shard_map/ppermute | solution.py:41
  32.3 5.0 %collective-permute-done.6 = bf16[4,128,384]{2,1,0:T(8,128)(2,1)S(1)} collective-permute-done((bf16[4,128,384]{2,1,0:T(8,128)(2,1)S(1)}, bf16[4,128,384]{2,1,0:T(8,128)(2,1)S(1)}, u32[]{:S(2)}, u32[]{:S(2)}) %collective-permute-start.6) | collective-permute-done | bytes 393248 | tf_op jit(solution)/shard_map/ppermute | solution.py:41
  38.7 1.9 %collective-permute-start.3 = (bf16[8,128,384]{2,1,0:T(8,128)(2,1)S(1)}, bf16[8,128,384]{2,1,0:T(8,128)(2,1)S(1)}, u32[]{:S(2)}, u32[]{:S(2)}) collective-permute-start(bf16[8,128,384]{2,1,0:T(8,128)(2,1)S(1)} %pad_maximum_fusion), channel_id=1, source_target_pairs={{0,12},{1,13},{2,14},{3,15},{4,8},{5,9},{6,10},{7,11},{8,4},{9,5},... | collective-permute-start | bytes 2359304 | tf_op jit(solution)/shard_map/ppermute | solution.py:41
  42.6 13.5 %collective-permute-done.7 = bf16[8,128,384]{2,1,0:T(8,128)(2,1)S(1)} collective-permute-done((bf16[8,128,384]{2,1,0:T(8,128)(2,1)S(1)}, bf16[8,128,384]{2,1,0:T(8,128)(2,1)S(1)}, u32[]{:S(2)}, u32[]{:S(2)}) %collective-permute-start.7) | collective-permute-done | bytes 786464 | tf_op jit(solution)/shard_map/ppermute | solution.py:41
  59.9 24.7 %experts.1 = (bf16[8,128,384]{2,1,0:T(8,128)(2,1)S(1)}, bf16[8,128,384]{2,1,0:T(8,128)(2,1)S(1)}, bf16[8,128,384]{2,1,0:T(8,128)(2,1)}, bf16[8,128,384]{2,1,0:T(...) custom-call(s32[1]{0:T(128)} %bitcast.1.me_ref, ...), custom_call_target="tpu_custom_call" | custom-call | flops 9663676416 | bytes 18874368 | tf_op jit(solution)/shard_map/experts/pallas_call | solution.py:164
  84.6 2.4 %collective-permute-start.25 = (bf16[8,128,384]{2,1,0:T(8,128)(2,1)}, bf16[8,128,384]{2,1,0:T(8,128)(2,1)}, u32[]{:S(2)}, u32[]{:S(2)}) collective-permute-start(bf16[8,128,384]{2,1,0:T(8,128)(2,1)} %get-tuple-element.24), channel_id=1, source_target_pairs={{0,3},{1,2},{2,1},{3,0},{4,7},{5,6},{6,5},{7,4},{8,11},{9,10},{10,... | collective-permute-start | bytes 2359304 | tf_op jit(solution)/shard_map/ppermute | solution.py:41
  87.0 1.9 %collective-permute-start.17 = (bf16[8,128,384]{2,1,0:T(8,128)(2,1)S(1)}, bf16[8,128,384]{2,1,0:T(8,128)(2,1)}, u32[]{:S(2)}, u32[]{:S(2)}) collective-permute-start(bf16[8,128,384]{2,1,0:T(8,128)(2,1)S(1)} %get-tuple-element.20), channel_id=1, source_target_pairs={{0,12},{1,13},{2,14},{3,15},{4,8},{5,9},{6,10},{7,11},{8,4},{9,5},... | collective-permute-start | bytes 2359304 | tf_op jit(solution)/shard_map/ppermute | solution.py:41
  89.7 11.8 %collective-permute-done.25 = bf16[8,128,384]{2,1,0:T(8,128)(2,1)} collective-permute-done((bf16[8,128,384]{2,1,0:T(8,128)(2,1)}, bf16[8,128,384]{2,1,0:T(8,128)(2,1)}, u32[]{:S(2)}, u32[]{:S(2)}) %collective-permute-start.25) | collective-permute-done | bytes 786464 | tf_op jit(solution)/shard_map/ppermute | solution.py:41
  101.6 1.9 %convert_add_fusion.1 = f32[8,128,384]{2,1,0:T(8,128)S(1)} fusion(f32[8,128,384]{2,1,0:T(8,128)} %get-tuple-element.23, bf16[8,128,384]{2,1,0:T(8,128)(2,1)} %collective-permute-done.25), kind=kLoop, calls=%fused_computation.1 | loop fusion | flops 786432 | bytes 3932160 | tf_op jit(solution)/shard_map/add | solution.py:211
  103.5 4.4 %collective-permute-start.26 = (bf16[4,128,384]{2,1,0:T(8,128)(2,1)S(1)}, bf16[4,128,384]{2,1,0:T(8,128)(2,1)S(1)}, u32[]{:S(2)}, u32[]{:S(2)}) collective-permute-start(bf16[4,128,384]{2,1,0:T(8,128)(2,1)S(1)} %slice.203), channel_id=1, source_target_pairs={{0,12},{1,13},{2,14},{3,15},{4,8},{5,9},{6,10},{7,11},{8,4},{9,5},... | collective-permute-start | bytes 1179656 | tf_op jit(solution)/shard_map/ppermute | solution.py:41
  114.0 1.7 %collective-permute-start.27 = (bf16[2,128,384]{2,1,0:T(8,128)(2,1)S(1)}, bf16[2,128,384]{2,1,0:T(8,128)(2,1)S(1)}, u32[]{:S(2)}, u32[]{:S(2)}) collective-permute-start(bf16[2,128,384]{2,1,0:T(8,128)(2,1)S(1)} %slice.207), channel_id=1, source_target_pairs={{0,1},{1,0},{2,3},{3,2},{4,5},{5,4},{6,7},{7,6},{8,9},{9,8},{10,11... | collective-permute-start | bytes 589832 | tf_op jit(solution)/shard_map/ppermute | solution.py:41
  121.0 2.4 %collective-permute-done.27 = bf16[2,128,384]{2,1,0:T(8,128)(2,1)S(1)} collective-permute-done((bf16[2,128,384]{2,1,0:T(8,128)(2,1)S(1)}, bf16[2,128,384]{2,1,0:T(8,128)(2,1)S(1)}, u32[]{:S(2)}, u32[]{:S(2)}) %collective-permute-start.27) | collective-permute-done | bytes 196640 | tf_op jit(solution)/shard_map/ppermute | solution.py:41
  128.0 1.5 %collective-permute-done.32 = bf16[1,128,384]{2,1,0:T(8,128)(2,1)S(1)} collective-permute-done((bf16[1,128,384]{2,1,0:T(8,128)(2,1)S(1)}, bf16[1,128,384]{2,1,0:T(8,128)(2,1)S(1)}, u32[]{:S(2)}, u32[]{:S(2)}) %collective-permute-start.32) | collective-permute-done | bytes 98336 | tf_op jit(solution)/shard_map/ppermute | solution.py:41
  129.6 7.6 %collective-permute-start.33 = (bf16[256,384]{1,0:T(8,128)(2,1)S(1)}, bf16[256,384]{1,0:T(8,128)(2,1)S(1)}, u32[]{:S(2)}, u32[]{:S(2)}) collective-permute-start(bf16[256,384]{1,0:T(8,128)(2,1)S(1)} %pad_maximum_fusion.13), channel_id=1, source_target_pairs={{0,16},{16,0},{1,17},{17,1},{2,18},{18,2},{3,19},{19,3},{4,20},{20... | collective-permute-start | bytes 589832 | tf_op jit(solution)/shard_map/ppermute | solution.py:219
  139.0 2.5 %combine.1 = bf16[512,384]{1,0:T(8,128)(2,1)} custom-call(s32[1]{0:T(128)} %bitcast.core_ref, s32[512,2]{1,0:T(8,128)} %copy.8.ids_ref, f32[512,2]{1,0:T(8,128)} %copy.9.gates_ref, s32[512,128]{1,0:T(8,128)} %get-tuple-element.16.pos_ref, bf16[256,384]{1,0:T(8,128)(2,1)} %pad_maximum_fusion.12.own_ref, bf16[256,384]{1,0:T(8,128)(2,1)} %copy-done.2), custom_call_target="tpu_custom_call" | custom-call | tf_op jit(solution)/shard_map/combine/pallas_call | solution.py:99
  (129 shorter events, 32.9 us)
Async XLA Ops:
  4.6 11.9 %collective-permute-start.8 = (bf16[256,384]{1,0:T(8,128)(2,1)}, bf16[256,384]{1,0:T(8,128)(2,1)S(1)}, u32[]{:S(2)}, u32[]{:S(2)}) collective-permute-start(bf16[256,384]{1,0:T(8,128)(2,1)} %get-tuple-element.18), channel_id=1, source_target_pairs={{0,16},{16,0},{1,17},{17,1},{2,18},{18,2},{3,19},{19,3},{4,20},{20... | collective-permute-start | bytes 589832 | tf_op jit(solution)/shard_map/ppermute | solution.py:200
  14.5 10.0 %collective-permute-start.5 = (bf16[2,128,384]{2,1,0:T(8,128)(2,1)S(1)}, bf16[2,128,384]{2,1,0:T(8,128)(2,1)S(1)}, u32[]{:S(2)}, u32[]{:S(2)}) collective-permute-start(bf16[2,128,384]{2,1,0:T(8,128)(2,1)S(1)} %pad_maximum_fusion.9), channel_id=1, source_target_pairs={{0,12},{1,13},{2,14},{3,15},{4,8},{5,9},{6,10},{7,11},{8,4},{9,5},... | collective-permute-start | bytes 589832 | tf_op jit(solution)/shard_map/ppermute | solution.py:41
  15.6 10.5 %collective-permute-start.1 = (bf16[2,128,384]{2,1,0:T(8,128)(2,1)S(1)}, bf16[2,128,384]{2,1,0:T(8,128)(2,1)S(1)}, u32[]{:S(2)}, u32[]{:S(2)}) collective-permute-start(bf16[2,128,384]{2,1,0:T(8,128)(2,1)S(1)} %pad_maximum_fusion.8), channel_id=1, source_target_pairs={{0,4},{1,5},{2,6},{3,7},{4,0},{5,1},{6,2},{7,3},{8,12},{9,13},{10,... | collective-permute-start | bytes 589832 | tf_op jit(solution)/shard_map/ppermute | solution.py:41
  16.5 7.1 %collective-permute-start.13 = (bf16[1,128,384]{2,1,0:T(8,128)(2,1)S(1)}, bf16[1,128,384]{2,1,0:T(8,128)(2,1)S(1)}, u32[]{:S(2)}, u32[]{:S(2)}) collective-permute-start(bf16[1,128,384]{2,1,0:T(8,128)(2,1)S(1)} %get-tuple-element.27), channel_id=1, source_target_pairs={{0,12},{1,13},{2,14},{3,15},{4,8},{5,9},{6,10},{7,11},{8,4},{9,5},... | collective-permute-start | bytes 294920 | tf_op jit(solution)/shard_map/ppermute | solution.py:41
  24.6 12.7 %collective-permute-start.6 = (bf16[4,128,384]{2,1,0:T(8,128)(2,1)S(1)}, bf16[4,128,384]{2,1,0:T(8,128)(2,1)S(1)}, u32[]{:S(2)}, u32[]{:S(2)}) collective-permute-start(bf16[4,128,384]{2,1,0:T(8,128)(2,1)S(1)} %pad_maximum_fusion.5), channel_id=1, source_target_pairs={{0,1},{1,0},{2,3},{3,2},{4,5},{5,4},{6,7},{7,6},{8,9},{9,8},{10,11... | collective-permute-start | bytes 1179656 | tf_op jit(solution)/shard_map/ppermute | solution.py:41
  26.2 12.4 %collective-permute-start.2 = (bf16[4,128,384]{2,1,0:T(8,128)(2,1)S(1)}, bf16[4,128,384]{2,1,0:T(8,128)(2,1)S(1)}, u32[]{:S(2)}, u32[]{:S(2)}) collective-permute-start(bf16[4,128,384]{2,1,0:T(8,128)(2,1)S(1)} %pad_maximum_fusion.4), channel_id=1, source_target_pairs={{0,3},{1,2},{2,1},{3,0},{4,7},{5,6},{6,5},{7,4},{8,11},{9,10},{10,... | collective-permute-start | bytes 1179656 | tf_op jit(solution)/shard_map/ppermute | solution.py:41
  29.5 11.1 %collective-permute-start.15 = (bf16[4,128,384]{2,1,0:T(8,128)(2,1)S(1)}, bf16[4,128,384]{2,1,0:T(8,128)(2,1)S(1)}, u32[]{:S(2)}, u32[]{:S(2)}) collective-permute-start(bf16[4,128,384]{2,1,0:T(8,128)(2,1)S(1)} %pad_maximum_fusion.7), channel_id=1, source_target_pairs={{0,4},{1,5},{2,6},{3,7},{4,0},{5,1},{6,2},{7,3},{8,12},{9,13},{10,... | collective-permute-start | bytes 1179656 | tf_op jit(solution)/shard_map/ppermute | solution.py:41
  29.6 11.4 %collective-permute-start.11 = (bf16[4,128,384]{2,1,0:T(8,128)(2,1)S(1)}, bf16[4,128,384]{2,1,0:T(8,128)(2,1)S(1)}, u32[]{:S(2)}, u32[]{:S(2)}) collective-permute-start(bf16[4,128,384]{2,1,0:T(8,128)(2,1)S(1)} %pad_maximum_fusion.6), channel_id=1, source_target_pairs={{0,12},{1,13},{2,14},{3,15},{4,8},{5,9},{6,10},{7,11},{8,4},{9,5},... | collective-permute-start | bytes 1179656 | tf_op jit(solution)/shard_map/ppermute | solution.py:41
  37.4 18.6 %collective-permute-start.7 = (bf16[8,128,384]{2,1,0:T(8,128)(2,1)S(1)}, bf16[8,128,384]{2,1,0:T(8,128)(2,1)S(1)}, u32[]{:S(2)}, u32[]{:S(2)}) collective-permute-start(bf16[8,128,384]{2,1,0:T(8,128)(2,1)S(1)} %pad_maximum_fusion.1), channel_id=1, source_target_pairs={{0,4},{1,5},{2,6},{3,7},{4,0},{5,1},{6,2},{7,3},{8,12},{9,13},{10,... | collective-permute-start | bytes 2359304 | tf_op jit(solution)/shard_map/ppermute | solution.py:41
  38.7 18.7 %collective-permute-start.3 = (bf16[8,128,384]{2,1,0:T(8,128)(2,1)S(1)}, bf16[8,128,384]{2,1,0:T(8,128)(2,1)S(1)}, u32[]{:S(2)}, u32[]{:S(2)}) collective-permute-start(bf16[8,128,384]{2,1,0:T(8,128)(2,1)S(1)} %pad_maximum_fusion), channel_id=1, source_target_pairs={{0,12},{1,13},{2,14},{3,15},{4,8},{5,9},{6,10},{7,11},{8,4},{9,5},... | collective-permute-start | bytes 2359304 | tf_op jit(solution)/shard_map/ppermute | solution.py:41
  40.7 16.9 %collective-permute-start.16 = (bf16[8,128,384]{2,1,0:T(8,128)(2,1)S(1)}, bf16[8,128,384]{2,1,0:T(8,128)(2,1)S(1)}, u32[]{:S(2)}, u32[]{:S(2)}) collective-permute-start(bf16[8,128,384]{2,1,0:T(8,128)(2,1)S(1)} %pad_maximum_fusion.3), channel_id=1, source_target_pairs={{0,1},{1,0},{2,3},{3,2},{4,5},{5,4},{6,7},{7,6},{8,9},{9,8},{10,11... | collective-permute-start | bytes 2359304 | tf_op jit(solution)/shard_map/ppermute | solution.py:41
  41.1 17.4 %collective-permute-start.12 = (bf16[8,128,384]{2,1,0:T(8,128)(2,1)S(1)}, bf16[8,128,384]{2,1,0:T(8,128)(2,1)S(1)}, u32[]{:S(2)}, u32[]{:S(2)}) collective-permute-start(bf16[8,128,384]{2,1,0:T(8,128)(2,1)S(1)} %pad_maximum_fusion.2), channel_id=1, source_target_pairs={{0,3},{1,2},{2,1},{3,0},{4,7},{5,6},{6,5},{7,4},{8,11},{9,10},{10,... | collective-permute-start | bytes 2359304 | tf_op jit(solution)/shard_map/ppermute | solution.py:41
  84.6 17.0 %collective-permute-start.25 = (bf16[8,128,384]{2,1,0:T(8,128)(2,1)}, bf16[8,128,384]{2,1,0:T(8,128)(2,1)}, u32[]{:S(2)}, u32[]{:S(2)}) collective-permute-start(bf16[8,128,384]{2,1,0:T(8,128)(2,1)} %get-tuple-element.24), channel_id=1, source_target_pairs={{0,3},{1,2},{2,1},{3,0},{4,7},{5,6},{6,5},{7,4},{8,11},{9,10},{10,... | collective-permute-start | bytes 2359304 | tf_op jit(solution)/shard_map/ppermute | solution.py:41
  87.0 20.9 %collective-permute-start.29 = (bf16[8,128,384]{2,1,0:T(8,128)(2,1)}, bf16[8,128,384]{2,1,0:T(8,128)(2,1)}, u32[]{:S(2)}, u32[]{:S(2)}) collective-permute-start(bf16[8,128,384]{2,1,0:T(8,128)(2,1)} %get-tuple-element.26), channel_id=1, source_target_pairs={{0,1},{1,0},{2,3},{3,2},{4,5},{5,4},{6,7},{7,6},{8,9},{9,8},{10,11... | collective-permute-start | bytes 2359304 | tf_op jit(solution)/shard_map/ppermute | solution.py:41
  87.0 22.4 %collective-permute-start.17 = (bf16[8,128,384]{2,1,0:T(8,128)(2,1)S(1)}, bf16[8,128,384]{2,1,0:T(8,128)(2,1)}, u32[]{:S(2)}, u32[]{:S(2)}) collective-permute-start(bf16[8,128,384]{2,1,0:T(8,128)(2,1)S(1)} %get-tuple-element.20), channel_id=1, source_target_pairs={{0,12},{1,13},{2,14},{3,15},{4,8},{5,9},{6,10},{7,11},{8,4},{9,5},... | collective-permute-start | bytes 2359304 | tf_op jit(solution)/shard_map/ppermute | solution.py:41
  89.7 22.4 %collective-permute-start.21 = (bf16[8,128,384]{2,1,0:T(8,128)(2,1)S(1)}, bf16[8,128,384]{2,1,0:T(8,128)(2,1)S(1)}, u32[]{:S(2)}, u32[]{:S(2)}) collective-permute-start(bf16[8,128,384]{2,1,0:T(8,128)(2,1)S(1)} %get-tuple-element.22), channel_id=1, source_target_pairs={{0,4},{1,5},{2,6},{3,7},{4,0},{5,1},{6,2},{7,3},{8,12},{9,13},{10,... | collective-permute-start | bytes 2359304 | tf_op jit(solution)/shard_map/ppermute | solution.py:41
  103.5 10.4 %collective-permute-start.26 = (bf16[4,128,384]{2,1,0:T(8,128)(2,1)S(1)}, bf16[4,128,384]{2,1,0:T(8,128)(2,1)S(1)}, u32[]{:S(2)}, u32[]{:S(2)}) collective-permute-start(bf16[4,128,384]{2,1,0:T(8,128)(2,1)S(1)} %slice.203), channel_id=1, source_target_pairs={{0,12},{1,13},{2,14},{3,15},{4,8},{5,9},{6,10},{7,11},{8,4},{9,5},... | collective-permute-start | bytes 1179656 | tf_op jit(solution)/shard_map/ppermute | solution.py:41
  110.8 8.2 %collective-permute-start.18 = (bf16[4,128,384]{2,1,0:T(8,128)(2,1)S(1)}, bf16[4,128,384]{2,1,0:T(8,128)(2,1)S(1)}, u32[]{:S(2)}, u32[]{:S(2)}) collective-permute-start(bf16[4,128,384]{2,1,0:T(8,128)(2,1)S(1)} %slice.205), channel_id=1, source_target_pairs={{0,3},{1,2},{2,1},{3,0},{4,7},{5,6},{6,5},{7,4},{8,11},{9,10},{10,... | collective-permute-start | bytes 1179656 | tf_op jit(solution)/shard_map/ppermute | solution.py:41
  112.3 8.1 %collective-permute-start.22 = (bf16[4,128,384]{2,1,0:T(8,128)(2,1)S(1)}, bf16[4,128,384]{2,1,0:T(8,128)(2,1)S(1)}, u32[]{:S(2)}, u32[]{:S(2)}) collective-permute-start(bf16[4,128,384]{2,1,0:T(8,128)(2,1)S(1)} %slice.204), channel_id=1, source_target_pairs={{0,1},{1,0},{2,3},{3,2},{4,5},{5,4},{6,7},{7,6},{8,9},{9,8},{10,11... | collective-permute-start | bytes 1179656 | tf_op jit(solution)/shard_map/ppermute | solution.py:41
  114.0 9.4 %collective-permute-start.27 = (bf16[2,128,384]{2,1,0:T(8,128)(2,1)S(1)}, bf16[2,128,384]{2,1,0:T(8,128)(2,1)S(1)}, u32[]{:S(2)}, u32[]{:S(2)}) collective-permute-start(bf16[2,128,384]{2,1,0:T(8,128)(2,1)S(1)} %slice.207), channel_id=1, source_target_pairs={{0,1},{1,0},{2,3},{3,2},{4,5},{5,4},{6,7},{7,6},{8,9},{9,8},{10,11... | collective-permute-start | bytes 589832 | tf_op jit(solution)/shard_map/ppermute | solution.py:41
  116.4 8.3 %collective-permute-start.31 = (bf16[2,128,384]{2,1,0:T(8,128)(2,1)S(1)}, bf16[2,128,384]{2,1,0:T(8,128)(2,1)S(1)}, u32[]{:S(2)}, u32[]{:S(2)}) collective-permute-start(bf16[2,128,384]{2,1,0:T(8,128)(2,1)S(1)} %slice.206), channel_id=1, source_target_pairs={{0,3},{1,2},{2,1},{3,0},{4,7},{5,6},{6,5},{7,4},{8,11},{9,10},{10,... | collective-permute-start | bytes 589832 | tf_op jit(solution)/shard_map/ppermute | solution.py:41
  125.5 11.7 %collective-permute-start.20 = (bf16[1,128,384]{2,1,0:T(8,128)(2,1)S(1)}, bf16[1,128,384]{2,1,0:T(8,128)(2,1)S(1)}, u32[]{:S(2)}, u32[]{:S(2)}) collective-permute-start(bf16[1,128,384]{2,1,0:T(8,128)(2,1)S(1)} %slice.213), channel_id=1, source_target_pairs={{0,1},{1,0},{2,3},{3,2},{4,5},{5,4},{6,7},{7,6},{8,9},{9,8},{10,11... | collective-permute-start | bytes 294920 | tf_op jit(solution)/shard_map/ppermute | solution.py:41
  126.7 10.5 %collective-permute-start.24 = (bf16[1,128,384]{2,1,0:T(8,128)(2,1)S(1)}, bf16[1,128,384]{2,1,0:T(8,128)(2,1)S(1)}, u32[]{:S(2)}, u32[]{:S(2)}) collective-permute-start(bf16[1,128,384]{2,1,0:T(8,128)(2,1)S(1)} %slice.212), channel_id=1, source_target_pairs={{0,3},{1,2},{2,1},{3,0},{4,7},{5,6},{6,5},{7,4},{8,11},{9,10},{10,... | collective-permute-start | bytes 294920 | tf_op jit(solution)/shard_map/ppermute | solution.py:41
  129.6 8.7 %collective-permute-start.33 = (bf16[256,384]{1,0:T(8,128)(2,1)S(1)}, bf16[256,384]{1,0:T(8,128)(2,1)S(1)}, u32[]{:S(2)}, u32[]{:S(2)}) collective-permute-start(bf16[256,384]{1,0:T(8,128)(2,1)S(1)} %pad_maximum_fusion.13), channel_id=1, source_target_pairs={{0,16},{16,0},{1,17},{17,1},{2,18},{18,2},{3,19},{19,3},{4,20},{20... | collective-permute-start | bytes 589832 | tf_op jit(solution)/shard_map/ppermute | solution.py:219
  (19 other events, 113.5 us)

commit v2 on v0

v2 whole, which is shorter than its diff:
```python
import jax
import jax.numpy as jnp
from jax import lax
from jax.experimental import pallas as pl
from jax.experimental.pallas import tpu as pltpu
from jax.sharding import PartitionSpec as P

TENSOR = 16
MASKS = (1, 3, 4, 12)
VMEM_LIMIT = 16 << 20


CHAINS = (((0, 2, 1, 3), (1, 3, 0, 2)), ((2, 0, 3, 1), (3, 1, 2, 0)))
SWAP = [(0, 1), (1, 0)]


def mask_of(core, chain, bits):
    mask = 0
    for phase in range(4):
        if bits >> phase & 1:
            mask ^= MASKS[CHAINS[core][chain][phase]]
    return mask


def block_of(core, me, chain, bits):
    return me ^ jnp.where(core == 0, mask_of(0, chain, bits), mask_of(1, chain, bits))


def exchange(value, chain, bits):
    pairs = []
    for core in range(2):
        mask = mask_of(core, chain, bits)
        pairs += [(core * TENSOR + t, core * TENSOR + (t ^ mask)) for t in range(TENSOR)]
    return lax.ppermute(value, ("expert", "tensor"), pairs)


together = lax.optimization_barrier


def exchange_pair(values, bits):
    values = together(list(values))
    return together([exchange(values[i], i, bits) for i in range(2)])


def dispatch_kernel(core_ref, ids_ref, tok_ref, own_ref, oth_ref, pos_ref):
    rows = tok_ref.shape[0]
    cap = own_ref.shape[0]
    core = core_ref[0]
    first, second = ids_ref[:, 0:1], ids_ref[:, 1:2]
    tri = (
        lax.broadcasted_iota(jnp.int32, (rows, rows), 0) > lax.broadcasted_iota(jnp.int32, (rows, rows), 1)
    ).astype(jnp.bfloat16)
    lane = lax.broadcasted_iota(jnp.int32, (rows, 128), 1)
    wanted = jnp.where(lane == 0, core, jnp.where(lane == 1, 1 - core, -1))
    match = ((first == wanted) | (second == wanted)).astype(jnp.bfloat16)
    earlier = jnp.dot(tri, match, preferred_element_type=jnp.float32).astype(jnp.int32)
    slot = jnp.where(match > 0, earlier, -1)
    pos_ref[...] = slot
    slots = lax.broadcasted_iota(jnp.int32, (rows, cap), 1)
    for k, out in enumerate((own_ref, oth_ref)):
        onehot = (slot[:, k : k + 1] == slots).astype(jnp.bfloat16)
        picked = lax.dot_general(
            onehot, tok_ref[...], (((0,), (0,)), ((), ())), preferred_element_type=jnp.float32
        )
        out[...] = picked.astype(jnp.bfloat16)


def dispatch(core, ids, tokens, cap):
    rows, width = tokens.shape
    vmem = pl.BlockSpec(memory_space=pltpu.VMEM)
    return pl.pallas_call(
        dispatch_kernel,
        in_specs=[pl.BlockSpec(memory_space=pltpu.SMEM), vmem, vmem],
        out_specs=[vmem, vmem, vmem],
        out_shape=[
            jax.ShapeDtypeStruct((cap, width), jnp.bfloat16),
            jax.ShapeDtypeStruct((cap, width), jnp.bfloat16),
            jax.ShapeDtypeStruct((rows, 128), jnp.int32),
        ],
        name="dispatch",
    )(core, ids, tokens)


def combine_kernel(core_ref, ids_ref, gates_ref, pos_ref, own_ref, oth_ref, out_ref):
    rows = ids_ref.shape[0]
    cap = own_ref.shape[0]
    core = core_ref[0]
    slots = lax.broadcasted_iota(jnp.int32, (rows, cap), 1)
    total = jnp.zeros(out_ref.shape, jnp.float32)
    for k, src in enumerate((own_ref, oth_ref)):
        expert = core if k == 0 else 1 - core
        weight = jnp.sum(jnp.where(ids_ref[...] == expert, gates_ref[...], 0.0), axis=1, keepdims=True)
        onehot = (pos_ref[:, k : k + 1] == slots).astype(jnp.bfloat16)
        total += weight * jnp.dot(onehot, src[...], preferred_element_type=jnp.float32)
    out_ref[...] = total.astype(jnp.bfloat16)


def combine(core, ids, gates, slot, own, oth):
    vmem = pl.BlockSpec(memory_space=pltpu.VMEM)
    return pl.pallas_call(
        combine_kernel,
        in_specs=[pl.BlockSpec(memory_space=pltpu.SMEM)] + [vmem] * 5,
        out_specs=vmem,
        out_shape=jax.ShapeDtypeStruct((ids.shape[0], own.shape[1]), jnp.bfloat16),
        name="combine",
    )(core, ids, gates, slot, own, oth)


def add_blocks(here_ref, pieces, wg, wu, acc_g, acc_u, fresh):
    core, me = here_ref[0], here_ref[1]
    rows, width = pieces[0][2].shape[1:]
    hidden = wg.shape[1]
    tile = hidden // 2
    for chain in range(2):
        at = slice(chain * rows, (chain + 1) * rows)
        for acc, w in ((acc_g, wg), (acc_u, wu)):
            for n in range(2):
                cols = slice(n * tile, (n + 1) * tile)
                total = jnp.zeros((rows, tile), jnp.float32) if fresh else acc[at, cols]
                for owner, first, ref in pieces:
                    if owner != chain:
                        continue
                    for k in range(ref.shape[0]):
                        start = pl.multiple_of(block_of(core, me, chain, first + k) * width, width)
                        total += jnp.dot(
                            ref[k], w[pl.ds(start, width), cols], preferred_element_type=jnp.float32
                        )
                yield acc, at, cols, total


def early_kernel(here_ref, ha, hb, ta, tb, fa, fb, wg, wu, acc_g, acc_u):
    pieces = [(0, 0, ha), (1, 0, hb), (0, 4, ta), (1, 4, tb), (0, 8, fa), (1, 8, fb)]
    for acc, at, cols, total in add_blocks(here_ref, pieces, wg, wu, acc_g, acc_u, True):
        acc[at, cols] = total


def down_blocks(here_ref, gated, wd, first, outs):
    core, me = here_ref[0], here_ref[1]
    count, rows, width = outs[0].shape
    for chain in range(2):
        for k in range(count):
            start = pl.multiple_of(block_of(core, me, chain, first + k) * width, width)
            y = jnp.dot(
                gated[chain * rows : (chain + 1) * rows, :],
                wd[:, pl.ds(start, width)],
                preferred_element_type=jnp.float32,
            )
            outs[chain][k] = y.astype(outs[chain].dtype)


def middle_kernel(here_ref, la, lb, acc_g, acc_u, wg, wu, wd, gated, sa, sb):
    pieces = [(0, 12, la), (1, 12, lb)]
    sums = {}
    for acc, at, cols, total in add_blocks(here_ref, pieces, wg, wu, acc_g, acc_u, False):
        if acc is acc_g:
            sums[at.start, cols.start] = total
        else:
            v = sums.pop((at.start, cols.start))
            gated[at, cols] = (v / (1.0 + jnp.exp(-v)) * total).astype(jnp.bfloat16)
    down_blocks(here_ref, gated, wd, 12, (sa, sb))


def late_kernel(here_ref, gated, wd, sa, sb, ka, kb, ra, rb):
    down_blocks(here_ref, gated, wd, 8, (sa, sb))
    down_blocks(here_ref, gated, wd, 4, (ka, kb))
    down_blocks(here_ref, gated, wd, 0, (ra, rb))


def local_kernel(kernel, name, cost, outs, here, *operands):
    vmem = pl.BlockSpec(memory_space=pltpu.VMEM)
    return pl.pallas_call(
        kernel,
        in_specs=[pl.BlockSpec(memory_space=pltpu.SMEM)] + [vmem] * len(operands),
        out_specs=[vmem] * len(outs),
        out_shape=[jax.ShapeDtypeStruct(shape, dtype) for shape, dtype in outs],
        compiler_params=pltpu.CompilerParams(vmem_limit_bytes=VMEM_LIMIT),
        cost_estimate=pl.CostEstimate(flops=cost, bytes_accessed=1 << 16, transcendentals=0),
        name=name,
    )(here, *operands)


def body(tokens, route_ids, route_gates, w_gate, w_up, w_down):
    rows, width = tokens.shape
    cap = rows // 2
    part = cap // 2
    hidden = w_gate.shape[2]
    wg, wu, wd = w_gate[0], w_up[0], w_down[0]
    core = lax.axis_index("expert").astype(jnp.int32).reshape(1)
    here = jnp.stack([lax.axis_index("expert"), lax.axis_index("tensor")]).astype(jnp.int32)
    both = range(2)

    own, oth, slot = dispatch(core, route_ids, tokens, cap)
    got = lax.ppermute(oth, "expert", SWAP)
    mine = [jnp.concatenate([v[i * part : (i + 1) * part] for v in (own, got)]) for i in both]
    mine = together(mine)
    near = together([[exchange(mine[i], i, bits) for bits in (1, 2, 3)] for i in both])
    held = together([jnp.stack([mine[i], *near[i]]) for i in both])
    third = exchange_pair(held, 4)
    fourth = exchange_pair(held, 8)
    last = exchange_pair(third, 8)

    bf16, f32 = jnp.bfloat16, jnp.float32
    block, square = (4, cap, width), (rows, hidden)
    sums = local_kernel(early_kernel, "early", 1 << 33, [(square, f32)] * 2, here, *held, *third, *fourth, wg, wu)
    gated, *send = local_kernel(
        middle_kernel, "middle", 1 << 32, [(square, bf16)] + [(block, bf16)] * 2, here, *last, *sums, wg, wu, wd
    )
    gone = exchange_pair(send, 8)
    out = local_kernel(late_kernel, "late", 1 << 20, [(block, bf16)] * 2 + [(block, f32)] * 4, here, gated, wd)
    also = exchange_pair(out[0:2], 8)
    second = exchange_pair([(out[2 + i] + gone[i].astype(f32)).astype(bf16) for i in both], 4)
    total = [out[4 + i] + also[i].astype(f32) + second[i].astype(f32) for i in both]
    send = together([total[i].astype(bf16) for i in both])
    near = together([[exchange(send[i][bits], i, bits) for bits in (1, 2, 3)] for i in both])
    done = [
        (total[i][0] + near[i][0].astype(f32) + near[i][1].astype(f32) + near[i][2].astype(f32)).astype(bf16)
        for i in both
    ]
    kept = jnp.concatenate([d[:part] for d in done])
    theirs = jnp.concatenate([d[part:] for d in done])
    back = lax.ppermute(theirs, "expert", SWAP)
    return combine(core, route_ids, route_gates, slot, kept, back)


def solution(mesh):
    placed = (
        P(("dp", "expert"), "tensor"),
        P(("dp", "expert"), None),
        P(("dp", "expert"), None),
        P("expert", None, "tensor"),
        P("expert", None, "tensor"),
        P("expert", "tensor", None),
    )
    return jax.shard_map(
        body, mesh=mesh, in_specs=placed, out_specs=P(("dp", "expert"), "tensor"), check_vma=False
    )
```

time: 239 us -> 124 us (0.52)
  waiting for transfers between devices: 172 us -> 52.1 us
  starting transfers between devices: 0.04 us -> 34.8 us
  Pallas kernels: 0 us -> 22.7 us
  matrix products: 20.9 us -> 0 us
  between operations: 13.6 us -> 0.23 us
  blocking collectives: 12.2 us -> 0 us
  other arithmetic: 6.63 us -> 3.28 us
  local copies, waits for them, and re-layouts: 13.7 us -> 10.4 us
    reduce_scatter x1 -> x0, waiting for transfers between devices: 99 us -> none  [body(): lax.psum_scatter(partial_out, 'tensor', scatter_dimension=2, tiled=True)]
    all_gather x1 -> x0, waiting for transfers between devices: 73 us -> none  [body(): piece = lax.all_gather(received, 'tensor', axis=2, tiled=True)]
    ppermute x0 -> x26, waiting for transfers between devices: none -> 52.1 us  [the longest x24 51.8 us: exchange(): return lax.ppermute(value, ('expert', 'tensor'), pairs)]
    ppermute x0 -> x26, starting transfers between devices: none -> 34.8 us  [the longest x24 31.5 us: exchange(): return lax.ppermute(value, ('expert', 'tensor'), pairs)]
    pallas_call x0 -> x5, Pallas kernels: none -> 22.7 us  [the longest x3 17.1 us: local_kernel(): pl.pallas_call(kernel, in_specs=[pl.BlockSpec(memory_space=pltpu.SMEM)] +...]
    dot_general x3 -> x0, matrix products: 20.9 us -> none  [the longest x1 8.05 us: body(): jnp.einsum('secd,edf->secf', grouped, w_gate, preferred_element_type=jnp....]
    all_to_all x2 -> x0, blocking collectives: 12.2 us -> none  [the longest x1 7.65 us: body(): lax.all_to_all(buffer, 'expert', split_axis=0, concat_axis=0, tiled=True)]
    unnamed x10 -> x20, local copies, waits for them, and re-layouts: 1.64 us -> 9.23 us
  transfers between devices with their start and end apart: 2 -> 26, of which waited for: 2 -> 11; matrix products, arithmetic and copies ran while one was open for 0% -> 3% of each run, Pallas kernels for 0% -> 11%
where the time goes in v2:
time: 124 us
  waiting for transfers between devices  52.1 us (42%)
  starting transfers between devices  34.8 us (28%)
  Pallas kernels  22.7 us (18%)
  local copies, waits for them, and re-layouts  10.4 us (8%)
  other arithmetic  3.28 us (3%)
    ppermute x24, waiting for transfers between devices, exchange(): return lax.ppermute(value, ('expert', 'tensor'), pairs)  51.8 us
    ppermute x24, starting transfers between devices, exchange(): return lax.ppermute(value, ('expert', 'tensor'), pairs)  31.5 us
    pallas_call x3, Pallas kernels, local_kernel(): pl.pallas_call(kernel, in_specs=[pl.BlockSpec(memory_space=pltpu.SMEM)] +...  17.1 us
    unnamed x20, local copies, waits for them, and re-layouts  9.23 us
    ppermute x1, starting transfers between devices, body(): got = lax.ppermute(oth, 'expert', SWAP)  3.24 us
    pallas_call x1, Pallas kernels, dispatch(): pl.pallas_call(dispatch_kernel, in_specs=[pl.BlockSpec(memory_space=pltpu...  3.02 us
    pallas_call x1, Pallas kernels, combine(): pl.pallas_call(combine_kernel, in_specs=[pl.BlockSpec(memory_space=pltpu....  2.53 us
  transfers between devices with their start and end apart: 26, of which 11 were waited for; matrix products, arithmetic and copies ran while one was open for 3% of the time, Pallas kernels for 11%

profile of v2, /device:TPU:1, one launch (start us, length us, event | category | flops | bytes accessed | tf_op | source)
XLA Modules:
  0.0 123.5 jit_solution(10029421598168955275)
XLA Ops:
  1.5 3.0 %dispatch.1 = (bf16[256,384]{1,0:T(8,128)(2,1)}, bf16[256,384]{1,0:T(8,128)(2,1)}, s32[512,128]{1,0:T(8,128)}) custom-call(s32[1]{0:T(128)} %bitcast.core_ref, s32[512,2]{1,0:T(8,128)} %copy.8.ids_ref, bf16[512,384]{1,0:T(8,128)(2,1)} %tok_ref.1), custom_call_target="tpu_custom_call" | custom-call | tf_op jit(solution)/shard_map/dispatch/pallas_call | solution.py:71
  4.6 3.2 %collective-permute-start = (bf16[256,384]{1,0:T(8,128)(2,1)}, bf16[256,384]{1,0:T(8,128)(2,1)S(1)}, u32[]{:S(2)}, u32[]{:S(2)}) collective-permute-start(bf16[256,384]{1,0:T(8,128)(2,1)} %get-tuple-element.61), channel_id=1, source_target_pairs={{0,16},{16,0},{1,17},{17,1},{2,18},{18,2},{3,19},{19,3},{4,20},{20... | collective-permute-start | bytes 589832 | tf_op jit(solution)/shard_map/ppermute | solution.py:193
  12.9 2.5 %collective-permute-start.5 = (bf16[256,384]{1,0:T(8,128)(2,1)S(1)}, bf16[256,384]{1,0:T(8,128)(2,1)S(1)}, u32[]{:S(2)}, u32[]{:S(2)}) collective-permute-start(bf16[256,384]{1,0:T(8,128)(2,1)S(1)} %get-tuple-element.63), channel_id=1, source_target_pairs={{0,12},{1,13},{2,14},{3,15},{4,8},{5,9},{6,10},{7,11},{8,4},{9,5},... | collective-permute-start | bytes 589832 | tf_op jit(solution)/shard_map/ppermute | solution.py:34
  15.4 2.3 %collective-permute-start.6 = (bf16[256,384]{1,0:T(8,128)(2,1)S(1)}, bf16[256,384]{1,0:T(8,128)(2,1)S(1)}, u32[]{:S(2)}, u32[]{:S(2)}) collective-permute-start(bf16[256,384]{1,0:T(8,128)(2,1)S(1)} %get-tuple-element.63), channel_id=1, source_target_pairs={{0,15},{1,14},{2,13},{3,12},{4,11},{5,10},{6,9},{7,8},{8,7},{9,6},... | collective-permute-start | bytes 589832 | tf_op jit(solution)/shard_map/ppermute | solution.py:34
  17.7 2.9 %collective-permute-done.3 = bf16[256,384]{1,0:T(8,128)(2,1)S(1)} collective-permute-done((bf16[256,384]{1,0:T(8,128)(2,1)S(1)}, bf16[256,384]{1,0:T(8,128)(2,1)S(1)}, u32[]{:S(2)}, u32[]{:S(2)}) %collective-permute-start.3) | collective-permute-done | bytes 196640 | tf_op jit(solution)/shard_map/ppermute | solution.py:34
  20.5 4.6 %collective-permute-done.6 = bf16[256,384]{1,0:T(8,128)(2,1)S(1)} collective-permute-done((bf16[256,384]{1,0:T(8,128)(2,1)S(1)}, bf16[256,384]{1,0:T(8,128)(2,1)S(1)}, u32[]{:S(2)}, u32[]{:S(2)}) %collective-permute-start.6) | collective-permute-done | bytes 196640 | tf_op jit(solution)/shard_map/ppermute | solution.py:34
  28.7 15.0 %collective-permute-done.11.fa = bf16[4,256,384]{2,1,0:T(8,128)(2,1)} collective-permute-done((bf16[4,256,384]{2,1,0:T(8,128)(2,1)}, bf16[4,256,384]{2,1,0:T(8,128)(2,1)}, u32[]{:S(2)}, u32[]{:S(2)}) %collective-permute-start.11) | collective-permute-done | bytes 786464 | tf_op jit(solution)/shard_map/ppermute | solution.py:34
  43.7 2.6 %collective-permute-done.7.ta = bf16[4,256,384]{2,1,0:T(8,128)(2,1)} collective-permute-done((bf16[4,256,384]{2,1,0:T(8,128)(2,1)}, bf16[4,256,384]{2,1,0:T(8,128)(2,1)}, u32[]{:S(2)}, u32[]{:S(2)}) %collective-permute-start.7) | collective-permute-done | bytes 786464 | tf_op jit(solution)/shard_map/ppermute | solution.py:34
  46.3 2.2 %collective-permute-start.10 = (bf16[4,256,384]{2,1,0:T(8,128)(2,1)}, bf16[4,256,384]{2,1,0:T(8,128)(2,1)S(1)}, u32[]{:S(2)}, u32[]{:S(2)}) collective-permute-start(bf16[4,256,384]{2,1,0:T(8,128)(2,1)} %collective-permute-done.8.tb), channel_id=1, source_target_pairs={{0,4},{1,5},{2,6},{3,7},{4,0},{5,1},{6,2},{7,3},{8,12},{9,13},{10,... | collective-permute-start | bytes 2359304 | tf_op jit(solution)/shard_map/ppermute | solution.py:34
  48.5 1.9 %collective-permute-start.9 = (bf16[4,256,384]{2,1,0:T(8,128)(2,1)}, bf16[4,256,384]{2,1,0:T(8,128)(2,1)S(1)}, u32[]{:S(2)}, u32[]{:S(2)}) collective-permute-start(bf16[4,256,384]{2,1,0:T(8,128)(2,1)} %collective-permute-done.7.ta), channel_id=1, source_target_pairs={{0,12},{1,13},{2,14},{3,15},{4,8},{5,9},{6,10},{7,11},{8,4},{9,5},... | collective-permute-start | bytes 2359304 | tf_op jit(solution)/shard_map/ppermute | solution.py:34
  50.4 2.9 %copy-done = bf16[1,6144,512]{2,1,0:T(8,128)(2,1)S(1)} copy-done((bf16[1,6144,512]{2,1,0:T(8,128)(2,1)S(1)}, bf16[1,6144,512]{2,1,0:T(8,128)(2,1)}, u32[]{:S(2)}) %copy-start) | copy-done | bytes 6291480
  53.3 2.9 %copy-done.1 = bf16[1,6144,512]{2,1,0:T(8,128)(2,1)S(1)} copy-done((bf16[1,6144,512]{2,1,0:T(8,128)(2,1)S(1)}, bf16[1,6144,512]{2,1,0:T(8,128)(2,1)}, u32[]{:S(2)}) %copy-start.1) | copy-done | bytes 6291480
  56.3 8.9 %early.1 = (f32[512,512]{1,0:T(8,128)S(1)}, f32[512,512]{1,0:T(8,128)S(1)}) custom-call(s32[2]{0:T(128)S(1)} %pad_add_fusion.here_ref, bf16[4,256,384]{2,1,0:T(8,128)(2,1)} %pad_maximum_fusion.ha, bf16[4,256,384]{2,1,0:T(8,128)(2,1)S(1)} %pad_maximum_fusion.1.hb, bf16[4,256,384]{2,1,0:T(8,128)(2,1)} %collective-permute-done.7.ta, ...), custom_call_target="tpu_custom_call" | custom-call | flops 8589934592 | bytes 65536 | tf_op jit(solution)/shard_map/early/pallas_call | solution.py:171
  65.3 4.1 %middle.1 = (bf16[512,512]{1,0:T(8,128)(2,1)S(1)}, bf16[4,256,384]{2,1,0:T(8,128)(2,1)S(1)}, bf16[4,256,384]{2,1,0:T(8,128)(2,1)S(1)}) custom-call(s32[2]{0:T(128)S(1)} %pad_add_fusion.here_ref, bf16[4,256,384]{2,1,0:T(8,128)(2,1)S(1)} %collective-permute-done.9.la, bf16[4,256,384]{2,1,0:T(8,128)(2,1)S(1)} %collective-permute-done.10.lb, ...), custom_call_target="tpu_custom_call" | custom-call | flops 4294967296 | bytes 65536 | tf_op jit(solution)/shard_map/middle/pallas_call | solution.py:171
  70.3 4.0 %late.1 = (bf16[4,256,384]{2,1,0:T(8,128)(2,1)S(1)}, bf16[4,256,384]{2,1,0:T(8,128)(2,1)S(1)}, f32[4,256,384]{2,1,0:T(8,128)S(1)}, f32[4,256,384]{2,1,0:T(8,128)...) custom-call(s32[2]{0:T(128)S(1)} %pad_add_fusion.here_ref, bf16[512,512]{1,0:T(8,128)(2,1)S(1)} %get-tuple-element.84.gated, ...), custom_call_target="tpu_custom_call" | custom-call | flops 1048576 | bytes 65536 | tf_op jit(solution)/shard_map/late/pallas_call | solution.py:171
  74.4 2.0 %collective-permute-start.13 = (bf16[4,256,384]{2,1,0:T(8,128)(2,1)S(1)}, bf16[4,256,384]{2,1,0:T(8,128)(2,1)S(1)}, u32[]{:S(2)}, u32[]{:S(2)}) collective-permute-start(bf16[4,256,384]{2,1,0:T(8,128)(2,1)S(1)} %get-tuple-element.88), channel_id=1, source_target_pairs={{0,12},{1,13},{2,14},{3,15},{4,8},{5,9},{6,10},{7,11},{8,4},{9,5},... | collective-permute-start | bytes 2359304 | tf_op jit(solution)/shard_map/ppermute | solution.py:34
  77.2 4.7 %collective-permute-done.15 = bf16[4,256,384]{2,1,0:T(8,128)(2,1)S(1)} collective-permute-done((bf16[4,256,384]{2,1,0:T(8,128)(2,1)S(1)}, bf16[4,256,384]{2,1,0:T(8,128)(2,1)S(1)}, u32[]{:S(2)}, u32[]{:S(2)}) %collective-permute-start.15) | collective-permute-done | bytes 786464 | tf_op jit(solution)/shard_map/ppermute | solution.py:34
  83.6 8.7 %collective-permute-done.13 = bf16[4,256,384]{2,1,0:T(8,128)(2,1)S(1)} collective-permute-done((bf16[4,256,384]{2,1,0:T(8,128)(2,1)S(1)}, bf16[4,256,384]{2,1,0:T(8,128)(2,1)S(1)}, u32[]{:S(2)}, u32[]{:S(2)}) %collective-permute-start.13) | collective-permute-done | bytes 786464 | tf_op jit(solution)/shard_map/ppermute | solution.py:34
  92.3 6.5 %collective-permute-done.17 = bf16[4,256,384]{2,1,0:T(8,128)(2,1)S(1)} collective-permute-done((bf16[4,256,384]{2,1,0:T(8,128)(2,1)S(1)}, bf16[4,256,384]{2,1,0:T(8,128)(2,1)S(1)}, u32[]{:S(2)}, u32[]{:S(2)}) %collective-permute-start.17) | collective-permute-done | bytes 786464 | tf_op jit(solution)/shard_map/ppermute | solution.py:34
  104.1 2.0 %collective-permute-start.23 = (bf16[256,384]{1,0:T(8,128)(2,1)S(1)}, bf16[256,384]{1,0:T(8,128)(2,1)S(1)}, u32[]{:S(2)}, u32[]{:S(2)}) collective-permute-start(bf16[256,384]{1,0:T(8,128)(2,1)S(1)} %get-tuple-element.118), channel_id=1, source_target_pairs={{0,12},{1,13},{2,14},{3,15},{4,8},{5,9},{6,10},{7,11},{8,4},{9,5},... | collective-permute-start | bytes 589832 | tf_op jit(solution)/shard_map/ppermute | solution.py:34
  106.1 2.1 %collective-permute-done.19 = bf16[256,384]{1,0:T(8,128)(2,1)S(1)} collective-permute-done((bf16[256,384]{1,0:T(8,128)(2,1)S(1)}, bf16[256,384]{1,0:T(8,128)(2,1)S(1)}, u32[]{:S(2)}, u32[]{:S(2)}) %collective-permute-start.19) | collective-permute-done | bytes 196640 | tf_op jit(solution)/shard_map/ppermute | solution.py:34
  108.2 5.8 %collective-permute-start.24 = (bf16[256,384]{1,0:T(8,128)(2,1)S(1)}, bf16[256,384]{1,0:T(8,128)(2,1)S(1)}, u32[]{:S(2)}, u32[]{:S(2)}) collective-permute-start(bf16[256,384]{1,0:T(8,128)(2,1)S(1)} %get-tuple-element.117), channel_id=1, source_target_pairs={{0,15},{1,14},{2,13},{3,12},{4,11},{5,10},{6,9},{7,8},{8,7},{9,6},... | collective-permute-start | bytes 589832 | tf_op jit(solution)/shard_map/ppermute | solution.py:34
  114.1 4.0 %collective-permute-done.24 = bf16[256,384]{1,0:T(8,128)(2,1)S(1)} collective-permute-done((bf16[256,384]{1,0:T(8,128)(2,1)S(1)}, bf16[256,384]{1,0:T(8,128)(2,1)S(1)}, u32[]{:S(2)}, u32[]{:S(2)}) %collective-permute-start.24) | collective-permute-done | bytes 196640 | tf_op jit(solution)/shard_map/ppermute | solution.py:34
  121.0 2.5 %combine.1 = bf16[512,384]{1,0:T(8,128)(2,1)} custom-call(s32[1]{0:T(128)} %bitcast.core_ref, s32[512,2]{1,0:T(8,128)} %copy.8.ids_ref, f32[512,2]{1,0:T(8,128)} %copy.9.gates_ref, s32[512,128]{1,0:T(8,128)} %get-tuple-element.59.pos_ref, bf16[256,384]{1,0:T(8,128)(2,1)} %pad_maximum_fusion.4.own_ref, bf16[256,384]{1,0:T(8,128)(2,1)} %copy-done.3), custom_call_target="tpu_custom_call" | custom-call | tf_op jit(solution)/shard_map/combine/pallas_call | solution.py:100
  (73 shorter events, 21.8 us)
Async XLA Ops:
  9.2 6.2 %collective-permute-start.1 = (bf16[256,384]{1,0:T(8,128)(2,1)S(1)}, bf16[256,384]{1,0:T(8,128)(2,1)S(1)}, u32[]{:S(2)}, u32[]{:S(2)}) collective-permute-start(bf16[256,384]{1,0:T(8,128)(2,1)S(1)} %get-tuple-element.62), channel_id=1, source_target_pairs={{0,1},{1,0},{2,3},{3,2},{4,5},{5,4},{6,7},{7,6},{8,9},{9,8},{10,11... | collective-permute-start | bytes 589832 | tf_op jit(solution)/shard_map/ppermute | solution.py:34
  9.3 8.4 %collective-permute-start.2 = (bf16[256,384]{1,0:T(8,128)(2,1)S(1)}, bf16[256,384]{1,0:T(8,128)(2,1)S(1)}, u32[]{:S(2)}, u32[]{:S(2)}) collective-permute-start(bf16[256,384]{1,0:T(8,128)(2,1)S(1)} %get-tuple-element.62), channel_id=1, source_target_pairs={{0,4},{1,5},{2,6},{3,7},{4,0},{5,1},{6,2},{7,3},{8,12},{9,13},{10,... | collective-permute-start | bytes 589832 | tf_op jit(solution)/shard_map/ppermute | solution.py:34
  10.0 10.5 %collective-permute-start.3 = (bf16[256,384]{1,0:T(8,128)(2,1)S(1)}, bf16[256,384]{1,0:T(8,128)(2,1)S(1)}, u32[]{:S(2)}, u32[]{:S(2)}) collective-permute-start(bf16[256,384]{1,0:T(8,128)(2,1)S(1)} %get-tuple-element.62), channel_id=1, source_target_pairs={{0,5},{1,4},{2,7},{3,6},{4,1},{5,0},{6,3},{7,2},{8,13},{9,12},{10,... | collective-permute-start | bytes 589832 | tf_op jit(solution)/shard_map/ppermute | solution.py:34
  11.9 8.6 %collective-permute-start.4 = (bf16[256,384]{1,0:T(8,128)(2,1)S(1)}, bf16[256,384]{1,0:T(8,128)(2,1)S(1)}, u32[]{:S(2)}, u32[]{:S(2)}) collective-permute-start(bf16[256,384]{1,0:T(8,128)(2,1)S(1)} %get-tuple-element.63), channel_id=1, source_target_pairs={{0,3},{1,2},{2,1},{3,0},{4,7},{5,6},{6,5},{7,4},{8,11},{9,10},{10,... | collective-permute-start | bytes 589832 | tf_op jit(solution)/shard_map/ppermute | solution.py:34
  12.9 7.6 %collective-permute-start.5 = (bf16[256,384]{1,0:T(8,128)(2,1)S(1)}, bf16[256,384]{1,0:T(8,128)(2,1)S(1)}, u32[]{:S(2)}, u32[]{:S(2)}) collective-permute-start(bf16[256,384]{1,0:T(8,128)(2,1)S(1)} %get-tuple-element.63), channel_id=1, source_target_pairs={{0,12},{1,13},{2,14},{3,15},{4,8},{5,9},{6,10},{7,11},{8,4},{9,5},... | collective-permute-start | bytes 589832 | tf_op jit(solution)/shard_map/ppermute | solution.py:34
  15.4 9.8 %collective-permute-start.6 = (bf16[256,384]{1,0:T(8,128)(2,1)S(1)}, bf16[256,384]{1,0:T(8,128)(2,1)S(1)}, u32[]{:S(2)}, u32[]{:S(2)}) collective-permute-start(bf16[256,384]{1,0:T(8,128)(2,1)S(1)} %get-tuple-element.63), channel_id=1, source_target_pairs={{0,15},{1,14},{2,13},{3,12},{4,11},{5,10},{6,9},{7,8},{8,7},{9,6},... | collective-permute-start | bytes 589832 | tf_op jit(solution)/shard_map/ppermute | solution.py:34
  26.3 17.4 %collective-permute-start.11 = (bf16[4,256,384]{2,1,0:T(8,128)(2,1)}, bf16[4,256,384]{2,1,0:T(8,128)(2,1)}, u32[]{:S(2)}, u32[]{:S(2)}) collective-permute-start(bf16[4,256,384]{2,1,0:T(8,128)(2,1)} %pad_maximum_fusion.ha), channel_id=1, source_target_pairs={{0,12},{1,13},{2,14},{3,15},{4,8},{5,9},{6,10},{7,11},{8,4},{9,5},... | collective-permute-start | bytes 2359304 | tf_op jit(solution)/shard_map/ppermute | solution.py:34
  27.0 16.7 %collective-permute-start.12 = (bf16[4,256,384]{2,1,0:T(8,128)(2,1)S(1)}, bf16[4,256,384]{2,1,0:T(8,128)(2,1)}, u32[]{:S(2)}, u32[]{:S(2)}) collective-permute-start(bf16[4,256,384]{2,1,0:T(8,128)(2,1)S(1)} %pad_maximum_fusion.1.hb), channel_id=1, source_target_pairs={{0,4},{1,5},{2,6},{3,7},{4,0},{5,1},{6,2},{7,3},{8,12},{9,13},{10,... | collective-permute-start | bytes 2359304 | tf_op jit(solution)/shard_map/ppermute | solution.py:34
  27.0 19.3 %collective-permute-start.7 = (bf16[4,256,384]{2,1,0:T(8,128)(2,1)}, bf16[4,256,384]{2,1,0:T(8,128)(2,1)}, u32[]{:S(2)}, u32[]{:S(2)}) collective-permute-start(bf16[4,256,384]{2,1,0:T(8,128)(2,1)} %pad_maximum_fusion.ha), channel_id=1, source_target_pairs={{0,3},{1,2},{2,1},{3,0},{4,7},{5,6},{6,5},{7,4},{8,11},{9,10},{10,... | collective-permute-start | bytes 2359304 | tf_op jit(solution)/shard_map/ppermute | solution.py:34
  27.8 18.5 %collective-permute-start.8 = (bf16[4,256,384]{2,1,0:T(8,128)(2,1)S(1)}, bf16[4,256,384]{2,1,0:T(8,128)(2,1)}, u32[]{:S(2)}, u32[]{:S(2)}) collective-permute-start(bf16[4,256,384]{2,1,0:T(8,128)(2,1)S(1)} %pad_maximum_fusion.1.hb), channel_id=1, source_target_pairs={{0,1},{1,0},{2,3},{3,2},{4,5},{5,4},{6,7},{7,6},{8,9},{9,8},{10,11... | collective-permute-start | bytes 2359304 | tf_op jit(solution)/shard_map/ppermute | solution.py:34
  46.3 18.9 %collective-permute-start.10 = (bf16[4,256,384]{2,1,0:T(8,128)(2,1)}, bf16[4,256,384]{2,1,0:T(8,128)(2,1)S(1)}, u32[]{:S(2)}, u32[]{:S(2)}) collective-permute-start(bf16[4,256,384]{2,1,0:T(8,128)(2,1)} %collective-permute-done.8.tb), channel_id=1, source_target_pairs={{0,4},{1,5},{2,6},{3,7},{4,0},{5,1},{6,2},{7,3},{8,12},{9,13},{10,... | collective-permute-start | bytes 2359304 | tf_op jit(solution)/shard_map/ppermute | solution.py:34
  48.5 16.7 %collective-permute-start.9 = (bf16[4,256,384]{2,1,0:T(8,128)(2,1)}, bf16[4,256,384]{2,1,0:T(8,128)(2,1)S(1)}, u32[]{:S(2)}, u32[]{:S(2)}) collective-permute-start(bf16[4,256,384]{2,1,0:T(8,128)(2,1)} %collective-permute-done.7.ta), channel_id=1, source_target_pairs={{0,12},{1,13},{2,14},{3,15},{4,8},{5,9},{6,10},{7,11},{8,4},{9,5},... | collective-permute-start | bytes 2359304 | tf_op jit(solution)/shard_map/ppermute | solution.py:34
  69.4 12.4 %collective-permute-start.15 = (bf16[4,256,384]{2,1,0:T(8,128)(2,1)S(1)}, bf16[4,256,384]{2,1,0:T(8,128)(2,1)S(1)}, u32[]{:S(2)}, u32[]{:S(2)}) collective-permute-start(bf16[4,256,384]{2,1,0:T(8,128)(2,1)S(1)} %get-tuple-element.94), channel_id=1, source_target_pairs={{0,12},{1,13},{2,14},{3,15},{4,8},{5,9},{6,10},{7,11},{8,4},{9,5},... | collective-permute-start | bytes 2359304 | tf_op jit(solution)/shard_map/ppermute | solution.py:34
  70.3 11.6 %collective-permute-start.16 = (bf16[4,256,384]{2,1,0:T(8,128)(2,1)S(1)}, bf16[4,256,384]{2,1,0:T(8,128)(2,1)S(1)}, u32[]{:S(2)}, u32[]{:S(2)}) collective-permute-start(bf16[4,256,384]{2,1,0:T(8,128)(2,1)S(1)} %get-tuple-element.95), channel_id=1, source_target_pairs={{0,4},{1,5},{2,6},{3,7},{4,0},{5,1},{6,2},{7,3},{8,12},{9,13},{10,... | collective-permute-start | bytes 2359304 | tf_op jit(solution)/shard_map/ppermute | solution.py:34
  74.4 17.9 %collective-permute-start.13 = (bf16[4,256,384]{2,1,0:T(8,128)(2,1)S(1)}, bf16[4,256,384]{2,1,0:T(8,128)(2,1)S(1)}, u32[]{:S(2)}, u32[]{:S(2)}) collective-permute-start(bf16[4,256,384]{2,1,0:T(8,128)(2,1)S(1)} %get-tuple-element.88), channel_id=1, source_target_pairs={{0,12},{1,13},{2,14},{3,15},{4,8},{5,9},{6,10},{7,11},{8,4},{9,5},... | collective-permute-start | bytes 2359304 | tf_op jit(solution)/shard_map/ppermute | solution.py:34
  76.3 16.0 %collective-permute-start.14 = (bf16[4,256,384]{2,1,0:T(8,128)(2,1)S(1)}, bf16[4,256,384]{2,1,0:T(8,128)(2,1)S(1)}, u32[]{:S(2)}, u32[]{:S(2)}) collective-permute-start(bf16[4,256,384]{2,1,0:T(8,128)(2,1)S(1)} %get-tuple-element.89), channel_id=1, source_target_pairs={{0,4},{1,5},{2,6},{3,7},{4,0},{5,1},{6,2},{7,3},{8,12},{9,13},{10,... | collective-permute-start | bytes 2359304 | tf_op jit(solution)/shard_map/ppermute | solution.py:34
  82.4 16.4 %collective-permute-start.17 = (bf16[4,256,384]{2,1,0:T(8,128)(2,1)S(1)}, bf16[4,256,384]{2,1,0:T(8,128)(2,1)S(1)}, u32[]{:S(2)}, u32[]{:S(2)}) collective-permute-start(bf16[4,256,384]{2,1,0:T(8,128)(2,1)S(1)} %add_convert_fusion.1), channel_id=1, source_target_pairs={{0,3},{1,2},{2,1},{3,0},{4,7},{5,6},{6,5},{7,4},{8,11},{9,10},{10,... | collective-permute-start | bytes 2359304 | tf_op jit(solution)/shard_map/ppermute | solution.py:34
  83.6 15.8 %collective-permute-start.18 = (bf16[4,256,384]{2,1,0:T(8,128)(2,1)S(1)}, bf16[4,256,384]{2,1,0:T(8,128)(2,1)S(1)}, u32[]{:S(2)}, u32[]{:S(2)}) collective-permute-start(bf16[4,256,384]{2,1,0:T(8,128)(2,1)S(1)} %add_convert_fusion), channel_id=1, source_target_pairs={{0,1},{1,0},{2,3},{3,2},{4,5},{5,4},{6,7},{7,6},{8,9},{9,8},{10,11... | collective-permute-start | bytes 2359304 | tf_op jit(solution)/shard_map/ppermute | solution.py:34
  100.1 8.1 %collective-permute-start.19 = (bf16[256,384]{1,0:T(8,128)(2,1)S(1)}, bf16[256,384]{1,0:T(8,128)(2,1)S(1)}, u32[]{:S(2)}, u32[]{:S(2)}) collective-permute-start(bf16[256,384]{1,0:T(8,128)(2,1)S(1)} %get-tuple-element.122), channel_id=1, source_target_pairs={{0,1},{1,0},{2,3},{3,2},{4,5},{5,4},{6,7},{7,6},{8,9},{9,8},{10,11... | collective-permute-start | bytes 589832 | tf_op jit(solution)/shard_map/ppermute | solution.py:34
  100.4 13.6 %collective-permute-start.20 = (bf16[256,384]{1,0:T(8,128)(2,1)S(1)}, bf16[256,384]{1,0:T(8,128)(2,1)S(1)}, u32[]{:S(2)}, u32[]{:S(2)}) collective-permute-start(bf16[256,384]{1,0:T(8,128)(2,1)S(1)} %get-tuple-element.121), channel_id=1, source_target_pairs={{0,4},{1,5},{2,6},{3,7},{4,0},{5,1},{6,2},{7,3},{8,12},{9,13},{10,... | collective-permute-start | bytes 589832 | tf_op jit(solution)/shard_map/ppermute | solution.py:34
  101.2 12.8 %collective-permute-start.21 = (bf16[256,384]{1,0:T(8,128)(2,1)S(1)}, bf16[256,384]{1,0:T(8,128)(2,1)S(1)}, u32[]{:S(2)}, u32[]{:S(2)}) collective-permute-start(bf16[256,384]{1,0:T(8,128)(2,1)S(1)} %get-tuple-element.120), channel_id=1, source_target_pairs={{0,5},{1,4},{2,7},{3,6},{4,1},{5,0},{6,3},{7,2},{8,13},{9,12},{10,... | collective-permute-start | bytes 589832 | tf_op jit(solution)/shard_map/ppermute | solution.py:34
  102.9 11.1 %collective-permute-start.22 = (bf16[256,384]{1,0:T(8,128)(2,1)S(1)}, bf16[256,384]{1,0:T(8,128)(2,1)S(1)}, u32[]{:S(2)}, u32[]{:S(2)}) collective-permute-start(bf16[256,384]{1,0:T(8,128)(2,1)S(1)} %get-tuple-element.119), channel_id=1, source_target_pairs={{0,3},{1,2},{2,1},{3,0},{4,7},{5,6},{6,5},{7,4},{8,11},{9,10},{10,... | collective-permute-start | bytes 589832 | tf_op jit(solution)/shard_map/ppermute | solution.py:34
  104.1 9.9 %collective-permute-start.23 = (bf16[256,384]{1,0:T(8,128)(2,1)S(1)}, bf16[256,384]{1,0:T(8,128)(2,1)S(1)}, u32[]{:S(2)}, u32[]{:S(2)}) collective-permute-start(bf16[256,384]{1,0:T(8,128)(2,1)S(1)} %get-tuple-element.118), channel_id=1, source_target_pairs={{0,12},{1,13},{2,14},{3,15},{4,8},{5,9},{6,10},{7,11},{8,4},{9,5},... | collective-permute-start | bytes 589832 | tf_op jit(solution)/shard_map/ppermute | solution.py:34
  108.2 9.8 %collective-permute-start.24 = (bf16[256,384]{1,0:T(8,128)(2,1)S(1)}, bf16[256,384]{1,0:T(8,128)(2,1)S(1)}, u32[]{:S(2)}, u32[]{:S(2)}) collective-permute-start(bf16[256,384]{1,0:T(8,128)(2,1)S(1)} %get-tuple-element.117), channel_id=1, source_target_pairs={{0,15},{1,14},{2,13},{3,12},{4,11},{5,10},{6,9},{7,8},{8,7},{9,6},... | collective-permute-start | bytes 589832 | tf_op jit(solution)/shard_map/ppermute | solution.py:34
  (11 other events, 111.7 us)

commit v3 on v2

--- a/solution.py
+++ b/solution.py
@@ -8,9 +8,11 @@
 TENSOR = 16
 MASKS = (1, 3, 4, 12)
 VMEM_LIMIT = 16 << 20
-
-
-CHAINS = (((0, 2, 1, 3), (1, 3, 0, 2)), ((2, 0, 3, 1), (3, 1, 2, 0)))
+LOAD_VMEM = 32 << 20
+LOAD, EARLY, MIDDLE, LATE = 1 << 33, 1 << 33, 1 << 32, 1 << 20
+
+
+CHAINS = (((0, 2, 1, 3), (1, 3, 0, 2)), ((1, 3, 2, 0), (0, 2, 3, 1)))
 SWAP = [(0, 1), (1, 0)]
 
 
@@ -42,68 +44,119 @@
     return together([exchange(values[i], i, bits) for i in range(2)])
 
 
-def dispatch_kernel(core_ref, ids_ref, tok_ref, own_ref, oth_ref, pos_ref):
+def dispatch_kernel(core_ref, ids_ref, tok_ref, out_ref, slot_ref):
     rows = tok_ref.shape[0]
-    cap = own_ref.shape[0]
+    cap = out_ref.shape[0] // 2
     core = core_ref[0]
-    first, second = ids_ref[:, 0:1], ids_ref[:, 1:2]
+    kinds = slot_ref.shape[0]
     tri = (
-        lax.broadcasted_iota(jnp.int32, (rows, rows), 0) > lax.broadcasted_iota(jnp.int32, (rows, rows), 1)
+        lax.broadcasted_iota(jnp.int32, (rows, rows), 0) < lax.broadcasted_iota(jnp.int32, (rows, rows), 1)
     ).astype(jnp.bfloat16)
-    lane = lax.broadcasted_iota(jnp.int32, (rows, 128), 1)
-    wanted = jnp.where(lane == 0, core, jnp.where(lane == 1, 1 - core, -1))
-    match = ((first == wanted) | (second == wanted)).astype(jnp.bfloat16)
-    earlier = jnp.dot(tri, match, preferred_element_type=jnp.float32).astype(jnp.int32)
+    kind = lax.broadcasted_iota(jnp.int32, (kinds, rows), 0)
+    wanted = jnp.where(kind == 0, core, jnp.where(kind == 1, 1 - core, -1))
+    match = ((ids_ref[0:1, :] == wanted) | (ids_ref[1:2, :] == wanted)).astype(jnp.bfloat16)
+    earlier = jnp.dot(match, tri, preferred_element_type=jnp.float32).astype(jnp.int32)
     slot = jnp.where(match > 0, earlier, -1)
-    pos_ref[...] = slot
-    slots = lax.broadcasted_iota(jnp.int32, (rows, cap), 1)
-    for k, out in enumerate((own_ref, oth_ref)):
-        onehot = (slot[:, k : k + 1] == slots).astype(jnp.bfloat16)
-        picked = lax.dot_general(
-            onehot, tok_ref[...], (((0,), (0,)), ((), ())), preferred_element_type=jnp.float32
-        )
-        out[...] = picked.astype(jnp.bfloat16)
-
-
-def dispatch(core, ids, tokens, cap):
+    slot_ref[...] = slot
+    slots = lax.broadcasted_iota(jnp.int32, (cap, rows), 0)
+    for k in range(2):
+        onehot = (slot[k : k + 1, :] == slots).astype(jnp.bfloat16)
+        picked = jnp.dot(onehot, tok_ref[...], preferred_element_type=jnp.float32)
+        out_ref[k * cap : (k + 1) * cap, :] = picked.astype(jnp.bfloat16)
+
+
+def dispatch(core, ids, tokens):
     rows, width = tokens.shape
     vmem = pl.BlockSpec(memory_space=pltpu.VMEM)
     return pl.pallas_call(
         dispatch_kernel,
         in_specs=[pl.BlockSpec(memory_space=pltpu.SMEM), vmem, vmem],
-        out_specs=[vmem, vmem, vmem],
+        out_specs=[vmem, vmem],
         out_shape=[
-            jax.ShapeDtypeStruct((cap, width), jnp.bfloat16),
-            jax.ShapeDtypeStruct((cap, width), jnp.bfloat16),
-            jax.ShapeDtypeStruct((rows, 128), jnp.int32),
+            jax.ShapeDtypeStruct((rows, width), jnp.bfloat16),
+            jax.ShapeDtypeStruct((16, rows), jnp.int32),
         ],
         name="dispatch",
     )(core, ids, tokens)
 
 
-def combine_kernel(core_ref, ids_ref, gates_ref, pos_ref, own_ref, oth_ref, out_ref):
-    rows = ids_ref.shape[0]
-    cap = own_ref.shape[0]
+def weigh_kernel(core_ref, ids_ref, gates_ref, slot_ref, pick_ref, weight_ref):
+    rows = pick_ref.shape[0]
+    cap = pick_ref.shape[1] // 2
     core = core_ref[0]
-    slots = lax.broadcasted_iota(jnp.int32, (rows, cap), 1)
+    kind = lax.broadcasted_iota(jnp.int32, (128, rows), 0)
+    wanted = jnp.where(kind == 0, core, jnp.where(kind == 1, 1 - core, -1))
+    weight = jnp.where(ids_ref[0:1, :] == wanted, gates_ref[0:1, :], 0.0)
+    weight += jnp.where(ids_ref[1:2, :] == wanted, gates_ref[1:2, :], 0.0)
+    weight_ref[...] = weight.T
+    slot = jnp.where(kind == 0, slot_ref[0:1, :], slot_ref[1:2, :]).astype(jnp.float32).T
+    slots = lax.broadcasted_iota(jnp.int32, (rows, cap), 1).astype(jnp.float32)
+    for k in range(2):
+        pick_ref[:, k * cap : (k + 1) * cap] = (slot[:, k : k + 1] == slots).astype(jnp.bfloat16)
+
+
+def weigh(core, ids, gates, slot):
+    rows = ids.shape[1]
+    vmem = pl.BlockSpec(memory_space=pltpu.VMEM)
+    return pl.pallas_call(
+        weigh_kernel,
+        in_specs=[pl.BlockSpec(memory_space=pltpu.SMEM)] + [vmem] * 3,
+        out_specs=[vmem, vmem],
+        out_shape=[
+            jax.ShapeDtypeStruct((rows, rows), jnp.bfloat16),
+            jax.ShapeDtypeStruct((rows, 128), jnp.float32),
+        ],
+        cost_estimate=pl.CostEstimate(flops=1 << 30, bytes_accessed=1 << 16, transcendentals=0),
+        name="weigh",
+    )(core, ids, gates, slot)
+
+
+def combine_kernel(pick_ref, weight_ref, own_ref, back_ref, na_ref, nb_ref, nc_ref, out_ref):
+    cap = own_ref.shape[1]
     total = jnp.zeros(out_ref.shape, jnp.float32)
-    for k, src in enumerate((own_ref, oth_ref)):
-        expert = core if k == 0 else 1 - core
-        weight = jnp.sum(jnp.where(ids_ref[...] == expert, gates_ref[...], 0.0), axis=1, keepdims=True)
-        onehot = (pos_ref[:, k : k + 1] == slots).astype(jnp.bfloat16)
-        total += weight * jnp.dot(onehot, src[...], preferred_element_type=jnp.float32)
+    for k, first in enumerate((own_ref, back_ref)):
+        at = slice(k * cap, (k + 1) * cap)
+        done = first[0].astype(jnp.float32)
+        for ref in (na_ref, nb_ref, nc_ref):
+            done += ref[at, :].astype(jnp.float32)
+        row = jnp.dot(pick_ref[:, at], done.astype(jnp.bfloat16), preferred_element_type=jnp.float32)
+        total += weight_ref[:, k : k + 1] * row
     out_ref[...] = total.astype(jnp.bfloat16)
 
 
-def combine(core, ids, gates, slot, own, oth):
+def combine(pick, weight, own, back, near):
     vmem = pl.BlockSpec(memory_space=pltpu.VMEM)
     return pl.pallas_call(
         combine_kernel,
-        in_specs=[pl.BlockSpec(memory_space=pltpu.SMEM)] + [vmem] * 5,
+        in_specs=[vmem] * 7,
         out_specs=vmem,
-        out_shape=jax.ShapeDtypeStruct((ids.shape[0], own.shape[1]), jnp.bfloat16),
+        out_shape=jax.ShapeDtypeStruct((pick.shape[0], own.shape[2]), jnp.bfloat16),
         name="combine",
-    )(core, ids, gates, slot, own, oth)
+    )(pick, weight, own, back, *near)
+
+
+def load_kernel(here_ref, *refs):
+    sources, targets, sem = refs[:3], refs[3:6], refs[6]
+    copies = [pltpu.make_async_copy(a, b, sem.at[i]) for i, (a, b) in enumerate(zip(sources, targets))]
+    for copy in copies:
+        copy.start()
+    for copy in copies:
+        copy.wait()
+
+
+def load(here, *weights):
+    vmem = pl.BlockSpec(memory_space=pltpu.VMEM)
+    hbm = pl.BlockSpec(memory_space=pl.ANY)
+    return pl.pallas_call(
+        load_kernel,
+        in_specs=[pl.BlockSpec(memory_space=pltpu.SMEM)] + [hbm] * 3,
+        out_specs=[vmem] * 3,
+        out_shape=[jax.ShapeDtypeStruct(w.shape, w.dtype) for w in weights],
+        scratch_shapes=[pltpu.SemaphoreType.DMA((3,))],
+        compiler_params=pltpu.CompilerParams(vmem_limit_bytes=LOAD_VMEM),
+        cost_estimate=pl.CostEstimate(flops=LOAD, bytes_accessed=1 << 16, transcendentals=0),
+        name="load",
+    )(here, *weights)
 
 
 def add_blocks(here_ref, pieces, wg, wu, acc_g, acc_u, fresh):
@@ -189,37 +242,42 @@
     here = jnp.stack([lax.axis_index("expert"), lax.axis_index("tensor")]).astype(jnp.int32)
     both = range(2)
 
-    own, oth, slot = dispatch(core, route_ids, tokens, cap)
-    got = lax.ppermute(oth, "expert", SWAP)
-    mine = [jnp.concatenate([v[i * part : (i + 1) * part] for v in (own, got)]) for i in both]
-    mine = together(mine)
-    near = together([[exchange(mine[i], i, bits) for bits in (1, 2, 3)] for i in both])
-    held = together([jnp.stack([mine[i], *near[i]]) for i in both])
+    bf16, f32 = jnp.bfloat16, jnp.float32
+    block, square = (4, cap, width), (rows, hidden)
+
+    bf16, f32 = jnp.bfloat16, jnp.float32
+    block, square = (4, cap, width), (rows, hidden)
+
+    ids, gates = route_ids.T, route_gates.T
+    mine, slot = dispatch(core, ids, tokens)
+    near = together([exchange(mine, 0, bits) for bits in (1, 2, 3)])
+    own, oth = together([jnp.stack([x[i * cap : (i + 1) * cap] for x in (mine, *near)]) for i in both])
+    held = [own, lax.ppermute(oth, "expert", SWAP)]
+    held, there, slot = together((held, here, slot))
+    wg, wu, wd = load(there, wg, wu, wd)
+    pick, weight = weigh(core, ids, gates, slot)
     third = exchange_pair(held, 4)
     fourth = exchange_pair(held, 8)
     last = exchange_pair(third, 8)
-
-    bf16, f32 = jnp.bfloat16, jnp.float32
-    block, square = (4, cap, width), (rows, hidden)
-    sums = local_kernel(early_kernel, "early", 1 << 33, [(square, f32)] * 2, here, *held, *third, *fourth, wg, wu)
+    third, pick, weight = together((third, pick, weight))
+    sums = local_kernel(
+        early_kernel, "early", EARLY, [(square, f32)] * 2, here, *held, *third, *fourth, wg, wu
+    )
     gated, *send = local_kernel(
-        middle_kernel, "middle", 1 << 32, [(square, bf16)] + [(block, bf16)] * 2, here, *last, *sums, wg, wu, wd
+        middle_kernel, "middle", MIDDLE, [(square, bf16)] + [(block, bf16)] * 2, here, *last, *sums, wg, wu, wd
     )
     gone = exchange_pair(send, 8)
-    out = local_kernel(late_kernel, "late", 1 << 20, [(block, bf16)] * 2 + [(block, f32)] * 4, here, gated, wd)
+    out = local_kernel(late_kernel, "late", LATE, [(block, bf16)] * 2 + [(block, f32)] * 4, here, gated, wd)
     also = exchange_pair(out[0:2], 8)
     second = exchange_pair([(out[2 + i] + gone[i].astype(f32)).astype(bf16) for i in both], 4)
     total = [out[4 + i] + also[i].astype(f32) + second[i].astype(f32) for i in both]
-    send = together([total[i].astype(bf16) for i in both])
-    near = together([[exchange(send[i][bits], i, bits) for bits in (1, 2, 3)] for i in both])
-    done = [
-        (total[i][0] + near[i][0].astype(f32) + near[i][1].astype(f32) + near[i][2].astype(f32)).astype(bf16)
-        for i in both
-    ]
-    kept = jnp.concatenate([d[:part] for d in done])
-    theirs = jnp.concatenate([d[part:] for d in done])
-    back = lax.ppermute(theirs, "expert", SWAP)
-    return combine(core, route_ids, route_gates, slot, kept, back)
+    own, oth = together(total)
+    back = lax.ppermute(oth.astype(bf16), "expert", SWAP)
+    own, back = together((own, back))
+    send = [jnp.concatenate([own[bits].astype(bf16), back[bits]]) for bits in (1, 2, 3)]
+    send = together(send)
+    near = together([exchange(x, 0, bits) for bits, x in zip((1, 2, 3), send)])
+    return combine(pick, weight, own[:1], back[:1], near)
 
 
 def solution(mesh):

time: 124 us -> 113 us (0.911)
  starting transfers between devices: 34.8 us -> 23.5 us
  Pallas kernels: 22.7 us -> 30.9 us
  local copies, waits for them, and re-layouts: 10.4 us -> 3.73 us
  other arithmetic: 3.28 us -> 1.53 us
  waiting for transfers between devices: 52.1 us -> 53.5 us
    pallas_call x1 -> x3, Pallas kernels: 2.53 us -> 11.9 us  [the longest x1 6.96 us: load(): pl.pallas_call(load_kernel, in_specs=[pl.BlockSpec(memory_space=pltpu.SME...]
    unnamed x20 -> x6, local copies, waits for them, and re-layouts: 9.23 us -> 0.92 us
    ppermute x24 -> x18, starting transfers between devices: 31.5 us -> 23.3 us  [exchange(): return lax.ppermute(value, ('expert', 'tensor'), pairs)]
    ppermute x2, waiting for transfers between devices: 0.32 us -> 4.46 us  [the longest x1 2.27 us: body(): back = lax.ppermute(oth.astype(bf16), 'expert', SWAP)]
    ppermute x2, starting transfers between devices: 3.33 us -> 0.19 us  [the longest x1 0.09 us: body(): held = [own, lax.ppermute(oth, 'expert', SWAP)]]
    ppermute x24 -> x18, waiting for transfers between devices: 51.8 us -> 49 us  [exchange(): return lax.ppermute(value, ('expert', 'tensor'), pairs)]
  transfers between devices with their start and end apart: 26 -> 20, of which waited for: 11 -> 17; matrix products, arithmetic and copies ran while one was open for 3% -> 2% of each run, Pallas kernels for 11% -> 19%
where the time goes in v3:
time: 113 us
  waiting for transfers between devices  53.5 us (47%)
  Pallas kernels  30.9 us (27%)
  starting transfers between devices  23.5 us (21%)
  local copies, waits for them, and re-layouts  3.73 us (3%)
  other arithmetic  1.53 us (1%)
    ppermute x18, waiting for transfers between devices, exchange(): return lax.ppermute(value, ('expert', 'tensor'), pairs)  49 us
    ppermute x18, starting transfers between devices, exchange(): return lax.ppermute(value, ('expert', 'tensor'), pairs)  23.3 us
    pallas_call x3, Pallas kernels, local_kernel(): pl.pallas_call(kernel, in_specs=[pl.BlockSpec(memory_space=pltpu.SMEM)] +...  16.7 us
    pallas_call x1, Pallas kernels, load(): pl.pallas_call(load_kernel, in_specs=[pl.BlockSpec(memory_space=pltpu.SME...  6.96 us
    pallas_call x1, Pallas kernels, combine(): pl.pallas_call(combine_kernel, in_specs=[vmem] * 7, out_specs=vmem, out_s...  2.94 us
    pallas_call x1, Pallas kernels, dispatch(): pl.pallas_call(dispatch_kernel, in_specs=[pl.BlockSpec(memory_space=pltpu...  2.33 us
    ppermute x1, waiting for transfers between devices, body(): back = lax.ppermute(oth.astype(bf16), 'expert', SWAP)  2.27 us
  transfers between devices with their start and end apart: 20, of which 17 were waited for; matrix products, arithmetic and copies ran while one was open for 2% of the time, Pallas kernels for 19%

profile of v3, /device:TPU:1, one launch (start us, length us, event | category | flops | bytes accessed | tf_op | source)
XLA Modules:
  0.0 113.2 jit_solution(7572774841530689227)
XLA Ops:
  0.0 2.3 %dispatch.1 = (bf16[512,384]{1,0:T(8,128)(2,1)}, s32[16,512]{1,0:T(8,128)}) custom-call(s32[1]{0:T(128)} %bitcast.core_ref, s32[2,512]{1,0:T(2,128)} %bitcast.35, bf16[512,384]{1,0:T(8,128)(2,1)} %tok_ref.1), custom_call_target="tpu_custom_call" | custom-call | tf_op jit(solution)/shard_map/dispatch/pallas_call | solution.py:71
  2.3 3.3 %collective-permute-start = (bf16[512,384]{1,0:T(8,128)(2,1)}, bf16[512,384]{1,0:T(8,128)(2,1)S(1)}, u32[]{:S(2)}, u32[]{:S(2)}) collective-permute-start(bf16[512,384]{1,0:T(8,128)(2,1)} %get-tuple-element.68), channel_id=1, source_target_pairs={{0,1},{1,0},{2,3},{3,2},{4,5},{5,4},{6,7},{7,6},{8,9},{9,8},{10,11... | collective-permute-start | bytes 1179656 | tf_op jit(solution)/shard_map/ppermute | solution.py:36
  5.6 2.7 %collective-permute-start.1 = (bf16[512,384]{1,0:T(8,128)(2,1)}, bf16[512,384]{1,0:T(8,128)(2,1)S(1)}, u32[]{:S(2)}, u32[]{:S(2)}) collective-permute-start(bf16[512,384]{1,0:T(8,128)(2,1)} %get-tuple-element.68), channel_id=1, source_target_pairs={{0,4},{1,5},{2,6},{3,7},{4,0},{5,1},{6,2},{7,3},{8,12},{9,13},{10,... | collective-permute-start | bytes 1179656 | tf_op jit(solution)/shard_map/ppermute | solution.py:36
  11.0 6.6 %collective-permute-done.1 = bf16[512,384]{1,0:T(8,128)(2,1)S(1)} collective-permute-done((bf16[512,384]{1,0:T(8,128)(2,1)}, bf16[512,384]{1,0:T(8,128)(2,1)S(1)}, u32[]{:S(2)}, u32[]{:S(2)}) %collective-permute-start.1) | collective-permute-done | bytes 393248 | tf_op jit(solution)/shard_map/ppermute | solution.py:36
  19.1 2.2 %collective-permute-done.3.hb = bf16[4,256,384]{2,1,0:T(8,128)(2,1)S(1)} collective-permute-done((bf16[4,256,384]{2,1,0:T(8,128)(2,1)S(1)}, bf16[4,256,384]{2,1,0:T(8,128)(2,1)S(1)}, u32[]{:S(2)}, u32[]{:S(2)}) %collective-permute-start.3) | collective-permute-done | bytes 786464 | tf_op jit(solution)/shard_map/ppermute | solution.py:255
  21.9 2.0 %collective-permute-start.9 = (bf16[4,256,384]{2,1,0:T(8,128)(2,1)S(1)}, bf16[4,256,384]{2,1,0:T(8,128)(2,1)}, u32[]{:S(2)}, u32[]{:S(2)}) collective-permute-start(bf16[4,256,384]{2,1,0:T(8,128)(2,1)S(1)} %collective-permute-done.3.hb), channel_id=1, source_target_pairs={{0,4},{1,5},{2,6},{3,7},{4,0},{5,1},{6,2},{7,3},{8,12},{9,13},{10,... | collective-permute-start | bytes 2359304 | tf_op jit(solution)/shard_map/ppermute | solution.py:36
  24.0 1.9 %collective-permute-start.5 = (bf16[4,256,384]{2,1,0:T(8,128)(2,1)S(1)}, bf16[4,256,384]{2,1,0:T(8,128)(2,1)}, u32[]{:S(2)}, u32[]{:S(2)}) collective-permute-start(bf16[4,256,384]{2,1,0:T(8,128)(2,1)S(1)} %collective-permute-done.3.hb), channel_id=1, source_target_pairs={{0,1},{1,0},{2,3},{3,2},{4,5},{5,4},{6,7},{7,6},{8,9},{9,8},{10,11... | collective-permute-start | bytes 2359304 | tf_op jit(solution)/shard_map/ppermute | solution.py:36
  25.9 2.0 %weigh.1 = (bf16[512,512]{1,0:T(8,128)(2,1)}, f32[512,128]{1,0:T(8,128)}) custom-call(s32[1]{0:T(128)} %bitcast.core_ref, s32[2,512]{1,0:T(2,128)} %bitcast.36, f32[2,512]{1,0:T(2,128)} %bitcast.40, s32[16,512]{1,0:T(8,128)} %get-tuple-element.81.slot_ref), custom_call_target="tpu_custom_call" | custom-call | flops 1073741824 | bytes 65536 | tf_op jit(solution)/shard_map/weigh/pallas_call | solution.py:101
  27.8 7.0 %load.1 = (bf16[6144,512]{1,0:T(8,128)(2,1)S(1)}, bf16[6144,512]{1,0:T(8,128)(2,1)S(1)}, bf16[512,6144]{1,0:T(8,128)(2,1)S(1)}) custom-call(s32[2]{0:T(128)S(1)} %pad_add_fusion.here_ref, bf16[6144,512]{1,0:T(8,128)(2,1)} %bitcast.37, bf16[6144,512]{1,0:T(8,128)(2,1)} %bitcast.38, bf16[512,6144]{1,0:T(8,128)(2,1)} %bitcast.39), custom_call_target="tpu_custom_call" | custom-call | flops 8589934592 | bytes 65536 | tf_op jit(solution)/shard_map/load/pallas_call | solution.py:150
  36.2 4.2 %collective-permute-done.9.fb = bf16[4,256,384]{2,1,0:T(8,128)(2,1)} collective-permute-done((bf16[4,256,384]{2,1,0:T(8,128)(2,1)S(1)}, bf16[4,256,384]{2,1,0:T(8,128)(2,1)}, u32[]{:S(2)}, u32[]{:S(2)}) %collective-permute-start.9) | collective-permute-done | bytes 786464 | tf_op jit(solution)/shard_map/ppermute | solution.py:36
  40.4 2.4 %collective-permute-done.5.tb = bf16[4,256,384]{2,1,0:T(8,128)(2,1)} collective-permute-done((bf16[4,256,384]{2,1,0:T(8,128)(2,1)S(1)}, bf16[4,256,384]{2,1,0:T(8,128)(2,1)}, u32[]{:S(2)}, u32[]{:S(2)}) %collective-permute-start.5) | collective-permute-done | bytes 786464 | tf_op jit(solution)/shard_map/ppermute | solution.py:36
  44.6 8.6 %early.1 = (f32[512,512]{1,0:T(8,128)S(1)}, f32[512,512]{1,0:T(8,128)S(1)}) custom-call(s32[2]{0:T(128)S(1)} %pad_add_fusion.here_ref, bf16[4,256,384]{2,1,0:T(8,128)(2,1)S(1)} %pad_maximum_fusion.ha, bf16[4,256,384]{2,1,0:T(8,128)(2,1)S(1)} %collective-permute-done.3.hb, bf16[4,256,384]{2,1,0:T(8,128)(2,1)} %collective-permute-done.4.ta, ...), custom_call_target="tpu_custom_call" | custom-call | flops 8589934592 | bytes 65536 | tf_op jit(solution)/shard_map/early/pallas_call | solution.py:224
  54.1 1.8 %collective-permute-done.7.lb = bf16[4,256,384]{2,1,0:T(8,128)(2,1)S(1)} collective-permute-done((bf16[4,256,384]{2,1,0:T(8,128)(2,1)}, bf16[4,256,384]{2,1,0:T(8,128)(2,1)S(1)}, u32[]{:S(2)}, u32[]{:S(2)}) %collective-permute-start.7) | collective-permute-done | bytes 786464 | tf_op jit(solution)/shard_map/ppermute | solution.py:36
  55.9 4.1 %middle.1 = (bf16[512,512]{1,0:T(8,128)(2,1)S(1)}, bf16[4,256,384]{2,1,0:T(8,128)(2,1)S(1)}, bf16[4,256,384]{2,1,0:T(8,128)(2,1)S(1)}) custom-call(s32[2]{0:T(128)S(1)} %pad_add_fusion.here_ref, bf16[4,256,384]{2,1,0:T(8,128)(2,1)S(1)} %collective-permute-done.6.la, bf16[4,256,384]{2,1,0:T(8,128)(2,1)S(1)} %collective-permute-done.7.lb, ...), custom_call_target="tpu_custom_call" | custom-call | flops 4294967296 | bytes 65536 | tf_op jit(solution)/shard_map/middle/pallas_call | solution.py:224
  61.6 4.0 %late.1 = (bf16[4,256,384]{2,1,0:T(8,128)(2,1)S(1)}, bf16[4,256,384]{2,1,0:T(8,128)(2,1)S(1)}, f32[4,256,384]{2,1,0:T(8,128)S(1)}, f32[4,256,384]{2,1,0:T(8,128)...) custom-call(s32[2]{0:T(128)S(1)} %pad_add_fusion.here_ref, bf16[512,512]{1,0:T(8,128)(2,1)S(1)} %get-tuple-element.100.gated, ...), custom_call_target="tpu_custom_call" | custom-call | flops 1048576 | bytes 65536 | tf_op jit(solution)/shard_map/late/pallas_call | solution.py:224
  67.8 3.5 %collective-permute-done.12 = bf16[4,256,384]{2,1,0:T(8,128)(2,1)S(1)} collective-permute-done((bf16[4,256,384]{2,1,0:T(8,128)(2,1)S(1)}, bf16[4,256,384]{2,1,0:T(8,128)(2,1)S(1)}, u32[]{:S(2)}, u32[]{:S(2)}) %collective-permute-start.12) | collective-permute-done | bytes 786464 | tf_op jit(solution)/shard_map/ppermute | solution.py:36
  75.0 4.7 %collective-permute-done.10 = bf16[4,256,384]{2,1,0:T(8,128)(2,1)S(1)} collective-permute-done((bf16[4,256,384]{2,1,0:T(8,128)(2,1)S(1)}, bf16[4,256,384]{2,1,0:T(8,128)(2,1)S(1)}, u32[]{:S(2)}, u32[]{:S(2)}) %collective-permute-start.10) | collective-permute-done | bytes 786464 | tf_op jit(solution)/shard_map/ppermute | solution.py:36
  79.7 2.2 %collective-permute-done.11 = bf16[4,256,384]{2,1,0:T(8,128)(2,1)S(1)} collective-permute-done((bf16[4,256,384]{2,1,0:T(8,128)(2,1)S(1)}, bf16[4,256,384]{2,1,0:T(8,128)(2,1)S(1)}, u32[]{:S(2)}, u32[]{:S(2)}) %collective-permute-start.11) | collective-permute-done | bytes 786464 | tf_op jit(solution)/shard_map/ppermute | solution.py:36
  81.9 9.1 %collective-permute-done.14 = bf16[4,256,384]{2,1,0:T(8,128)(2,1)S(1)} collective-permute-done((bf16[4,256,384]{2,1,0:T(8,128)(2,1)S(1)}, bf16[4,256,384]{2,1,0:T(8,128)(2,1)S(1)}, u32[]{:S(2)}, u32[]{:S(2)}) %collective-permute-start.14) | collective-permute-done | bytes 786464 | tf_op jit(solution)/shard_map/ppermute | solution.py:36
  91.7 2.3 %collective-permute-done.16 = bf16[4,256,384]{2,1,0:T(8,128)(2,1)S(1)} collective-permute-done((bf16[4,256,384]{2,1,0:T(8,128)(2,1)S(1)}, bf16[4,256,384]{2,1,0:T(8,128)(2,1)S(1)}, u32[]{:S(2)}, u32[]{:S(2)}) %collective-permute-start.16) | collective-permute-done | bytes 786464 | tf_op jit(solution)/shard_map/ppermute | solution.py:275
  95.0 2.3 %collective-permute-start.17 = (bf16[512,384]{1,0:T(8,128)(2,1)S(1)}, bf16[512,384]{1,0:T(8,128)(2,1)S(1)}, u32[]{:S(2)}, u32[]{:S(2)}) collective-permute-start(bf16[512,384]{1,0:T(8,128)(2,1)S(1)} %pad_maximum_fusion.2), channel_id=1, source_target_pairs={{0,1},{1,0},{2,3},{3,2},{4,5},{5,4},{6,7},{7,6},{8,9},{9,8},{10,11... | collective-permute-start | bytes 1179656 | tf_op jit(solution)/shard_map/ppermute | solution.py:36
  100.9 2.1 %collective-permute-done.17.na_ref = bf16[512,384]{1,0:T(8,128)(2,1)S(1)} collective-permute-done((bf16[512,384]{1,0:T(8,128)(2,1)S(1)}, bf16[512,384]{1,0:T(8,128)(2,1)S(1)}, u32[]{:S(2)}, u32[]{:S(2)}) %collective-permute-start.17) | collective-permute-done | bytes 393248 | tf_op jit(solution)/shard_map/ppermute | solution.py:36
  103.1 6.3 %collective-permute-done.18.nb_ref = bf16[512,384]{1,0:T(8,128)(2,1)S(1)} collective-permute-done((bf16[512,384]{1,0:T(8,128)(2,1)S(1)}, bf16[512,384]{1,0:T(8,128)(2,1)S(1)}, u32[]{:S(2)}, u32[]{:S(2)}) %collective-permute-start.18) | collective-permute-done | bytes 393248 | tf_op jit(solution)/shard_map/ppermute | solution.py:36
  110.3 2.9 %combine.1 = bf16[512,384]{1,0:T(8,128)(2,1)} custom-call(bf16[512,512]{1,0:T(8,128)(2,1)} %get-tuple-element.84.pick_ref, f32[512,128]{1,0:T(8,128)} %get-tuple-element.85.weight_ref, f32[1,256,384]{2,1,0:T(8,128)} %slice.59.own_ref, bf16[1,256,384]{2,1,0:T(8,128)(2,1)} %get-tuple-element.137.back_ref, bf16[512,384]{1,0:T(8,128)(2,1)} %copy-done, ...), custom_call_target="tpu_custom_call" | custom-call | tf_op jit(solution)/shard_map/combine/pallas_call | solution.py:129
  (46 shorter events, 22.6 us)
Async XLA Ops:
  2.3 8.7 %collective-permute-start = (bf16[512,384]{1,0:T(8,128)(2,1)}, bf16[512,384]{1,0:T(8,128)(2,1)S(1)}, u32[]{:S(2)}, u32[]{:S(2)}) collective-permute-start(bf16[512,384]{1,0:T(8,128)(2,1)} %get-tuple-element.68), channel_id=1, source_target_pairs={{0,1},{1,0},{2,3},{3,2},{4,5},{5,4},{6,7},{7,6},{8,9},{9,8},{10,11... | collective-permute-start | bytes 1179656 | tf_op jit(solution)/shard_map/ppermute | solution.py:36
  5.6 12.0 %collective-permute-start.1 = (bf16[512,384]{1,0:T(8,128)(2,1)}, bf16[512,384]{1,0:T(8,128)(2,1)S(1)}, u32[]{:S(2)}, u32[]{:S(2)}) collective-permute-start(bf16[512,384]{1,0:T(8,128)(2,1)} %get-tuple-element.68), channel_id=1, source_target_pairs={{0,4},{1,5},{2,6},{3,7},{4,0},{5,1},{6,2},{7,3},{8,12},{9,13},{10,... | collective-permute-start | bytes 1179656 | tf_op jit(solution)/shard_map/ppermute | solution.py:36
  8.4 10.2 %collective-permute-start.2 = (bf16[512,384]{1,0:T(8,128)(2,1)}, bf16[512,384]{1,0:T(8,128)(2,1)S(1)}, u32[]{:S(2)}, u32[]{:S(2)}) collective-permute-start(bf16[512,384]{1,0:T(8,128)(2,1)} %get-tuple-element.68), channel_id=1, source_target_pairs={{0,5},{1,4},{2,7},{3,6},{4,1},{5,0},{6,3},{7,2},{8,13},{9,12},{10,... | collective-permute-start | bytes 1179656 | tf_op jit(solution)/shard_map/ppermute | solution.py:36
  18.9 2.4 %collective-permute-start.3 = (bf16[4,256,384]{2,1,0:T(8,128)(2,1)S(1)}, bf16[4,256,384]{2,1,0:T(8,128)(2,1)S(1)}, u32[]{:S(2)}, u32[]{:S(2)}) collective-permute-start(bf16[4,256,384]{2,1,0:T(8,128)(2,1)S(1)} %pad_maximum_fusion.1), channel_id=1, source_target_pairs={{0,16},{16,0},{1,17},{17,1},{2,18},{18,2},{3,19},{19,3},{4,20},{20... | collective-permute-start | bytes 2359304 | tf_op jit(solution)/shard_map/ppermute | solution.py:255
  21.3 14.9 %collective-permute-start.8 = (bf16[4,256,384]{2,1,0:T(8,128)(2,1)S(1)}, bf16[4,256,384]{2,1,0:T(8,128)(2,1)}, u32[]{:S(2)}, u32[]{:S(2)}) collective-permute-start(bf16[4,256,384]{2,1,0:T(8,128)(2,1)S(1)} %pad_maximum_fusion.ha), channel_id=1, source_target_pairs={{0,12},{1,13},{2,14},{3,15},{4,8},{5,9},{6,10},{7,11},{8,4},{9,5},... | collective-permute-start | bytes 2359304 | tf_op jit(solution)/shard_map/ppermute | solution.py:36
  21.9 18.5 %collective-permute-start.4 = (bf16[4,256,384]{2,1,0:T(8,128)(2,1)S(1)}, bf16[4,256,384]{2,1,0:T(8,128)(2,1)}, u32[]{:S(2)}, u32[]{:S(2)}) collective-permute-start(bf16[4,256,384]{2,1,0:T(8,128)(2,1)S(1)} %pad_maximum_fusion.ha), channel_id=1, source_target_pairs={{0,3},{1,2},{2,1},{3,0},{4,7},{5,6},{6,5},{7,4},{8,11},{9,10},{10,... | collective-permute-start | bytes 2359304 | tf_op jit(solution)/shard_map/ppermute | solution.py:36
  21.9 18.4 %collective-permute-start.9 = (bf16[4,256,384]{2,1,0:T(8,128)(2,1)S(1)}, bf16[4,256,384]{2,1,0:T(8,128)(2,1)}, u32[]{:S(2)}, u32[]{:S(2)}) collective-permute-start(bf16[4,256,384]{2,1,0:T(8,128)(2,1)S(1)} %collective-permute-done.3.hb), channel_id=1, source_target_pairs={{0,4},{1,5},{2,6},{3,7},{4,0},{5,1},{6,2},{7,3},{8,12},{9,13},{10,... | collective-permute-start | bytes 2359304 | tf_op jit(solution)/shard_map/ppermute | solution.py:36
  24.0 18.8 %collective-permute-start.5 = (bf16[4,256,384]{2,1,0:T(8,128)(2,1)S(1)}, bf16[4,256,384]{2,1,0:T(8,128)(2,1)}, u32[]{:S(2)}, u32[]{:S(2)}) collective-permute-start(bf16[4,256,384]{2,1,0:T(8,128)(2,1)S(1)} %collective-permute-done.3.hb), channel_id=1, source_target_pairs={{0,1},{1,0},{2,3},{3,2},{4,5},{5,4},{6,7},{7,6},{8,9},{9,8},{10,11... | collective-permute-start | bytes 2359304 | tf_op jit(solution)/shard_map/ppermute | solution.py:36
  42.8 11.3 %collective-permute-start.6 = (bf16[4,256,384]{2,1,0:T(8,128)(2,1)}, bf16[4,256,384]{2,1,0:T(8,128)(2,1)S(1)}, u32[]{:S(2)}, u32[]{:S(2)}) collective-permute-start(bf16[4,256,384]{2,1,0:T(8,128)(2,1)} %collective-permute-done.4.ta), channel_id=1, source_target_pairs={{0,12},{1,13},{2,14},{3,15},{4,8},{5,9},{6,10},{7,11},{8,4},{9,5},... | collective-permute-start | bytes 2359304 | tf_op jit(solution)/shard_map/ppermute | solution.py:36
  43.3 12.6 %collective-permute-start.7 = (bf16[4,256,384]{2,1,0:T(8,128)(2,1)}, bf16[4,256,384]{2,1,0:T(8,128)(2,1)S(1)}, u32[]{:S(2)}, u32[]{:S(2)}) collective-permute-start(bf16[4,256,384]{2,1,0:T(8,128)(2,1)} %collective-permute-done.5.tb), channel_id=1, source_target_pairs={{0,4},{1,5},{2,6},{3,7},{4,0},{5,1},{6,2},{7,3},{8,12},{9,13},{10,... | collective-permute-start | bytes 2359304 | tf_op jit(solution)/shard_map/ppermute | solution.py:36
  60.0 11.2 %collective-permute-start.12 = (bf16[4,256,384]{2,1,0:T(8,128)(2,1)S(1)}, bf16[4,256,384]{2,1,0:T(8,128)(2,1)S(1)}, u32[]{:S(2)}, u32[]{:S(2)}) collective-permute-start(bf16[4,256,384]{2,1,0:T(8,128)(2,1)S(1)} %get-tuple-element.110), channel_id=1, source_target_pairs={{0,12},{1,13},{2,14},{3,15},{4,8},{5,9},{6,10},{7,11},{8,4},{9,5},... | collective-permute-start | bytes 2359304 | tf_op jit(solution)/shard_map/ppermute | solution.py:36
  60.1 12.4 %collective-permute-start.13 = (bf16[4,256,384]{2,1,0:T(8,128)(2,1)S(1)}, bf16[4,256,384]{2,1,0:T(8,128)(2,1)S(1)}, u32[]{:S(2)}, u32[]{:S(2)}) collective-permute-start(bf16[4,256,384]{2,1,0:T(8,128)(2,1)S(1)} %get-tuple-element.111), channel_id=1, source_target_pairs={{0,4},{1,5},{2,6},{3,7},{4,0},{5,1},{6,2},{7,3},{8,12},{9,13},{10,... | collective-permute-start | bytes 2359304 | tf_op jit(solution)/shard_map/ppermute | solution.py:36
  65.6 14.0 %collective-permute-start.10 = (bf16[4,256,384]{2,1,0:T(8,128)(2,1)S(1)}, bf16[4,256,384]{2,1,0:T(8,128)(2,1)S(1)}, u32[]{:S(2)}, u32[]{:S(2)}) collective-permute-start(bf16[4,256,384]{2,1,0:T(8,128)(2,1)S(1)} %get-tuple-element.104), channel_id=1, source_target_pairs={{0,12},{1,13},{2,14},{3,15},{4,8},{5,9},{6,10},{7,11},{8,4},{9,5},... | collective-permute-start | bytes 2359304 | tf_op jit(solution)/shard_map/ppermute | solution.py:36
  66.4 15.5 %collective-permute-start.11 = (bf16[4,256,384]{2,1,0:T(8,128)(2,1)S(1)}, bf16[4,256,384]{2,1,0:T(8,128)(2,1)S(1)}, u32[]{:S(2)}, u32[]{:S(2)}) collective-permute-start(bf16[4,256,384]{2,1,0:T(8,128)(2,1)S(1)} %get-tuple-element.105), channel_id=1, source_target_pairs={{0,4},{1,5},{2,6},{3,7},{4,0},{5,1},{6,2},{7,3},{8,12},{9,13},{10,... | collective-permute-start | bytes 2359304 | tf_op jit(solution)/shard_map/ppermute | solution.py:36
  73.0 18.0 %collective-permute-start.14 = (bf16[4,256,384]{2,1,0:T(8,128)(2,1)S(1)}, bf16[4,256,384]{2,1,0:T(8,128)(2,1)S(1)}, u32[]{:S(2)}, u32[]{:S(2)}) collective-permute-start(bf16[4,256,384]{2,1,0:T(8,128)(2,1)S(1)} %add_convert_fusion.1), channel_id=1, source_target_pairs={{0,3},{1,2},{2,1},{3,0},{4,7},{5,6},{6,5},{7,4},{8,11},{9,10},{10,... | collective-permute-start | bytes 2359304 | tf_op jit(solution)/shard_map/ppermute | solution.py:36
  73.8 17.2 %collective-permute-start.15 = (bf16[4,256,384]{2,1,0:T(8,128)(2,1)S(1)}, bf16[4,256,384]{2,1,0:T(8,128)(2,1)S(1)}, u32[]{:S(2)}, u32[]{:S(2)}) collective-permute-start(bf16[4,256,384]{2,1,0:T(8,128)(2,1)S(1)} %add_convert_fusion), channel_id=1, source_target_pairs={{0,1},{1,0},{2,3},{3,2},{4,5},{5,4},{6,7},{7,6},{8,9},{9,8},{10,11... | collective-permute-start | bytes 2359304 | tf_op jit(solution)/shard_map/ppermute | solution.py:36
  91.6 2.4 %collective-permute-start.16 = (bf16[4,256,384]{2,1,0:T(8,128)(2,1)S(1)}, bf16[4,256,384]{2,1,0:T(8,128)(2,1)S(1)}, u32[]{:S(2)}, u32[]{:S(2)}) collective-permute-start(bf16[4,256,384]{2,1,0:T(8,128)(2,1)S(1)} %convert_add_fusion), channel_id=1, source_target_pairs={{0,16},{16,0},{1,17},{17,1},{2,18},{18,2},{3,19},{19,3},{4,20},{20... | collective-permute-start | bytes 2359304 | tf_op jit(solution)/shard_map/ppermute | solution.py:275
  95.0 8.1 %collective-permute-start.17 = (bf16[512,384]{1,0:T(8,128)(2,1)S(1)}, bf16[512,384]{1,0:T(8,128)(2,1)S(1)}, u32[]{:S(2)}, u32[]{:S(2)}) collective-permute-start(bf16[512,384]{1,0:T(8,128)(2,1)S(1)} %pad_maximum_fusion.2), channel_id=1, source_target_pairs={{0,1},{1,0},{2,3},{3,2},{4,5},{5,4},{6,7},{7,6},{8,9},{9,8},{10,11... | collective-permute-start | bytes 1179656 | tf_op jit(solution)/shard_map/ppermute | solution.py:36
  97.3 12.1 %collective-permute-start.18 = (bf16[512,384]{1,0:T(8,128)(2,1)S(1)}, bf16[512,384]{1,0:T(8,128)(2,1)S(1)}, u32[]{:S(2)}, u32[]{:S(2)}) collective-permute-start(bf16[512,384]{1,0:T(8,128)(2,1)S(1)} %pad_maximum_fusion.3), channel_id=1, source_target_pairs={{0,4},{1,5},{2,6},{3,7},{4,0},{5,1},{6,2},{7,3},{8,12},{9,13},{10,... | collective-permute-start | bytes 1179656 | tf_op jit(solution)/shard_map/ppermute | solution.py:36
  99.0 10.3 %collective-permute-start.19 = (bf16[512,384]{1,0:T(8,128)(2,1)S(1)}, bf16[512,384]{1,0:T(8,128)(2,1)S(1)}, u32[]{:S(2)}, u32[]{:S(2)}) collective-permute-start(bf16[512,384]{1,0:T(8,128)(2,1)S(1)} %pad_maximum_fusion.4), channel_id=1, source_target_pairs={{0,5},{1,4},{2,7},{3,6},{4,1},{5,0},{6,3},{7,2},{8,13},{9,12},{10,... | collective-permute-start | bytes 1179656 | tf_op jit(solution)/shard_map/ppermute | solution.py:36
  103.1 6.3 %copy-start = (bf16[512,384]{1,0:T(8,128)(2,1)}, bf16[512,384]{1,0:T(8,128)(2,1)S(1)}, u32[]{:S(2)}) copy-start(bf16[512,384]{1,0:T(8,128)(2,1)S(1)} %collective-permute-done.17.na_ref) | copy-start | bytes 1179652
  109.3 0.8 copy-start.1
  109.4 0.9 copy-start.2

commit v4 on v3

--- a/solution.py
+++ b/solution.py
@@ -1,3 +1,5 @@
+import functools
+
 import jax
 import jax.numpy as jnp
 from jax import lax
@@ -7,9 +9,9 @@
 
 TENSOR = 16
 MASKS = (1, 3, 4, 12)
-VMEM_LIMIT = 16 << 20
+VMEM_LIMIT = 8 << 20
 LOAD_VMEM = 32 << 20
-LOAD, EARLY, MIDDLE, LATE = 1 << 33, 1 << 33, 1 << 32, 1 << 20
+LOAD, EARLY, MIDDLE, LATE = 1 << 33, (1 << 32, 1 << 20), 1 << 20, 1 << 31
 
 
 CHAINS = (((0, 2, 1, 3), (1, 3, 0, 2)), ((1, 3, 2, 0), (0, 2, 3, 1)))
@@ -37,11 +39,6 @@
 
 
 together = lax.optimization_barrier
-
-
-def exchange_pair(values, bits):
-    values = together(list(values))
-    return together([exchange(values[i], i, bits) for i in range(2)])
 
 
 def dispatch_kernel(core_ref, ids_ref, tok_ref, out_ref, slot_ref):
@@ -76,6 +73,7 @@
             jax.ShapeDtypeStruct((rows, width), jnp.bfloat16),
             jax.ShapeDtypeStruct((16, rows), jnp.int32),
         ],
+        compiler_params=pltpu.CompilerParams(vmem_limit_bytes=VMEM_LIMIT),
         name="dispatch",
     )(core, ids, tokens)
 
@@ -107,6 +105,7 @@
             jax.ShapeDtypeStruct((rows, 128), jnp.float32),
         ],
         cost_estimate=pl.CostEstimate(flops=1 << 30, bytes_accessed=1 << 16, transcendentals=0),
+        compiler_params=pltpu.CompilerParams(vmem_limit_bytes=VMEM_LIMIT),
         name="weigh",
     )(core, ids, gates, slot)
 
@@ -131,6 +130,7 @@
         in_specs=[vmem] * 7,
         out_specs=vmem,
         out_shape=jax.ShapeDtypeStruct((pick.shape[0], own.shape[2]), jnp.bfloat16),
+        compiler_params=pltpu.CompilerParams(vmem_limit_bytes=VMEM_LIMIT),
         name="combine",
     )(pick, weight, own, back, *near)
 
@@ -159,70 +159,54 @@
     )(here, *weights)
 
 
-def add_blocks(here_ref, pieces, wg, wu, acc_g, acc_u, fresh):
+def add_blocks(chain, here_ref, pieces, wg, wu, acc_g=None, acc_u=None):
     core, me = here_ref[0], here_ref[1]
-    rows, width = pieces[0][2].shape[1:]
-    hidden = wg.shape[1]
-    tile = hidden // 2
-    for chain in range(2):
-        at = slice(chain * rows, (chain + 1) * rows)
+    rows, width = pieces[0][1].shape[1:]
+    tile = wg.shape[1] // 2
+    for n in range(2):
+        cols = slice(n * tile, (n + 1) * tile)
+        sums = []
         for acc, w in ((acc_g, wg), (acc_u, wu)):
-            for n in range(2):
-                cols = slice(n * tile, (n + 1) * tile)
-                total = jnp.zeros((rows, tile), jnp.float32) if fresh else acc[at, cols]
-                for owner, first, ref in pieces:
-                    if owner != chain:
-                        continue
-                    for k in range(ref.shape[0]):
-                        start = pl.multiple_of(block_of(core, me, chain, first + k) * width, width)
-                        total += jnp.dot(
-                            ref[k], w[pl.ds(start, width), cols], preferred_element_type=jnp.float32
-                        )
-                yield acc, at, cols, total
-
-
-def early_kernel(here_ref, ha, hb, ta, tb, fa, fb, wg, wu, acc_g, acc_u):
-    pieces = [(0, 0, ha), (1, 0, hb), (0, 4, ta), (1, 4, tb), (0, 8, fa), (1, 8, fb)]
-    for acc, at, cols, total in add_blocks(here_ref, pieces, wg, wu, acc_g, acc_u, True):
-        acc[at, cols] = total
-
-
-def down_blocks(here_ref, gated, wd, first, outs):
+            total = jnp.zeros((rows, tile), jnp.float32) if acc is None else acc[:, cols]
+            for first, ref in pieces:
+                for k in range(ref.shape[0]):
+                    start = pl.multiple_of(block_of(core, me, chain, first + k) * width, width)
+                    total += jnp.dot(ref[k], w[pl.ds(start, width), cols], preferred_element_type=jnp.float32)
+            sums.append(total)
+        yield cols, *sums
+
+
+def early_kernel(chain, here_ref, held, third, fourth, wg, wu, acc_g, acc_u):
+    for cols, g, u in add_blocks(chain, here_ref, [(0, held), (4, third), (8, fourth)], wg, wu):
+        acc_g[:, cols] = g
+        acc_u[:, cols] = u
+
+
+def down_blocks(chain, here_ref, gated, wd, first, out):
     core, me = here_ref[0], here_ref[1]
-    count, rows, width = outs[0].shape
-    for chain in range(2):
-        for k in range(count):
-            start = pl.multiple_of(block_of(core, me, chain, first + k) * width, width)
-            y = jnp.dot(
-                gated[chain * rows : (chain + 1) * rows, :],
-                wd[:, pl.ds(start, width)],
-                preferred_element_type=jnp.float32,
-            )
-            outs[chain][k] = y.astype(outs[chain].dtype)
-
-
-def middle_kernel(here_ref, la, lb, acc_g, acc_u, wg, wu, wd, gated, sa, sb):
-    pieces = [(0, 12, la), (1, 12, lb)]
-    sums = {}
-    for acc, at, cols, total in add_blocks(here_ref, pieces, wg, wu, acc_g, acc_u, False):
-        if acc is acc_g:
-            sums[at.start, cols.start] = total
-        else:
-            v = sums.pop((at.start, cols.start))
-            gated[at, cols] = (v / (1.0 + jnp.exp(-v)) * total).astype(jnp.bfloat16)
-    down_blocks(here_ref, gated, wd, 12, (sa, sb))
-
-
-def late_kernel(here_ref, gated, wd, sa, sb, ka, kb, ra, rb):
-    down_blocks(here_ref, gated, wd, 8, (sa, sb))
-    down_blocks(here_ref, gated, wd, 4, (ka, kb))
-    down_blocks(here_ref, gated, wd, 0, (ra, rb))
-
-
-def local_kernel(kernel, name, cost, outs, here, *operands):
-    vmem = pl.BlockSpec(memory_space=pltpu.VMEM)
-    return pl.pallas_call(
-        kernel,
+    count, rows, width = out.shape
+    for k in range(count):
+        start = pl.multiple_of(block_of(core, me, chain, first + k) * width, width)
+        y = jnp.dot(gated[...], wd[:, pl.ds(start, width)], preferred_element_type=jnp.float32)
+        out[k] = y.astype(out.dtype)
+
+
+def middle_kernel(chain, here_ref, last, acc_g, acc_u, wg, wu, wd, gated, send):
+    for cols, g, u in add_blocks(chain, here_ref, [(12, last)], wg, wu, acc_g, acc_u):
+        gated[:, cols] = (g / (1.0 + jnp.exp(-g)) * u).astype(jnp.bfloat16)
+    down_blocks(chain, here_ref, gated, wd, 12, send)
+
+
+def late_kernel(chain, here_ref, gated, wd, send, keep, rest):
+    down_blocks(chain, here_ref, gated, wd, 8, send)
+    down_blocks(chain, here_ref, gated, wd, 4, keep)
+    down_blocks(chain, here_ref, gated, wd, 0, rest)
+
+
+def local_kernel(kernel, name, cost, chain, outs, here, *operands):
+    vmem = pl.BlockSpec(memory_space=pltpu.VMEM)
+    return pl.pallas_call(
+        functools.partial(kernel, chain),
         in_specs=[pl.BlockSpec(memory_space=pltpu.SMEM)] + [vmem] * len(operands),
         out_specs=[vmem] * len(outs),
         out_shape=[jax.ShapeDtypeStruct(shape, dtype) for shape, dtype in outs],
@@ -243,34 +227,48 @@
     both = range(2)
 
     bf16, f32 = jnp.bfloat16, jnp.float32
-    block, square = (4, cap, width), (rows, hidden)
-
-    bf16, f32 = jnp.bfloat16, jnp.float32
-    block, square = (4, cap, width), (rows, hidden)
+    block, square = (4, cap, width), (cap, hidden)
 
     ids, gates = route_ids.T, route_gates.T
     mine, slot = dispatch(core, ids, tokens)
     near = together([exchange(mine, 0, bits) for bits in (1, 2, 3)])
-    own, oth = together([jnp.stack([x[i * cap : (i + 1) * cap] for x in (mine, *near)]) for i in both])
+    own, oth = [jnp.stack([x[i * cap : (i + 1) * cap] for x in (mine, *near)]) for i in both]
+    own, oth = together((own, oth))
     held = [own, lax.ppermute(oth, "expert", SWAP)]
-    held, there, slot = together((held, here, slot))
+    third = [exchange(held[i], i, 4) for i in both]
+    held[1], own = together((held[1], own))
+    fourth = [exchange(x, i, 8) for i, x in enumerate((own, held[1]))]
+    own, there, slot = together((own, here, slot))
     wg, wu, wd = load(there, wg, wu, wd)
+    third[0], wd = together((third[0], wd))
+    last = [exchange(x, i, 8) for i, x in enumerate(third)]
     pick, weight = weigh(core, ids, gates, slot)
-    third = exchange_pair(held, 4)
-    fourth = exchange_pair(held, 8)
-    last = exchange_pair(third, 8)
+
     third, pick, weight = together((third, pick, weight))
-    sums = local_kernel(
-        early_kernel, "early", EARLY, [(square, f32)] * 2, here, *held, *third, *fourth, wg, wu
-    )
-    gated, *send = local_kernel(
-        middle_kernel, "middle", MIDDLE, [(square, bf16)] + [(block, bf16)] * 2, here, *last, *sums, wg, wu, wd
-    )
-    gone = exchange_pair(send, 8)
-    out = local_kernel(late_kernel, "late", LATE, [(block, bf16)] * 2 + [(block, f32)] * 4, here, gated, wd)
-    also = exchange_pair(out[0:2], 8)
-    second = exchange_pair([(out[2 + i] + gone[i].astype(f32)).astype(bf16) for i in both], 4)
-    total = [out[4 + i] + also[i].astype(f32) + second[i].astype(f32) for i in both]
+    early, token = [], ()
+    for i in both:
+        pieces, token = together(((held[i], third[i], fourth[i]), token))
+        token = local_kernel(early_kernel, "early", EARLY[i], i, [(square, f32)] * 2, here, *pieces, wg, wu)
+        early.append(token)
+    middle, later = [], []
+    for i in both:
+        arrived, sums, token = together((last[i], early[i], token))
+        token = local_kernel(
+            middle_kernel, "middle", MIDDLE, i, [(square, bf16), (block, bf16)], here, arrived, *sums, wg, wu, wd
+        )
+        middle.append(token)
+    for i in both:
+        gated, token = together((middle[i][0], token))
+        token = local_kernel(late_kernel, "late", LATE, i, [(block, bf16)] + [(block, f32)] * 2, here, gated, wd)
+        later.append(token)
+
+    total = []
+    for i in both:
+        send, keep, rest = later[i]
+        gone = exchange(middle[i][1], i, 8)
+        also = exchange(send, i, 8)
+        second = exchange((keep + gone.astype(f32)).astype(bf16), i, 4)
+        total.append(rest + also.astype(f32) + second.astype(f32))
     own, oth = together(total)
     back = lax.ppermute(oth.astype(bf16), "expert", SWAP)
     own, back = together((own, back))

time: 113 us -> 108 us (0.956)
  Pallas kernels: 30.9 us -> 26.6 us
  starting transfers between devices: 23.5 us -> 27.5 us
  waiting for transfers between devices: 53.5 us -> 49.6 us
  local copies, waits for them, and re-layouts: 3.73 us -> 2.02 us
    ppermute x18, waiting for transfers between devices: 49 us -> 45.9 us  [exchange(): return lax.ppermute(value, ('expert', 'tensor'), pairs)]
    ppermute x18, starting transfers between devices: 23.3 us -> 25.6 us  [exchange(): return lax.ppermute(value, ('expert', 'tensor'), pairs)]
    pallas_call x1, Pallas kernels: 2.33 us -> 0.57 us  [dispatch(): pl.pallas_call(dispatch_kernel, in_specs=[pl.BlockSpec(memory_space=pltpu...]
    pallas_call x1, Pallas kernels: 2.94 us -> 1.25 us  [combine(): pl.pallas_call(combine_kernel, in_specs=[vmem] * 7, out_specs=vmem, out_s...]
    ppermute x1, starting transfers between devices: 0.09 us -> 1.77 us  [body(): back = lax.ppermute(oth.astype(bf16), 'expert', SWAP)]
    pallas_call x1, Pallas kernels: 1.95 us -> 0.36 us  [weigh(): pl.pallas_call(weigh_kernel, in_specs=[pl.BlockSpec(memory_space=pltpu.SM...]
    pallas_call x3 -> x6, Pallas kernels: 16.7 us -> 17.4 us  [local_kernel(): pl.pallas_call(functools.partial(kernel, chain), in_specs=[pl.BlockSpec(m...]
  transfers between devices with their start and end apart: 20 -> 20, of which waited for: 17 -> 13; matrix products, arithmetic and copies ran while one was open for 2% -> 1% of each run, Pallas kernels for 19% -> 23%
where the time goes in v4:
time: 108 us; the launch traced here: 107 us
  waiting for transfers between devices  49.6 us (46%)
  starting transfers between devices  27.5 us (25%)
  Pallas kernels  26.6 us (25%)
  local copies, waits for them, and re-layouts  2.02 us (2%)
  other arithmetic  1.41 us (1%)
    ppermute x18, waiting for transfers between devices, exchange(): return lax.ppermute(value, ('expert', 'tensor'), pairs)  45.9 us
    ppermute x18, starting transfers between devices, exchange(): return lax.ppermute(value, ('expert', 'tensor'), pairs)  25.6 us
    pallas_call x6, Pallas kernels, local_kernel(): pl.pallas_call(functools.partial(kernel, chain), in_specs=[pl.BlockSpec(m...  17.4 us
    pallas_call x1, Pallas kernels, load(): pl.pallas_call(load_kernel, in_specs=[pl.BlockSpec(memory_space=pltpu.SME...  6.96 us
  transfers between devices with their start and end apart: 20, of which 13 were waited for; matrix products, arithmetic and copies ran while one was open for 1% of the time, Pallas kernels for 23%

profile of v4, /device:TPU:1, one launch (start us, length us, event | category | flops | bytes accessed | tf_op | source)
XLA Modules:
  0.0 107.4 jit_solution(17795779545203521353)
XLA Ops:
  2.3 3.4 %collective-permute-start = (bf16[512,384]{1,0:T(8,128)(2,1)S(1)}, bf16[512,384]{1,0:T(8,128)(2,1)S(1)}, u32[]{:S(2)}, u32[]{:S(2)}) collective-permute-start(bf16[512,384]{1,0:T(8,128)(2,1)S(1)} %get-tuple-element.65), channel_id=1, source_target_pairs={{0,1},{1,0},{2,3},{3,2},{4,5},{5,4},{6,7},{7,6},{8,9},{9,8},{10,11... | collective-permute-start | bytes 1179656 | tf_op jit(solution)/shard_map/ppermute | solution.py:38
  5.7 2.7 %collective-permute-start.1 = (bf16[512,384]{1,0:T(8,128)(2,1)S(1)}, bf16[512,384]{1,0:T(8,128)(2,1)S(1)}, u32[]{:S(2)}, u32[]{:S(2)}) collective-permute-start(bf16[512,384]{1,0:T(8,128)(2,1)S(1)} %get-tuple-element.65), channel_id=1, source_target_pairs={{0,4},{1,5},{2,6},{3,7},{4,0},{5,1},{6,2},{7,3},{8,12},{9,13},{10,... | collective-permute-start | bytes 1179656 | tf_op jit(solution)/shard_map/ppermute | solution.py:38
  8.4 2.4 %collective-permute-done = bf16[512,384]{1,0:T(8,128)(2,1)S(1)} collective-permute-done((bf16[512,384]{1,0:T(8,128)(2,1)S(1)}, bf16[512,384]{1,0:T(8,128)(2,1)S(1)}, u32[]{:S(2)}, u32[]{:S(2)}) %collective-permute-start) | collective-permute-done | bytes 393248 | tf_op jit(solution)/shard_map/ppermute | solution.py:38
  10.8 6.5 %collective-permute-done.1 = bf16[512,384]{1,0:T(8,128)(2,1)S(1)} collective-permute-done((bf16[512,384]{1,0:T(8,128)(2,1)S(1)}, bf16[512,384]{1,0:T(8,128)(2,1)S(1)}, u32[]{:S(2)}, u32[]{:S(2)}) %collective-permute-start.1) | collective-permute-done | bytes 393248 | tf_op jit(solution)/shard_map/ppermute | solution.py:38
  22.9 2.3 %collective-permute-start.5 = (bf16[4,256,384]{2,1,0:T(8,128)(2,1)S(1)}, bf16[4,256,384]{2,1,0:T(8,128)(2,1)S(1)}, u32[]{:S(2)}, u32[]{:S(2)}) collective-permute-start(bf16[4,256,384]{2,1,0:T(8,128)(2,1)S(1)} %collective-permute-done.4.held), channel_id=1, source_target_pairs={{0,1},{1,0},{2,3},{3,2},{4,5},{5,4},{6,7},{7,6},{8,9},{9,8},{10,11... | collective-permute-start | bytes 2359304 | tf_op jit(solution)/shard_map/ppermute | solution.py:38
  25.2 7.0 %load.1 = (bf16[6144,512]{1,0:T(8,128)(2,1)S(1)}, bf16[6144,512]{1,0:T(8,128)(2,1)S(1)}, bf16[512,6144]{1,0:T(8,128)(2,1)S(1)}) custom-call(s32[2]{0:T(128)S(1)} %pad_add_fusion.here_ref, bf16[6144,512]{1,0:T(8,128)(2,1)} %bitcast.38, bf16[6144,512]{1,0:T(8,128)(2,1)} %bitcast.39, bf16[512,6144]{1,0:T(8,128)(2,1)} %bitcast.40), custom_call_target="tpu_custom_call" | custom-call | flops 8589934592 | bytes 65536 | tf_op jit(solution)/shard_map/load/pallas_call | solution.py:150
  33.3 2.0 %collective-permute-start.6 = (bf16[4,256,384]{2,1,0:T(8,128)(2,1)S(1)}, bf16[4,256,384]{2,1,0:T(8,128)(2,1)S(1)}, u32[]{:S(2)}, u32[]{:S(2)}) collective-permute-start(bf16[4,256,384]{2,1,0:T(8,128)(2,1)S(1)} %collective-permute-done.3.third), channel_id=1, source_target_pairs={{0,12},{1,13},{2,14},{3,15},{4,8},{5,9},{6,10},{7,11},{8,4},{9,5},... | collective-permute-start | bytes 2359304 | tf_op jit(solution)/shard_map/ppermute | solution.py:38
  35.6 6.8 %collective-permute-done.5.third = bf16[4,256,384]{2,1,0:T(8,128)(2,1)S(1)} collective-permute-done((bf16[4,256,384]{2,1,0:T(8,128)(2,1)S(1)}, bf16[4,256,384]{2,1,0:T(8,128)(2,1)S(1)}, u32[]{:S(2)}, u32[]{:S(2)}) %collective-permute-start.5) | collective-permute-done | bytes 786464 | tf_op jit(solution)/shard_map/ppermute | solution.py:38
  44.0 4.0 %early.2 = (f32[256,512]{1,0:T(8,128)S(1)}, f32[256,512]{1,0:T(8,128)S(1)}) custom-call(s32[2]{0:T(128)S(1)} %pad_add_fusion.here_ref, bf16[4,256,384]{2,1,0:T(8,128)(2,1)S(1)} %pad_maximum_fusion.held, bf16[4,256,384]{2,1,0:T(8,128)(2,1)S(1)} %collective-permute-done.3.third, bf16[4,256,384]{2,1,0:T(8,128)(2,1)S(1)} %collective-permute-done.7.fourth, ...), custom_call_target="tpu_custom_call" | custom-call | flops 4294967296 | bytes 65536 | tf_op jit(solution)/shard_map/early/pallas_call | solution.py:208
  48.0 4.0 %early.3 = (f32[256,512]{1,0:T(8,128)S(1)}, f32[256,512]{1,0:T(8,128)S(1)}) custom-call(s32[2]{0:T(128)S(1)} %pad_add_fusion.here_ref, bf16[4,256,384]{2,1,0:T(8,128)(2,1)S(1)} %collective-permute-done.4.held, bf16[4,256,384]{2,1,0:T(8,128)(2,1)S(1)} %collective-permute-done.5.third, bf16[4,256,384]{2,1,0:T(8,128)(2,1)S(1)} %collective-permute-done.8.fourth, ...), custom_call_target="tpu_custom_call" | custom-call | flops 1048576 | bytes 65536 | tf_op jit(solution)/shard_map/early/pallas_call | solution.py:208
  52.0 2.4 %middle.2 = (bf16[256,512]{1,0:T(8,128)(2,1)S(1)}, bf16[4,256,384]{2,1,0:T(8,128)(2,1)S(1)}) custom-call(s32[2]{0:T(128)S(1)} %pad_add_fusion.here_ref, bf16[4,256,384]{2,1,0:T(8,128)(2,1)S(1)} %collective-permute-done.6.last, f32[256,512]{1,0:T(8,128)S(1)} %get-tuple-element.97.acc_g, f32[256,512]{1,0:T(8,128)S(1)} %get-tuple-element.98.acc_u, ...), custom_call_target="tpu_custom_call" | custom-call | flops 1048576 | bytes 65536 | tf_op jit(solution)/shard_map/middle/pallas_call | solution.py:208
  54.6 2.4 %middle.3 = (bf16[256,512]{1,0:T(8,128)(2,1)S(1)}, bf16[4,256,384]{2,1,0:T(8,128)(2,1)S(1)}) custom-call(s32[2]{0:T(128)S(1)} %pad_add_fusion.here_ref, bf16[4,256,384]{2,1,0:T(8,128)(2,1)S(1)} %collective-permute-done.9.last, f32[256,512]{1,0:T(8,128)S(1)} %get-tuple-element.103.acc_g, f32[256,512]{1,0:T(8,128)S(1)} %get-tuple-element.104.acc_u, ...), custom_call_target="tpu_custom_call" | custom-call | flops 1048576 | bytes 65536 | tf_op jit(solution)/shard_map/middle/pallas_call | solution.py:208
  57.0 2.1 %collective-permute-start.14 = (bf16[4,256,384]{2,1,0:T(8,128)(2,1)S(1)}, bf16[4,256,384]{2,1,0:T(8,128)(2,1)S(1)}, u32[]{:S(2)}, u32[]{:S(2)}) collective-permute-start(bf16[4,256,384]{2,1,0:T(8,128)(2,1)S(1)} %get-tuple-element.106), channel_id=1, source_target_pairs={{0,4},{1,5},{2,6},{3,7},{4,0},{5,1},{6,2},{7,3},{8,12},{9,13},{10,... | collective-permute-start | bytes 2359304 | tf_op jit(solution)/shard_map/ppermute | solution.py:38
  59.1 2.4 %late.2 = (bf16[4,256,384]{2,1,0:T(8,128)(2,1)S(1)}, f32[4,256,384]{2,1,0:T(8,128)S(1)}, f32[4,256,384]{2,1,0:T(8,128)S(1)}) custom-call(s32[2]{0:T(128)S(1)} %pad_add_fusion.here_ref, bf16[256,512]{1,0:T(8,128)(2,1)S(1)} %get-tuple-element.107.gated, bf16[512,6144]{1,0:T(8,128)(2,1)S(1)} %get-tuple-element.99.wd), custom_call_target="tpu_custom_call" | custom-call | flops 2147483648 | bytes 65536 | tf_op jit(solution)/shard_map/late/pallas_call | solution.py:208
  61.6 4.0 %collective-permute-done.11 = bf16[4,256,384]{2,1,0:T(8,128)(2,1)S(1)} collective-permute-done((bf16[4,256,384]{2,1,0:T(8,128)(2,1)S(1)}, bf16[4,256,384]{2,1,0:T(8,128)(2,1)S(1)}, u32[]{:S(2)}, u32[]{:S(2)}) %collective-permute-start.11) | collective-permute-done | bytes 786464 | tf_op jit(solution)/shard_map/ppermute | solution.py:38
  66.1 2.4 %late.3 = (bf16[4,256,384]{2,1,0:T(8,128)(2,1)S(1)}, f32[4,256,384]{2,1,0:T(8,128)S(1)}, f32[4,256,384]{2,1,0:T(8,128)S(1)}) custom-call(s32[2]{0:T(128)S(1)} %pad_add_fusion.here_ref, bf16[256,512]{1,0:T(8,128)(2,1)S(1)} %get-tuple-element.111.gated, bf16[512,6144]{1,0:T(8,128)(2,1)S(1)} %get-tuple-element.99.wd), custom_call_target="tpu_custom_call" | custom-call | flops 2147483648 | bytes 65536 | tf_op jit(solution)/shard_map/late/pallas_call | solution.py:208
  69.9 2.3 %collective-permute-start.15 = (bf16[4,256,384]{2,1,0:T(8,128)(2,1)S(1)}, bf16[4,256,384]{2,1,0:T(8,128)(2,1)S(1)}, u32[]{:S(2)}, u32[]{:S(2)}) collective-permute-start(bf16[4,256,384]{2,1,0:T(8,128)(2,1)S(1)} %add_convert_fusion), channel_id=1, source_target_pairs={{0,1},{1,0},{2,3},{3,2},{4,5},{5,4},{6,7},{7,6},{8,9},{9,8},{10,11... | collective-permute-start | bytes 2359304 | tf_op jit(solution)/shard_map/ppermute | solution.py:38
  72.3 11.5 %collective-permute-done.12 = bf16[4,256,384]{2,1,0:T(8,128)(2,1)S(1)} collective-permute-done((bf16[4,256,384]{2,1,0:T(8,128)(2,1)S(1)}, bf16[4,256,384]{2,1,0:T(8,128)(2,1)S(1)}, u32[]{:S(2)}, u32[]{:S(2)}) %collective-permute-start.12) | collective-permute-done | bytes 786464 | tf_op jit(solution)/shard_map/ppermute | solution.py:38
  84.0 4.3 %collective-permute-done.13 = bf16[4,256,384]{2,1,0:T(8,128)(2,1)S(1)} collective-permute-done((bf16[4,256,384]{2,1,0:T(8,128)(2,1)S(1)}, bf16[4,256,384]{2,1,0:T(8,128)(2,1)S(1)}, u32[]{:S(2)}, u32[]{:S(2)}) %collective-permute-start.13) | collective-permute-done | bytes 786464 | tf_op jit(solution)/shard_map/ppermute | solution.py:38
  90.4 1.9 %collective-permute-done.16 = bf16[4,256,384]{2,1,0:T(8,128)(2,1)S(1)} collective-permute-done((bf16[4,256,384]{2,1,0:T(8,128)(2,1)S(1)}, bf16[4,256,384]{2,1,0:T(8,128)(2,1)S(1)}, u32[]{:S(2)}, u32[]{:S(2)}) %collective-permute-start.16) | collective-permute-done | bytes 786464 | tf_op jit(solution)/shard_map/ppermute | solution.py:273
  93.9 1.8 %collective-permute-start.18 = (bf16[512,384]{1,0:T(8,128)(2,1)S(1)}, bf16[512,384]{1,0:T(8,128)(2,1)S(1)}, u32[]{:S(2)}, u32[]{:S(2)}) collective-permute-start(bf16[512,384]{1,0:T(8,128)(2,1)S(1)} %pad_maximum_fusion.3), channel_id=1, source_target_pairs={{0,4},{1,5},{2,6},{3,7},{4,0},{5,1},{6,2},{7,3},{8,12},{9,13},{10,... | collective-permute-start | bytes 1179656 | tf_op jit(solution)/shard_map/ppermute | solution.py:38
  95.7 2.1 %collective-permute-start.19 = (bf16[512,384]{1,0:T(8,128)(2,1)S(1)}, bf16[512,384]{1,0:T(8,128)(2,1)S(1)}, u32[]{:S(2)}, u32[]{:S(2)}) collective-permute-start(bf16[512,384]{1,0:T(8,128)(2,1)S(1)} %pad_maximum_fusion.4), channel_id=1, source_target_pairs={{0,5},{1,4},{2,7},{3,6},{4,1},{5,0},{6,3},{7,2},{8,13},{9,12},{10,... | collective-permute-start | bytes 1179656 | tf_op jit(solution)/shard_map/ppermute | solution.py:38
  97.9 2.9 %collective-permute-done.17.na_ref = bf16[512,384]{1,0:T(8,128)(2,1)S(1)} collective-permute-done((bf16[512,384]{1,0:T(8,128)(2,1)S(1)}, bf16[512,384]{1,0:T(8,128)(2,1)S(1)}, u32[]{:S(2)}, u32[]{:S(2)}) %collective-permute-start.17) | collective-permute-done | bytes 393248 | tf_op jit(solution)/shard_map/ppermute | solution.py:38
  100.7 3.9 %collective-permute-done.18.nb_ref = bf16[512,384]{1,0:T(8,128)(2,1)S(1)} collective-permute-done((bf16[512,384]{1,0:T(8,128)(2,1)S(1)}, bf16[512,384]{1,0:T(8,128)(2,1)S(1)}, u32[]{:S(2)}, u32[]{:S(2)}) %collective-permute-start.18) | collective-permute-done | bytes 393248 | tf_op jit(solution)/shard_map/ppermute | solution.py:38
  (51 shorter events, 19.8 us)
Async XLA Ops:
  0.0 1.0 copy-start
  1.0 0.7 copy-start.1
  2.3 8.6 %collective-permute-start = (bf16[512,384]{1,0:T(8,128)(2,1)S(1)}, bf16[512,384]{1,0:T(8,128)(2,1)S(1)}, u32[]{:S(2)}, u32[]{:S(2)}) collective-permute-start(bf16[512,384]{1,0:T(8,128)(2,1)S(1)} %get-tuple-element.65), channel_id=1, source_target_pairs={{0,1},{1,0},{2,3},{3,2},{4,5},{5,4},{6,7},{7,6},{8,9},{9,8},{10,11... | collective-permute-start | bytes 1179656 | tf_op jit(solution)/shard_map/ppermute | solution.py:38
  5.7 11.7 %collective-permute-start.1 = (bf16[512,384]{1,0:T(8,128)(2,1)S(1)}, bf16[512,384]{1,0:T(8,128)(2,1)S(1)}, u32[]{:S(2)}, u32[]{:S(2)}) collective-permute-start(bf16[512,384]{1,0:T(8,128)(2,1)S(1)} %get-tuple-element.65), channel_id=1, source_target_pairs={{0,4},{1,5},{2,6},{3,7},{4,0},{5,1},{6,2},{7,3},{8,12},{9,13},{10,... | collective-permute-start | bytes 1179656 | tf_op jit(solution)/shard_map/ppermute | solution.py:38
  8.4 9.9 %collective-permute-start.2 = (bf16[512,384]{1,0:T(8,128)(2,1)S(1)}, bf16[512,384]{1,0:T(8,128)(2,1)S(1)}, u32[]{:S(2)}, u32[]{:S(2)}) collective-permute-start(bf16[512,384]{1,0:T(8,128)(2,1)S(1)} %get-tuple-element.65), channel_id=1, source_target_pairs={{0,5},{1,4},{2,7},{3,6},{4,1},{5,0},{6,3},{7,2},{8,13},{9,12},{10,... | collective-permute-start | bytes 1179656 | tf_op jit(solution)/shard_map/ppermute | solution.py:38
  18.7 2.4 %collective-permute-start.4 = (bf16[4,256,384]{2,1,0:T(8,128)(2,1)S(1)}, bf16[4,256,384]{2,1,0:T(8,128)(2,1)S(1)}, u32[]{:S(2)}, u32[]{:S(2)}) collective-permute-start(bf16[4,256,384]{2,1,0:T(8,128)(2,1)S(1)} %pad_maximum_fusion.1), channel_id=1, source_target_pairs={{0,16},{16,0},{1,17},{17,1},{2,18},{18,2},{3,19},{19,3},{4,20},{20... | collective-permute-start | bytes 2359304 | tf_op jit(solution)/shard_map/ppermute | solution.py:237
  18.9 14.4 %collective-permute-start.3 = (bf16[4,256,384]{2,1,0:T(8,128)(2,1)S(1)}, bf16[4,256,384]{2,1,0:T(8,128)(2,1)S(1)}, u32[]{:S(2)}, u32[]{:S(2)}) collective-permute-start(bf16[4,256,384]{2,1,0:T(8,128)(2,1)S(1)} %pad_maximum_fusion.held), channel_id=1, source_target_pairs={{0,3},{1,2},{2,1},{3,0},{4,7},{5,6},{6,5},{7,4},{8,11},{9,10},{10,... | collective-permute-start | bytes 2359304 | tf_op jit(solution)/shard_map/ppermute | solution.py:38
  21.1 21.4 %collective-permute-start.7 = (bf16[4,256,384]{2,1,0:T(8,128)(2,1)S(1)}, bf16[4,256,384]{2,1,0:T(8,128)(2,1)S(1)}, u32[]{:S(2)}, u32[]{:S(2)}) collective-permute-start(bf16[4,256,384]{2,1,0:T(8,128)(2,1)S(1)} %pad_maximum_fusion.held), channel_id=1, source_target_pairs={{0,12},{1,13},{2,14},{3,15},{4,8},{5,9},{6,10},{7,11},{8,4},{9,5},... | collective-permute-start | bytes 2359304 | tf_op jit(solution)/shard_map/ppermute | solution.py:38
  21.7 26.3 %collective-permute-start.8 = (bf16[4,256,384]{2,1,0:T(8,128)(2,1)S(1)}, bf16[4,256,384]{2,1,0:T(8,128)(2,1)S(1)}, u32[]{:S(2)}, u32[]{:S(2)}) collective-permute-start(bf16[4,256,384]{2,1,0:T(8,128)(2,1)S(1)} %collective-permute-done.4.held), channel_id=1, source_target_pairs={{0,4},{1,5},{2,6},{3,7},{4,0},{5,1},{6,2},{7,3},{8,12},{9,13},{10,... | collective-permute-start | bytes 2359304 | tf_op jit(solution)/shard_map/ppermute | solution.py:38
  22.9 19.5 %collective-permute-start.5 = (bf16[4,256,384]{2,1,0:T(8,128)(2,1)S(1)}, bf16[4,256,384]{2,1,0:T(8,128)(2,1)S(1)}, u32[]{:S(2)}, u32[]{:S(2)}) collective-permute-start(bf16[4,256,384]{2,1,0:T(8,128)(2,1)S(1)} %collective-permute-done.4.held), channel_id=1, source_target_pairs={{0,1},{1,0},{2,3},{3,2},{4,5},{5,4},{6,7},{7,6},{8,9},{9,8},{10,11... | collective-permute-start | bytes 2359304 | tf_op jit(solution)/shard_map/ppermute | solution.py:38
  25.2 10.1 %copy-start.2 = (s32[512,2]{0,1:T(2,128)S(1)}, s32[512,2]{0,1:T(2,128)}, u32[]{:S(2)}) copy-start(s32[512,2]{0,1:T(2,128)} %param.7) | copy-start | bytes 12292
  25.2 10.1 %copy-start.3 = (f32[512,2]{0,1:T(2,128)S(1)}, f32[512,2]{0,1:T(2,128)}, u32[]{:S(2)}) copy-start(f32[512,2]{0,1:T(2,128)} %param.8) | copy-start | bytes 12292
  33.3 18.7 %collective-permute-start.6 = (bf16[4,256,384]{2,1,0:T(8,128)(2,1)S(1)}, bf16[4,256,384]{2,1,0:T(8,128)(2,1)S(1)}, u32[]{:S(2)}, u32[]{:S(2)}) collective-permute-start(bf16[4,256,384]{2,1,0:T(8,128)(2,1)S(1)} %collective-permute-done.3.third), channel_id=1, source_target_pairs={{0,12},{1,13},{2,14},{3,15},{4,8},{5,9},{6,10},{7,11},{8,4},{9,5},... | collective-permute-start | bytes 2359304 | tf_op jit(solution)/shard_map/ppermute | solution.py:38
  42.5 12.2 %collective-permute-start.9 = (bf16[4,256,384]{2,1,0:T(8,128)(2,1)S(1)}, bf16[4,256,384]{2,1,0:T(8,128)(2,1)S(1)}, u32[]{:S(2)}, u32[]{:S(2)}) collective-permute-start(bf16[4,256,384]{2,1,0:T(8,128)(2,1)S(1)} %collective-permute-done.5.third), channel_id=1, source_target_pairs={{0,4},{1,5},{2,6},{3,7},{4,0},{5,1},{6,2},{7,3},{8,12},{9,13},{10,... | collective-permute-start | bytes 2359304 | tf_op jit(solution)/shard_map/ppermute | solution.py:38
  54.4 11.2 %collective-permute-start.11 = (bf16[4,256,384]{2,1,0:T(8,128)(2,1)S(1)}, bf16[4,256,384]{2,1,0:T(8,128)(2,1)S(1)}, u32[]{:S(2)}, u32[]{:S(2)}) collective-permute-start(bf16[4,256,384]{2,1,0:T(8,128)(2,1)S(1)} %get-tuple-element.101), channel_id=1, source_target_pairs={{0,12},{1,13},{2,14},{3,15},{4,8},{5,9},{6,10},{7,11},{8,4},{9,5},... | collective-permute-start | bytes 2359304 | tf_op jit(solution)/shard_map/ppermute | solution.py:38
  57.0 12.7 %collective-permute-start.14 = (bf16[4,256,384]{2,1,0:T(8,128)(2,1)S(1)}, bf16[4,256,384]{2,1,0:T(8,128)(2,1)S(1)}, u32[]{:S(2)}, u32[]{:S(2)}) collective-permute-start(bf16[4,256,384]{2,1,0:T(8,128)(2,1)S(1)} %get-tuple-element.106), channel_id=1, source_target_pairs={{0,4},{1,5},{2,6},{3,7},{4,0},{5,1},{6,2},{7,3},{8,12},{9,13},{10,... | collective-permute-start | bytes 2359304 | tf_op jit(solution)/shard_map/ppermute | solution.py:38
  61.5 22.3 %collective-permute-start.10 = (bf16[4,256,384]{2,1,0:T(8,128)(2,1)S(1)}, bf16[4,256,384]{2,1,0:T(8,128)(2,1)S(1)}, u32[]{:S(2)}, u32[]{:S(2)}) collective-permute-start(bf16[4,256,384]{2,1,0:T(8,128)(2,1)S(1)} %get-tuple-element.109), channel_id=1, source_target_pairs={{0,12},{1,13},{2,14},{3,15},{4,8},{5,9},{6,10},{7,11},{8,4},{9,5},... | collective-permute-start | bytes 2359304 | tf_op jit(solution)/shard_map/ppermute | solution.py:38
  65.8 18.0 %collective-permute-start.12 = (bf16[4,256,384]{2,1,0:T(8,128)(2,1)S(1)}, bf16[4,256,384]{2,1,0:T(8,128)(2,1)S(1)}, u32[]{:S(2)}, u32[]{:S(2)}) collective-permute-start(bf16[4,256,384]{2,1,0:T(8,128)(2,1)S(1)} %add_convert_fusion.1), channel_id=1, source_target_pairs={{0,3},{1,2},{2,1},{3,0},{4,7},{5,6},{6,5},{7,4},{8,11},{9,10},{10,... | collective-permute-start | bytes 2359304 | tf_op jit(solution)/shard_map/ppermute | solution.py:38
  68.5 19.8 %collective-permute-start.13 = (bf16[4,256,384]{2,1,0:T(8,128)(2,1)S(1)}, bf16[4,256,384]{2,1,0:T(8,128)(2,1)S(1)}, u32[]{:S(2)}, u32[]{:S(2)}) collective-permute-start(bf16[4,256,384]{2,1,0:T(8,128)(2,1)S(1)} %get-tuple-element.113), channel_id=1, source_target_pairs={{0,4},{1,5},{2,6},{3,7},{4,0},{5,1},{6,2},{7,3},{8,12},{9,13},{10,... | collective-permute-start | bytes 2359304 | tf_op jit(solution)/shard_map/ppermute | solution.py:38
  69.9 18.4 %collective-permute-start.15 = (bf16[4,256,384]{2,1,0:T(8,128)(2,1)S(1)}, bf16[4,256,384]{2,1,0:T(8,128)(2,1)S(1)}, u32[]{:S(2)}, u32[]{:S(2)}) collective-permute-start(bf16[4,256,384]{2,1,0:T(8,128)(2,1)S(1)} %add_convert_fusion), channel_id=1, source_target_pairs={{0,1},{1,0},{2,3},{3,2},{4,5},{5,4},{6,7},{7,6},{8,9},{9,8},{10,11... | collective-permute-start | bytes 2359304 | tf_op jit(solution)/shard_map/ppermute | solution.py:38
  88.6 3.7 %collective-permute-start.16 = (bf16[4,256,384]{2,1,0:T(8,128)(2,1)S(1)}, bf16[4,256,384]{2,1,0:T(8,128)(2,1)S(1)}, u32[]{:S(2)}, u32[]{:S(2)}) collective-permute-start(bf16[4,256,384]{2,1,0:T(8,128)(2,1)S(1)} %convert_add_fusion), channel_id=1, source_target_pairs={{0,16},{16,0},{1,17},{17,1},{2,18},{18,2},{3,19},{19,3},{4,20},{20... | collective-permute-start | bytes 2359304 | tf_op jit(solution)/shard_map/ppermute | solution.py:273
  92.7 8.1 %collective-permute-start.17 = (bf16[512,384]{1,0:T(8,128)(2,1)S(1)}, bf16[512,384]{1,0:T(8,128)(2,1)S(1)}, u32[]{:S(2)}, u32[]{:S(2)}) collective-permute-start(bf16[512,384]{1,0:T(8,128)(2,1)S(1)} %pad_maximum_fusion.2), channel_id=1, source_target_pairs={{0,1},{1,0},{2,3},{3,2},{4,5},{5,4},{6,7},{7,6},{8,9},{9,8},{10,11... | collective-permute-start | bytes 1179656 | tf_op jit(solution)/shard_map/ppermute | solution.py:38
  93.9 10.8 %collective-permute-start.18 = (bf16[512,384]{1,0:T(8,128)(2,1)S(1)}, bf16[512,384]{1,0:T(8,128)(2,1)S(1)}, u32[]{:S(2)}, u32[]{:S(2)}) collective-permute-start(bf16[512,384]{1,0:T(8,128)(2,1)S(1)} %pad_maximum_fusion.3), channel_id=1, source_target_pairs={{0,4},{1,5},{2,6},{3,7},{4,0},{5,1},{6,2},{7,3},{8,12},{9,13},{10,... | collective-permute-start | bytes 1179656 | tf_op jit(solution)/shard_map/ppermute | solution.py:38
  95.7 10.4 %collective-permute-start.19 = (bf16[512,384]{1,0:T(8,128)(2,1)S(1)}, bf16[512,384]{1,0:T(8,128)(2,1)S(1)}, u32[]{:S(2)}, u32[]{:S(2)}) collective-permute-start(bf16[512,384]{1,0:T(8,128)(2,1)S(1)} %pad_maximum_fusion.4), channel_id=1, source_target_pairs={{0,5},{1,4},{2,7},{3,6},{4,1},{5,0},{6,3},{7,2},{8,13},{9,12},{10,... | collective-permute-start | bytes 1179656 | tf_op jit(solution)/shard_map/ppermute | solution.py:38

commit v5 on v4

--- a/solution.py
+++ b/solution.py
@@ -235,12 +235,11 @@
     own, oth = [jnp.stack([x[i * cap : (i + 1) * cap] for x in (mine, *near)]) for i in both]
     own, oth = together((own, oth))
     held = [own, lax.ppermute(oth, "expert", SWAP)]
-    third = [exchange(held[i], i, 4) for i in both]
-    held[1], own = together((held[1], own))
-    fourth = [exchange(x, i, 8) for i, x in enumerate((own, held[1]))]
-    own, there, slot = together((own, here, slot))
+    third = together([exchange(x, i, 4) for i, x in enumerate(held)])
+    held, there, slot = together((held, here, slot))
     wg, wu, wd = load(there, wg, wu, wd)
-    third[0], wd = together((third[0], wd))
+    held, wd = together((held, wd))
+    fourth = [exchange(x, i, 8) for i, x in enumerate(held)]
     last = [exchange(x, i, 8) for i, x in enumerate(third)]
     pick, weight = weigh(core, ids, gates, slot)
 
@@ -262,6 +261,9 @@
         token = local_kernel(late_kernel, "late", LATE, i, [(block, bf16)] + [(block, f32)] * 2, here, gated, wd)
         later.append(token)
 
+    (send, keep, rest), other = later
+    keep, other = together((keep, other))
+    later = [(send, keep, rest), other]
     total = []
     for i in both:
         send, keep, rest = later[i]

time: 108 us -> 105 us (0.972)
  waiting for transfers between devices: 49.6 us -> 46.5 us
    ppermute x18, waiting for transfers between devices: 45.9 us -> 42.8 us  [exchange(): return lax.ppermute(value, ('expert', 'tensor'), pairs)]
    ppermute x1, starting transfers between devices: 1.77 us -> 3.26 us  [body(): back = lax.ppermute(oth.astype(bf16), 'expert', SWAP)]
  transfers between devices with their start and end apart: 20 -> 20, of which waited for: 13 -> 14; matrix products, arithmetic and copies ran while one was open for 1% -> 1% of each run, Pallas kernels for 23% -> 24%
where the time goes in v5:
time: 105 us
  waiting for transfers between devices  46.5 us (44%)
  starting transfers between devices  28 us (27%)
  Pallas kernels  26.6 us (25%)
  local copies, waits for them, and re-layouts  2.02 us (2%)
  other arithmetic  1.41 us (1%)
    ppermute x18, waiting for transfers between devices, exchange(): return lax.ppermute(value, ('expert', 'tensor'), pairs)  42.8 us
    ppermute x18, starting transfers between devices, exchange(): return lax.ppermute(value, ('expert', 'tensor'), pairs)  24.7 us
    pallas_call x6, Pallas kernels, local_kernel(): pl.pallas_call(functools.partial(kernel, chain), in_specs=[pl.BlockSpec(m...  17.4 us
    pallas_call x1, Pallas kernels, load(): pl.pallas_call(load_kernel, in_specs=[pl.BlockSpec(memory_space=pltpu.SME...  6.96 us
    ppermute x1, starting transfers between devices, body(): back = lax.ppermute(oth.astype(bf16), 'expert', SWAP)  3.26 us
  transfers between devices with their start and end apart: 20, of which 14 were waited for; matrix products, arithmetic and copies ran while one was open for 1% of the time, Pallas kernels for 24%

profile of v5, /device:TPU:1, one launch (start us, length us, event | category | flops | bytes accessed | tf_op | source)
XLA Modules:
  0.0 104.7 jit_solution(217262500960398305)
XLA Ops:
  2.3 3.4 %collective-permute-start = (bf16[512,384]{1,0:T(8,128)(2,1)S(1)}, bf16[512,384]{1,0:T(8,128)(2,1)S(1)}, u32[]{:S(2)}, u32[]{:S(2)}) collective-permute-start(bf16[512,384]{1,0:T(8,128)(2,1)S(1)} %get-tuple-element.72), channel_id=1, source_target_pairs={{0,1},{1,0},{2,3},{3,2},{4,5},{5,4},{6,7},{7,6},{8,9},{9,8},{10,11... | collective-permute-start | bytes 1179656 | tf_op jit(solution)/shard_map/ppermute | solution.py:38
  5.7 2.7 %collective-permute-start.1 = (bf16[512,384]{1,0:T(8,128)(2,1)S(1)}, bf16[512,384]{1,0:T(8,128)(2,1)S(1)}, u32[]{:S(2)}, u32[]{:S(2)}) collective-permute-start(bf16[512,384]{1,0:T(8,128)(2,1)S(1)} %get-tuple-element.72), channel_id=1, source_target_pairs={{0,4},{1,5},{2,6},{3,7},{4,0},{5,1},{6,2},{7,3},{8,12},{9,13},{10,... | collective-permute-start | bytes 1179656 | tf_op jit(solution)/shard_map/ppermute | solution.py:38
  8.4 2.4 %collective-permute-done = bf16[512,384]{1,0:T(8,128)(2,1)S(1)} collective-permute-done((bf16[512,384]{1,0:T(8,128)(2,1)S(1)}, bf16[512,384]{1,0:T(8,128)(2,1)S(1)}, u32[]{:S(2)}, u32[]{:S(2)}) %collective-permute-start) | collective-permute-done | bytes 393248 | tf_op jit(solution)/shard_map/ppermute | solution.py:38
  10.8 6.5 %collective-permute-done.1 = bf16[512,384]{1,0:T(8,128)(2,1)S(1)} collective-permute-done((bf16[512,384]{1,0:T(8,128)(2,1)S(1)}, bf16[512,384]{1,0:T(8,128)(2,1)S(1)}, u32[]{:S(2)}, u32[]{:S(2)}) %collective-permute-start.1) | collective-permute-done | bytes 393248 | tf_op jit(solution)/shard_map/ppermute | solution.py:38
  21.1 2.1 %collective-permute-start.5 = (bf16[4,256,384]{2,1,0:T(8,128)(2,1)S(1)}, bf16[4,256,384]{2,1,0:T(8,128)(2,1)S(1)}, u32[]{:S(2)}, u32[]{:S(2)}) collective-permute-start(bf16[4,256,384]{2,1,0:T(8,128)(2,1)S(1)} %collective-permute-done.4.held), channel_id=1, source_target_pairs={{0,1},{1,0},{2,3},{3,2},{4,5},{5,4},{6,7},{7,6},{8,9},{9,8},{10,11... | collective-permute-start | bytes 2359304 | tf_op jit(solution)/shard_map/ppermute | solution.py:38
  23.2 7.0 %load.1 = (bf16[6144,512]{1,0:T(8,128)(2,1)S(1)}, bf16[6144,512]{1,0:T(8,128)(2,1)S(1)}, bf16[512,6144]{1,0:T(8,128)(2,1)S(1)}) custom-call(s32[2]{0:T(128)S(1)} %pad_add_fusion.here_ref, bf16[6144,512]{1,0:T(8,128)(2,1)} %bitcast.38, bf16[6144,512]{1,0:T(8,128)(2,1)} %bitcast.39, bf16[512,6144]{1,0:T(8,128)(2,1)} %bitcast.40), custom_call_target="tpu_custom_call" | custom-call | flops 8589934592 | bytes 65536 | tf_op jit(solution)/shard_map/load/pallas_call | solution.py:150
  30.3 2.0 %collective-permute-start.8 = (bf16[4,256,384]{2,1,0:T(8,128)(2,1)S(1)}, bf16[4,256,384]{2,1,0:T(8,128)(2,1)S(1)}, u32[]{:S(2)}, u32[]{:S(2)}) collective-permute-start(bf16[4,256,384]{2,1,0:T(8,128)(2,1)S(1)} %collective-permute-done.4.held), channel_id=1, source_target_pairs={{0,4},{1,5},{2,6},{3,7},{4,0},{5,1},{6,2},{7,3},{8,12},{9,13},{10,... | collective-permute-start | bytes 2359304 | tf_op jit(solution)/shard_map/ppermute | solution.py:38
  33.8 2.1 %collective-permute-start.9 = (bf16[4,256,384]{2,1,0:T(8,128)(2,1)S(1)}, bf16[4,256,384]{2,1,0:T(8,128)(2,1)S(1)}, u32[]{:S(2)}, u32[]{:S(2)}) collective-permute-start(bf16[4,256,384]{2,1,0:T(8,128)(2,1)S(1)} %collective-permute-done.5.third), channel_id=1, source_target_pairs={{0,4},{1,5},{2,6},{3,7},{4,0},{5,1},{6,2},{7,3},{8,12},{9,13},{10,... | collective-permute-start | bytes 2359304 | tf_op jit(solution)/shard_map/ppermute | solution.py:38
  36.3 5.2 %collective-permute-done.7.fourth = bf16[4,256,384]{2,1,0:T(8,128)(2,1)S(1)} collective-permute-done((bf16[4,256,384]{2,1,0:T(8,128)(2,1)S(1)}, bf16[4,256,384]{2,1,0:T(8,128)(2,1)S(1)}, u32[]{:S(2)}, u32[]{:S(2)}) %collective-permute-start.7) | collective-permute-done | bytes 786464 | tf_op jit(solution)/shard_map/ppermute | solution.py:38
  41.5 4.0 %early.2 = (f32[256,512]{1,0:T(8,128)S(1)}, f32[256,512]{1,0:T(8,128)S(1)}) custom-call(s32[2]{0:T(128)S(1)} %pad_add_fusion.here_ref, bf16[4,256,384]{2,1,0:T(8,128)(2,1)S(1)} %pad_maximum_fusion.held, bf16[4,256,384]{2,1,0:T(8,128)(2,1)S(1)} %collective-permute-done.3.third, bf16[4,256,384]{2,1,0:T(8,128)(2,1)S(1)} %collective-permute-done.7.fourth, ...), custom_call_target="tpu_custom_call" | custom-call | flops 4294967296 | bytes 65536 | tf_op jit(solution)/shard_map/early/pallas_call | solution.py:208
  45.5 4.0 %early.3 = (f32[256,512]{1,0:T(8,128)S(1)}, f32[256,512]{1,0:T(8,128)S(1)}) custom-call(s32[2]{0:T(128)S(1)} %pad_add_fusion.here_ref, bf16[4,256,384]{2,1,0:T(8,128)(2,1)S(1)} %collective-permute-done.4.held, bf16[4,256,384]{2,1,0:T(8,128)(2,1)S(1)} %collective-permute-done.5.third, bf16[4,256,384]{2,1,0:T(8,128)(2,1)S(1)} %collective-permute-done.8.fourth, ...), custom_call_target="tpu_custom_call" | custom-call | flops 1048576 | bytes 65536 | tf_op jit(solution)/shard_map/early/pallas_call | solution.py:208
  50.0 2.4 %middle.2 = (bf16[256,512]{1,0:T(8,128)(2,1)S(1)}, bf16[4,256,384]{2,1,0:T(8,128)(2,1)S(1)}) custom-call(s32[2]{0:T(128)S(1)} %pad_add_fusion.here_ref, bf16[4,256,384]{2,1,0:T(8,128)(2,1)S(1)} %collective-permute-done.6.last, f32[256,512]{1,0:T(8,128)S(1)} %get-tuple-element.107.acc_g, f32[256,512]{1,0:T(8,128)S(1)} %get-tuple-element.108.acc_u, ...), custom_call_target="tpu_custom_call" | custom-call | flops 1048576 | bytes 65536 | tf_op jit(solution)/shard_map/middle/pallas_call | solution.py:208
  53.0 2.4 %middle.3 = (bf16[256,512]{1,0:T(8,128)(2,1)S(1)}, bf16[4,256,384]{2,1,0:T(8,128)(2,1)S(1)}) custom-call(s32[2]{0:T(128)S(1)} %pad_add_fusion.here_ref, bf16[4,256,384]{2,1,0:T(8,128)(2,1)S(1)} %collective-permute-done.9.last, f32[256,512]{1,0:T(8,128)S(1)} %get-tuple-element.113.acc_g, f32[256,512]{1,0:T(8,128)S(1)} %get-tuple-element.114.acc_u, ...), custom_call_target="tpu_custom_call" | custom-call | flops 1048576 | bytes 65536 | tf_op jit(solution)/shard_map/middle/pallas_call | solution.py:208
  56.8 2.4 %late.2 = (bf16[4,256,384]{2,1,0:T(8,128)(2,1)S(1)}, f32[4,256,384]{2,1,0:T(8,128)S(1)}, f32[4,256,384]{2,1,0:T(8,128)S(1)}) custom-call(s32[2]{0:T(128)S(1)} %pad_add_fusion.here_ref, bf16[256,512]{1,0:T(8,128)(2,1)S(1)} %get-tuple-element.117.gated, bf16[512,6144]{1,0:T(8,128)(2,1)S(1)} %get-tuple-element.109.wd), custom_call_target="tpu_custom_call" | custom-call | flops 2147483648 | bytes 65536 | tf_op jit(solution)/shard_map/late/pallas_call | solution.py:208
  60.0 2.4 %late.3 = (bf16[4,256,384]{2,1,0:T(8,128)(2,1)S(1)}, f32[4,256,384]{2,1,0:T(8,128)S(1)}, f32[4,256,384]{2,1,0:T(8,128)S(1)}) custom-call(s32[2]{0:T(128)S(1)} %pad_add_fusion.here_ref, bf16[256,512]{1,0:T(8,128)(2,1)S(1)} %get-tuple-element.121.gated, bf16[512,6144]{1,0:T(8,128)(2,1)S(1)} %get-tuple-element.109.wd), custom_call_target="tpu_custom_call" | custom-call | flops 2147483648 | bytes 65536 | tf_op jit(solution)/shard_map/late/pallas_call | solution.py:208
  65.6 2.3 %collective-permute-done.14 = bf16[4,256,384]{2,1,0:T(8,128)(2,1)S(1)} collective-permute-done((bf16[4,256,384]{2,1,0:T(8,128)(2,1)S(1)}, bf16[4,256,384]{2,1,0:T(8,128)(2,1)S(1)}, u32[]{:S(2)}, u32[]{:S(2)}) %collective-permute-start.14) | collective-permute-done | bytes 786464 | tf_op jit(solution)/shard_map/ppermute | solution.py:38
  69.4 2.6 %collective-permute-done.10 = bf16[4,256,384]{2,1,0:T(8,128)(2,1)S(1)} collective-permute-done((bf16[4,256,384]{2,1,0:T(8,128)(2,1)S(1)}, bf16[4,256,384]{2,1,0:T(8,128)(2,1)S(1)}, u32[]{:S(2)}, u32[]{:S(2)}) %collective-permute-start.10) | collective-permute-done | bytes 786464 | tf_op jit(solution)/shard_map/ppermute | solution.py:38
  72.0 11.5 %collective-permute-done.12 = bf16[4,256,384]{2,1,0:T(8,128)(2,1)S(1)} collective-permute-done((bf16[4,256,384]{2,1,0:T(8,128)(2,1)S(1)}, bf16[4,256,384]{2,1,0:T(8,128)(2,1)S(1)}, u32[]{:S(2)}, u32[]{:S(2)}) %collective-permute-start.12) | collective-permute-done | bytes 786464 | tf_op jit(solution)/shard_map/ppermute | solution.py:38
  84.0 3.3 %collective-permute-start.16 = (bf16[4,256,384]{2,1,0:T(8,128)(2,1)S(1)}, bf16[4,256,384]{2,1,0:T(8,128)(2,1)S(1)}, u32[]{:S(2)}, u32[]{:S(2)}) collective-permute-start(bf16[4,256,384]{2,1,0:T(8,128)(2,1)S(1)} %convert_add_fusion), channel_id=1, source_target_pairs={{0,16},{16,0},{1,17},{17,1},{2,18},{18,2},{3,19},{19,3},{4,20},{20... | collective-permute-start | bytes 2359304 | tf_op jit(solution)/shard_map/ppermute | solution.py:275
  87.3 1.9 %collective-permute-done.16 = bf16[4,256,384]{2,1,0:T(8,128)(2,1)S(1)} collective-permute-done((bf16[4,256,384]{2,1,0:T(8,128)(2,1)S(1)}, bf16[4,256,384]{2,1,0:T(8,128)(2,1)S(1)}, u32[]{:S(2)}, u32[]{:S(2)}) %collective-permute-start.16) | collective-permute-done | bytes 786464 | tf_op jit(solution)/shard_map/ppermute | solution.py:275
  89.6 1.8 %collective-permute-start.17 = (bf16[512,384]{1,0:T(8,128)(2,1)S(1)}, bf16[512,384]{1,0:T(8,128)(2,1)S(1)}, u32[]{:S(2)}, u32[]{:S(2)}) collective-permute-start(bf16[512,384]{1,0:T(8,128)(2,1)S(1)} %pad_maximum_fusion.2), channel_id=1, source_target_pairs={{0,1},{1,0},{2,3},{3,2},{4,5},{5,4},{6,7},{7,6},{8,9},{9,8},{10,11... | collective-permute-start | bytes 1179656 | tf_op jit(solution)/shard_map/ppermute | solution.py:38
  92.1 2.7 %collective-permute-start.19 = (bf16[512,384]{1,0:T(8,128)(2,1)S(1)}, bf16[512,384]{1,0:T(8,128)(2,1)S(1)}, u32[]{:S(2)}, u32[]{:S(2)}) collective-permute-start(bf16[512,384]{1,0:T(8,128)(2,1)S(1)} %pad_maximum_fusion.4), channel_id=1, source_target_pairs={{0,5},{1,4},{2,7},{3,6},{4,1},{5,0},{6,3},{7,2},{8,13},{9,12},{10,... | collective-permute-start | bytes 1179656 | tf_op jit(solution)/shard_map/ppermute | solution.py:38
  94.8 2.9 %collective-permute-done.17.na_ref = bf16[512,384]{1,0:T(8,128)(2,1)S(1)} collective-permute-done((bf16[512,384]{1,0:T(8,128)(2,1)S(1)}, bf16[512,384]{1,0:T(8,128)(2,1)S(1)}, u32[]{:S(2)}, u32[]{:S(2)}) %collective-permute-start.17) | collective-permute-done | bytes 393248 | tf_op jit(solution)/shard_map/ppermute | solution.py:38
  97.7 5.8 %collective-permute-done.18.nb_ref = bf16[512,384]{1,0:T(8,128)(2,1)S(1)} collective-permute-done((bf16[512,384]{1,0:T(8,128)(2,1)S(1)}, bf16[512,384]{1,0:T(8,128)(2,1)S(1)}, u32[]{:S(2)}, u32[]{:S(2)}) %collective-permute-start.18) | collective-permute-done | bytes 393248 | tf_op jit(solution)/shard_map/ppermute | solution.py:38
  (51 shorter events, 18.9 us)
Async XLA Ops:
  0.0 1.0 copy-start
  1.0 0.7 copy-start.1
  2.3 8.6 %collective-permute-start = (bf16[512,384]{1,0:T(8,128)(2,1)S(1)}, bf16[512,384]{1,0:T(8,128)(2,1)S(1)}, u32[]{:S(2)}, u32[]{:S(2)}) collective-permute-start(bf16[512,384]{1,0:T(8,128)(2,1)S(1)} %get-tuple-element.72), channel_id=1, source_target_pairs={{0,1},{1,0},{2,3},{3,2},{4,5},{5,4},{6,7},{7,6},{8,9},{9,8},{10,11... | collective-permute-start | bytes 1179656 | tf_op jit(solution)/shard_map/ppermute | solution.py:38
  5.7 11.7 %collective-permute-start.1 = (bf16[512,384]{1,0:T(8,128)(2,1)S(1)}, bf16[512,384]{1,0:T(8,128)(2,1)S(1)}, u32[]{:S(2)}, u32[]{:S(2)}) collective-permute-start(bf16[512,384]{1,0:T(8,128)(2,1)S(1)} %get-tuple-element.72), channel_id=1, source_target_pairs={{0,4},{1,5},{2,6},{3,7},{4,0},{5,1},{6,2},{7,3},{8,12},{9,13},{10,... | collective-permute-start | bytes 1179656 | tf_op jit(solution)/shard_map/ppermute | solution.py:38
  8.4 9.9 %collective-permute-start.2 = (bf16[512,384]{1,0:T(8,128)(2,1)S(1)}, bf16[512,384]{1,0:T(8,128)(2,1)S(1)}, u32[]{:S(2)}, u32[]{:S(2)}) collective-permute-start(bf16[512,384]{1,0:T(8,128)(2,1)S(1)} %get-tuple-element.72), channel_id=1, source_target_pairs={{0,5},{1,4},{2,7},{3,6},{4,1},{5,0},{6,3},{7,2},{8,13},{9,12},{10,... | collective-permute-start | bytes 1179656 | tf_op jit(solution)/shard_map/ppermute | solution.py:38
  18.7 2.4 %collective-permute-start.4 = (bf16[4,256,384]{2,1,0:T(8,128)(2,1)S(1)}, bf16[4,256,384]{2,1,0:T(8,128)(2,1)S(1)}, u32[]{:S(2)}, u32[]{:S(2)}) collective-permute-start(bf16[4,256,384]{2,1,0:T(8,128)(2,1)S(1)} %pad_maximum_fusion.1), channel_id=1, source_target_pairs={{0,16},{16,0},{1,17},{17,1},{2,18},{18,2},{3,19},{19,3},{4,20},{20... | collective-permute-start | bytes 2359304 | tf_op jit(solution)/shard_map/ppermute | solution.py:237
  18.9 13.3 %collective-permute-start.3 = (bf16[4,256,384]{2,1,0:T(8,128)(2,1)S(1)}, bf16[4,256,384]{2,1,0:T(8,128)(2,1)S(1)}, u32[]{:S(2)}, u32[]{:S(2)}) collective-permute-start(bf16[4,256,384]{2,1,0:T(8,128)(2,1)S(1)} %pad_maximum_fusion.held), channel_id=1, source_target_pairs={{0,3},{1,2},{2,1},{3,0},{4,7},{5,6},{6,5},{7,4},{8,11},{9,10},{10,... | collective-permute-start | bytes 2359304 | tf_op jit(solution)/shard_map/ppermute | solution.py:38
  21.1 12.1 %collective-permute-start.5 = (bf16[4,256,384]{2,1,0:T(8,128)(2,1)S(1)}, bf16[4,256,384]{2,1,0:T(8,128)(2,1)S(1)}, u32[]{:S(2)}, u32[]{:S(2)}) collective-permute-start(bf16[4,256,384]{2,1,0:T(8,128)(2,1)S(1)} %collective-permute-done.4.held), channel_id=1, source_target_pairs={{0,1},{1,0},{2,3},{3,2},{4,5},{5,4},{6,7},{7,6},{8,9},{9,8},{10,11... | collective-permute-start | bytes 2359304 | tf_op jit(solution)/shard_map/ppermute | solution.py:38
  23.2 12.7 %copy-start.2 = (s32[512,2]{0,1:T(2,128)S(1)}, s32[512,2]{0,1:T(2,128)}, u32[]{:S(2)}) copy-start(s32[512,2]{0,1:T(2,128)} %param.7) | copy-start | bytes 12292
  23.2 12.7 %copy-start.3 = (f32[512,2]{0,1:T(2,128)S(1)}, f32[512,2]{0,1:T(2,128)}, u32[]{:S(2)}) copy-start(f32[512,2]{0,1:T(2,128)} %param.8) | copy-start | bytes 12292
  30.2 11.4 %collective-permute-start.7 = (bf16[4,256,384]{2,1,0:T(8,128)(2,1)S(1)}, bf16[4,256,384]{2,1,0:T(8,128)(2,1)S(1)}, u32[]{:S(2)}, u32[]{:S(2)}) collective-permute-start(bf16[4,256,384]{2,1,0:T(8,128)(2,1)S(1)} %pad_maximum_fusion.held), channel_id=1, source_target_pairs={{0,12},{1,13},{2,14},{3,15},{4,8},{5,9},{6,10},{7,11},{8,4},{9,5},... | collective-permute-start | bytes 2359304 | tf_op jit(solution)/shard_map/ppermute | solution.py:38
  30.3 15.2 %collective-permute-start.8 = (bf16[4,256,384]{2,1,0:T(8,128)(2,1)S(1)}, bf16[4,256,384]{2,1,0:T(8,128)(2,1)S(1)}, u32[]{:S(2)}, u32[]{:S(2)}) collective-permute-start(bf16[4,256,384]{2,1,0:T(8,128)(2,1)S(1)} %collective-permute-done.4.held), channel_id=1, source_target_pairs={{0,4},{1,5},{2,6},{3,7},{4,0},{5,1},{6,2},{7,3},{8,12},{9,13},{10,... | collective-permute-start | bytes 2359304 | tf_op jit(solution)/shard_map/ppermute | solution.py:38
  33.2 16.8 %collective-permute-start.6 = (bf16[4,256,384]{2,1,0:T(8,128)(2,1)S(1)}, bf16[4,256,384]{2,1,0:T(8,128)(2,1)S(1)}, u32[]{:S(2)}, u32[]{:S(2)}) collective-permute-start(bf16[4,256,384]{2,1,0:T(8,128)(2,1)S(1)} %collective-permute-done.3.third), channel_id=1, source_target_pairs={{0,12},{1,13},{2,14},{3,15},{4,8},{5,9},{6,10},{7,11},{8,4},{9,5},... | collective-permute-start | bytes 2359304 | tf_op jit(solution)/shard_map/ppermute | solution.py:38
  33.8 19.3 %collective-permute-start.9 = (bf16[4,256,384]{2,1,0:T(8,128)(2,1)S(1)}, bf16[4,256,384]{2,1,0:T(8,128)(2,1)S(1)}, u32[]{:S(2)}, u32[]{:S(2)}) collective-permute-start(bf16[4,256,384]{2,1,0:T(8,128)(2,1)S(1)} %collective-permute-done.5.third), channel_id=1, source_target_pairs={{0,4},{1,5},{2,6},{3,7},{4,0},{5,1},{6,2},{7,3},{8,12},{9,13},{10,... | collective-permute-start | bytes 2359304 | tf_op jit(solution)/shard_map/ppermute | solution.py:38
  52.4 11.2 %collective-permute-start.11 = (bf16[4,256,384]{2,1,0:T(8,128)(2,1)S(1)}, bf16[4,256,384]{2,1,0:T(8,128)(2,1)S(1)}, u32[]{:S(2)}, u32[]{:S(2)}) collective-permute-start(bf16[4,256,384]{2,1,0:T(8,128)(2,1)S(1)} %get-tuple-element.111), channel_id=1, source_target_pairs={{0,12},{1,13},{2,14},{3,15},{4,8},{5,9},{6,10},{7,11},{8,4},{9,5},... | collective-permute-start | bytes 2359304 | tf_op jit(solution)/shard_map/ppermute | solution.py:38
  55.4 12.4 %collective-permute-start.14 = (bf16[4,256,384]{2,1,0:T(8,128)(2,1)S(1)}, bf16[4,256,384]{2,1,0:T(8,128)(2,1)S(1)}, u32[]{:S(2)}, u32[]{:S(2)}) collective-permute-start(bf16[4,256,384]{2,1,0:T(8,128)(2,1)S(1)} %get-tuple-element.116), channel_id=1, source_target_pairs={{0,4},{1,5},{2,6},{3,7},{4,0},{5,1},{6,2},{7,3},{8,12},{9,13},{10,... | collective-permute-start | bytes 2359304 | tf_op jit(solution)/shard_map/ppermute | solution.py:38
  59.2 12.9 %collective-permute-start.10 = (bf16[4,256,384]{2,1,0:T(8,128)(2,1)S(1)}, bf16[4,256,384]{2,1,0:T(8,128)(2,1)S(1)}, u32[]{:S(2)}, u32[]{:S(2)}) collective-permute-start(bf16[4,256,384]{2,1,0:T(8,128)(2,1)S(1)} %get-tuple-element.119), channel_id=1, source_target_pairs={{0,12},{1,13},{2,14},{3,15},{4,8},{5,9},{6,10},{7,11},{8,4},{9,5},... | collective-permute-start | bytes 2359304 | tf_op jit(solution)/shard_map/ppermute | solution.py:38
  63.8 19.7 %collective-permute-start.12 = (bf16[4,256,384]{2,1,0:T(8,128)(2,1)S(1)}, bf16[4,256,384]{2,1,0:T(8,128)(2,1)S(1)}, u32[]{:S(2)}, u32[]{:S(2)}) collective-permute-start(bf16[4,256,384]{2,1,0:T(8,128)(2,1)S(1)} %add_convert_fusion.1), channel_id=1, source_target_pairs={{0,3},{1,2},{2,1},{3,0},{4,7},{5,6},{6,5},{7,4},{8,11},{9,10},{10,... | collective-permute-start | bytes 2359304 | tf_op jit(solution)/shard_map/ppermute | solution.py:38
  63.9 19.8 %collective-permute-start.13 = (bf16[4,256,384]{2,1,0:T(8,128)(2,1)S(1)}, bf16[4,256,384]{2,1,0:T(8,128)(2,1)S(1)}, u32[]{:S(2)}, u32[]{:S(2)}) collective-permute-start(bf16[4,256,384]{2,1,0:T(8,128)(2,1)S(1)} %get-tuple-element.127), channel_id=1, source_target_pairs={{0,4},{1,5},{2,6},{3,7},{4,0},{5,1},{6,2},{7,3},{8,12},{9,13},{10,... | collective-permute-start | bytes 2359304 | tf_op jit(solution)/shard_map/ppermute | solution.py:38
  68.1 15.7 %collective-permute-start.15 = (bf16[4,256,384]{2,1,0:T(8,128)(2,1)S(1)}, bf16[4,256,384]{2,1,0:T(8,128)(2,1)S(1)}, u32[]{:S(2)}, u32[]{:S(2)}) collective-permute-start(bf16[4,256,384]{2,1,0:T(8,128)(2,1)S(1)} %add_convert_fusion), channel_id=1, source_target_pairs={{0,1},{1,0},{2,3},{3,2},{4,5},{5,4},{6,7},{7,6},{8,9},{9,8},{10,11... | collective-permute-start | bytes 2359304 | tf_op jit(solution)/shard_map/ppermute | solution.py:38
  84.0 5.2 %collective-permute-start.16 = (bf16[4,256,384]{2,1,0:T(8,128)(2,1)S(1)}, bf16[4,256,384]{2,1,0:T(8,128)(2,1)S(1)}, u32[]{:S(2)}, u32[]{:S(2)}) collective-permute-start(bf16[4,256,384]{2,1,0:T(8,128)(2,1)S(1)} %convert_add_fusion), channel_id=1, source_target_pairs={{0,16},{16,0},{1,17},{17,1},{2,18},{18,2},{3,19},{19,3},{4,20},{20... | collective-permute-start | bytes 2359304 | tf_op jit(solution)/shard_map/ppermute | solution.py:275
  89.6 8.1 %collective-permute-start.17 = (bf16[512,384]{1,0:T(8,128)(2,1)S(1)}, bf16[512,384]{1,0:T(8,128)(2,1)S(1)}, u32[]{:S(2)}, u32[]{:S(2)}) collective-permute-start(bf16[512,384]{1,0:T(8,128)(2,1)S(1)} %pad_maximum_fusion.2), channel_id=1, source_target_pairs={{0,1},{1,0},{2,3},{3,2},{4,5},{5,4},{6,7},{7,6},{8,9},{9,8},{10,11... | collective-permute-start | bytes 1179656 | tf_op jit(solution)/shard_map/ppermute | solution.py:38
  91.4 12.1 %collective-permute-start.18 = (bf16[512,384]{1,0:T(8,128)(2,1)S(1)}, bf16[512,384]{1,0:T(8,128)(2,1)S(1)}, u32[]{:S(2)}, u32[]{:S(2)}) collective-permute-start(bf16[512,384]{1,0:T(8,128)(2,1)S(1)} %pad_maximum_fusion.3), channel_id=1, source_target_pairs={{0,4},{1,5},{2,6},{3,7},{4,0},{5,1},{6,2},{7,3},{8,12},{9,13},{10,... | collective-permute-start | bytes 1179656 | tf_op jit(solution)/shard_map/ppermute | solution.py:38
  92.1 11.4 %collective-permute-start.19 = (bf16[512,384]{1,0:T(8,128)(2,1)S(1)}, bf16[512,384]{1,0:T(8,128)(2,1)S(1)}, u32[]{:S(2)}, u32[]{:S(2)}) collective-permute-start(bf16[512,384]{1,0:T(8,128)(2,1)S(1)} %pad_maximum_fusion.4), channel_id=1, source_target_pairs={{0,5},{1,4},{2,7},{3,6},{4,1},{5,0},{6,3},{7,2},{8,13},{9,12},{10,... | collective-permute-start | bytes 1179656 | tf_op jit(solution)/shard_map/ppermute | solution.py:38

commit v6 on v5

--- a/solution.py
+++ b/solution.py
@@ -11,7 +11,7 @@
 MASKS = (1, 3, 4, 12)
 VMEM_LIMIT = 8 << 20
 LOAD_VMEM = 32 << 20
-LOAD, EARLY, MIDDLE, LATE = 1 << 33, (1 << 32, 1 << 20), 1 << 20, 1 << 31
+LOAD, EARLY, MIDDLE, LATE = 1 << 33, (1 << 32, 1 << 20), 1 << 32, 1 << 20
 
 
 CHAINS = (((0, 2, 1, 3), (1, 3, 0, 2)), ((1, 3, 2, 0), (0, 2, 3, 1)))
@@ -30,15 +30,21 @@
     return me ^ jnp.where(core == 0, mask_of(0, chain, bits), mask_of(1, chain, bits))
 
 
-def exchange(value, chain, bits):
+def exchange(value, chain, bits, cross=False):
     pairs = []
     for core in range(2):
         mask = mask_of(core, chain, bits)
-        pairs += [(core * TENSOR + t, core * TENSOR + (t ^ mask)) for t in range(TENSOR)]
+        target = 1 - core if cross else core
+        pairs += [(core * TENSOR + t, target * TENSOR + (t ^ mask)) for t in range(TENSOR)]
     return lax.ppermute(value, ("expert", "tensor"), pairs)
 
 
 together = lax.optimization_barrier
+
+
+def exchange_pair(values, bits, cross=False):
+    values = together(list(values))
+    return together([exchange(values[i], i, bits, cross and i == 1) for i in range(2)])
 
 
 def dispatch_kernel(core_ref, ids_ref, tok_ref, out_ref, slot_ref):
@@ -191,22 +197,24 @@
         out[k] = y.astype(out.dtype)
 
 
-def middle_kernel(chain, here_ref, last, acc_g, acc_u, wg, wu, wd, gated, send):
-    for cols, g, u in add_blocks(chain, here_ref, [(12, last)], wg, wu, acc_g, acc_u):
-        gated[:, cols] = (g / (1.0 + jnp.exp(-g)) * u).astype(jnp.bfloat16)
-    down_blocks(chain, here_ref, gated, wd, 12, send)
-
-
-def late_kernel(chain, here_ref, gated, wd, send, keep, rest):
-    down_blocks(chain, here_ref, gated, wd, 8, send)
-    down_blocks(chain, here_ref, gated, wd, 4, keep)
-    down_blocks(chain, here_ref, gated, wd, 0, rest)
-
-
-def local_kernel(kernel, name, cost, chain, outs, here, *operands):
-    vmem = pl.BlockSpec(memory_space=pltpu.VMEM)
-    return pl.pallas_call(
-        functools.partial(kernel, chain),
+def middle_kernel(here_ref, la, lb, ga, ua, gb, ub, wg, wu, wd, gated_a, gated_b, send_a, send_b):
+    chains = ((la, ga, ua, gated_a, send_a), (lb, gb, ub, gated_b, send_b))
+    for chain, (last, acc_g, acc_u, gated, send) in enumerate(chains):
+        for cols, g, u in add_blocks(chain, here_ref, [(12, last)], wg, wu, acc_g, acc_u):
+            gated[:, cols] = (g / (1.0 + jnp.exp(-g)) * u).astype(jnp.bfloat16)
+        down_blocks(chain, here_ref, gated, wd, 12, send)
+
+
+def late_kernel(here_ref, gated_a, gated_b, wd, send_a, send_b, keep_a, keep_b, rest_a, rest_b):
+    for first, outs in ((8, (send_a, send_b)), (4, (keep_a, keep_b)), (0, (rest_a, rest_b))):
+        for chain, gated in enumerate((gated_a, gated_b)):
+            down_blocks(chain, here_ref, gated, wd, first, outs[chain])
+
+
+def local_kernel(kernel, name, cost, outs, here, *operands):
+    vmem = pl.BlockSpec(memory_space=pltpu.VMEM)
+    return pl.pallas_call(
+        kernel,
         in_specs=[pl.BlockSpec(memory_space=pltpu.SMEM)] + [vmem] * len(operands),
         out_specs=[vmem] * len(outs),
         out_shape=[jax.ShapeDtypeStruct(shape, dtype) for shape, dtype in outs],
@@ -247,33 +255,21 @@
     early, token = [], ()
     for i in both:
         pieces, token = together(((held[i], third[i], fourth[i]), token))
-        token = local_kernel(early_kernel, "early", EARLY[i], i, [(square, f32)] * 2, here, *pieces, wg, wu)
+        token = local_kernel(
+            functools.partial(early_kernel, i), "early", EARLY[i], [(square, f32)] * 2, here, *pieces, wg, wu
+        )
         early.append(token)
-    middle, later = [], []
-    for i in both:
-        arrived, sums, token = together((last[i], early[i], token))
-        token = local_kernel(
-            middle_kernel, "middle", MIDDLE, i, [(square, bf16), (block, bf16)], here, arrived, *sums, wg, wu, wd
-        )
-        middle.append(token)
-    for i in both:
-        gated, token = together((middle[i][0], token))
-        token = local_kernel(late_kernel, "late", LATE, i, [(block, bf16)] + [(block, f32)] * 2, here, gated, wd)
-        later.append(token)
-
-    (send, keep, rest), other = later
-    keep, other = together((keep, other))
-    later = [(send, keep, rest), other]
-    total = []
-    for i in both:
-        send, keep, rest = later[i]
-        gone = exchange(middle[i][1], i, 8)
-        also = exchange(send, i, 8)
-        second = exchange((keep + gone.astype(f32)).astype(bf16), i, 4)
-        total.append(rest + also.astype(f32) + second.astype(f32))
-    own, oth = together(total)
+    last = together(last)
+    *gated, send_a, send_b = local_kernel(
+        middle_kernel, "middle", MIDDLE, [(square, bf16)] * 2 + [(block, bf16)] * 2, here, *last, *early[0], *early[1], wg, wu, wd
+    )
+    gone = exchange_pair([send_a, send_b], 8)
+    out = local_kernel(late_kernel, "late", LATE, [(block, bf16)] * 2 + [(block, f32)] * 4, here, *gated, wd)
+    also = exchange_pair(out[0:2], 8)
+    second = exchange_pair([(out[2 + i] + gone[i].astype(f32)).astype(bf16) for i in both], 4, cross=True)
+    own, oth = [out[4 + i] + also[i].astype(f32) for i in both]
     back = lax.ppermute(oth.astype(bf16), "expert", SWAP)
-    own, back = together((own, back))
+    own, back = together((own + second[0].astype(f32), (back.astype(f32) + second[1].astype(f32)).astype(bf16)))
     send = [jnp.concatenate([own[bits].astype(bf16), back[bits]]) for bits in (1, 2, 3)]
     send = together(send)
     near = together([exchange(x, 0, bits) for bits, x in zip((1, 2, 3), send)])

time: 105 us -> 102 us (0.971)
  waiting for transfers between devices: 46.5 us -> 39.7 us
  starting transfers between devices: 28 us -> 33.5 us
  Pallas kernels: 26.6 us -> 25.2 us
    ppermute x18, waiting for transfers between devices: 42.8 us -> 37.6 us  [exchange(): return lax.ppermute(value, ('expert', 'tensor'), pairs)]
    ppermute x18, starting transfers between devices: 24.7 us -> 27.8 us  [exchange(): return lax.ppermute(value, ('expert', 'tensor'), pairs)]
    ppermute x1, starting transfers between devices: 3.26 us -> 5.65 us  [body(): back = lax.ppermute(oth.astype(bf16), 'expert', SWAP)]
    ppermute x1, waiting for transfers between devices: 1.91 us -> 0.35 us  [body(): back = lax.ppermute(oth.astype(bf16), 'expert', SWAP)]
    pallas_call x6 -> x4, Pallas kernels: 17.4 us -> 16 us  [local_kernel(): pl.pallas_call(kernel, in_specs=[pl.BlockSpec(memory_space=pltpu.SMEM)] +...]
  transfers between devices with their start and end apart: 20 -> 20, of which waited for: 14 -> 17; matrix products, arithmetic and copies ran while one was open for 1% -> 1% of each run, Pallas kernels for 24% -> 19%
where the time goes in v6:
time: 102 us
  waiting for transfers between devices  39.7 us (39%)
  starting transfers between devices  33.5 us (33%)
  Pallas kernels  25.2 us (25%)
  local copies, waits for them, and re-layouts  2.02 us (2%)
  other arithmetic  1.61 us (2%)
    ppermute x18, waiting for transfers between devices, exchange(): return lax.ppermute(value, ('expert', 'tensor'), pairs)  37.6 us
    ppermute x18, starting transfers between devices, exchange(): return lax.ppermute(value, ('expert', 'tensor'), pairs)  27.8 us
    pallas_call x4, Pallas kernels, local_kernel(): pl.pallas_call(kernel, in_specs=[pl.BlockSpec(memory_space=pltpu.SMEM)] +...  16 us
    pallas_call x1, Pallas kernels, load(): pl.pallas_call(load_kernel, in_specs=[pl.BlockSpec(memory_space=pltpu.SME...  6.96 us
    ppermute x1, starting transfers between devices, body(): back = lax.ppermute(oth.astype(bf16), 'expert', SWAP)  5.65 us
  transfers between devices with their start and end apart: 20, of which 17 were waited for; matrix products, arithmetic and copies ran while one was open for 1% of the time, Pallas kernels for 19%

profile of v6, /device:TPU:1, one launch (start us, length us, event | category | flops | bytes accessed | tf_op | source)
XLA Modules:
  0.0 102.2 jit_solution(17100274267842351038)
XLA Ops:
  2.3 3.4 %collective-permute-start = (bf16[512,384]{1,0:T(8,128)(2,1)S(1)}, bf16[512,384]{1,0:T(8,128)(2,1)S(1)}, u32[]{:S(2)}, u32[]{:S(2)}) collective-permute-start(bf16[512,384]{1,0:T(8,128)(2,1)S(1)} %get-tuple-element.72), channel_id=1, source_target_pairs={{0,1},{1,0},{2,3},{3,2},{4,5},{5,4},{6,7},{7,6},{8,9},{9,8},{10,11... | collective-permute-start | bytes 1179656 | tf_op jit(solution)/shard_map/ppermute | solution.py:39
  5.7 2.7 %collective-permute-start.1 = (bf16[512,384]{1,0:T(8,128)(2,1)S(1)}, bf16[512,384]{1,0:T(8,128)(2,1)S(1)}, u32[]{:S(2)}, u32[]{:S(2)}) collective-permute-start(bf16[512,384]{1,0:T(8,128)(2,1)S(1)} %get-tuple-element.72), channel_id=1, source_target_pairs={{0,4},{1,5},{2,6},{3,7},{4,0},{5,1},{6,2},{7,3},{8,12},{9,13},{10,... | collective-permute-start | bytes 1179656 | tf_op jit(solution)/shard_map/ppermute | solution.py:39
  8.4 2.4 %collective-permute-done = bf16[512,384]{1,0:T(8,128)(2,1)S(1)} collective-permute-done((bf16[512,384]{1,0:T(8,128)(2,1)S(1)}, bf16[512,384]{1,0:T(8,128)(2,1)S(1)}, u32[]{:S(2)}, u32[]{:S(2)}) %collective-permute-start) | collective-permute-done | bytes 393248 | tf_op jit(solution)/shard_map/ppermute | solution.py:39
  10.8 6.5 %collective-permute-done.1 = bf16[512,384]{1,0:T(8,128)(2,1)S(1)} collective-permute-done((bf16[512,384]{1,0:T(8,128)(2,1)S(1)}, bf16[512,384]{1,0:T(8,128)(2,1)S(1)}, u32[]{:S(2)}, u32[]{:S(2)}) %collective-permute-start.1) | collective-permute-done | bytes 393248 | tf_op jit(solution)/shard_map/ppermute | solution.py:39
  19.3 1.8 %collective-permute-done.4.held = bf16[4,256,384]{2,1,0:T(8,128)(2,1)S(1)} collective-permute-done((bf16[4,256,384]{2,1,0:T(8,128)(2,1)S(1)}, bf16[4,256,384]{2,1,0:T(8,128)(2,1)S(1)}, u32[]{:S(2)}, u32[]{:S(2)}) %collective-permute-start.4) | collective-permute-done | bytes 786464 | tf_op jit(solution)/shard_map/ppermute | solution.py:245
  21.1 2.1 %collective-permute-start.5 = (bf16[4,256,384]{2,1,0:T(8,128)(2,1)S(1)}, bf16[4,256,384]{2,1,0:T(8,128)(2,1)S(1)}, u32[]{:S(2)}, u32[]{:S(2)}) collective-permute-start(bf16[4,256,384]{2,1,0:T(8,128)(2,1)S(1)} %collective-permute-done.4.held), channel_id=1, source_target_pairs={{0,1},{1,0},{2,3},{3,2},{4,5},{5,4},{6,7},{7,6},{8,9},{9,8},{10,11... | collective-permute-start | bytes 2359304 | tf_op jit(solution)/shard_map/ppermute | solution.py:39
  23.2 7.0 %load.1 = (bf16[6144,512]{1,0:T(8,128)(2,1)S(1)}, bf16[6144,512]{1,0:T(8,128)(2,1)S(1)}, bf16[512,6144]{1,0:T(8,128)(2,1)S(1)}) custom-call(s32[2]{0:T(128)S(1)} %pad_add_fusion.here_ref, bf16[6144,512]{1,0:T(8,128)(2,1)} %bitcast.38, bf16[6144,512]{1,0:T(8,128)(2,1)} %bitcast.39, bf16[512,6144]{1,0:T(8,128)(2,1)} %bitcast.40), custom_call_target="tpu_custom_call" | custom-call | flops 8589934592 | bytes 65536 | tf_op jit(solution)/shard_map/load/pallas_call | solution.py:156
  30.3 2.0 %collective-permute-start.9 = (bf16[4,256,384]{2,1,0:T(8,128)(2,1)S(1)}, bf16[4,256,384]{2,1,0:T(8,128)(2,1)S(1)}, u32[]{:S(2)}, u32[]{:S(2)}) collective-permute-start(bf16[4,256,384]{2,1,0:T(8,128)(2,1)S(1)} %collective-permute-done.4.held), channel_id=1, source_target_pairs={{0,4},{1,5},{2,6},{3,7},{4,0},{5,1},{6,2},{7,3},{8,12},{9,13},{10,... | collective-permute-start | bytes 2359304 | tf_op jit(solution)/shard_map/ppermute | solution.py:39
  33.8 2.1 %collective-permute-start.7 = (bf16[4,256,384]{2,1,0:T(8,128)(2,1)S(1)}, bf16[4,256,384]{2,1,0:T(8,128)(2,1)S(1)}, u32[]{:S(2)}, u32[]{:S(2)}) collective-permute-start(bf16[4,256,384]{2,1,0:T(8,128)(2,1)S(1)} %collective-permute-done.5.third), channel_id=1, source_target_pairs={{0,4},{1,5},{2,6},{3,7},{4,0},{5,1},{6,2},{7,3},{8,12},{9,13},{10,... | collective-permute-start | bytes 2359304 | tf_op jit(solution)/shard_map/ppermute | solution.py:39
  36.3 5.2 %collective-permute-done.8.fourth = bf16[4,256,384]{2,1,0:T(8,128)(2,1)S(1)} collective-permute-done((bf16[4,256,384]{2,1,0:T(8,128)(2,1)S(1)}, bf16[4,256,384]{2,1,0:T(8,128)(2,1)S(1)}, u32[]{:S(2)}, u32[]{:S(2)}) %collective-permute-start.8) | collective-permute-done | bytes 786464 | tf_op jit(solution)/shard_map/ppermute | solution.py:39
  41.5 4.0 %early.2 = (f32[256,512]{1,0:T(8,128)S(1)}, f32[256,512]{1,0:T(8,128)S(1)}) custom-call(s32[2]{0:T(128)S(1)} %pad_add_fusion.here_ref, bf16[4,256,384]{2,1,0:T(8,128)(2,1)S(1)} %pad_maximum_fusion.held, bf16[4,256,384]{2,1,0:T(8,128)(2,1)S(1)} %collective-permute-done.3.third, bf16[4,256,384]{2,1,0:T(8,128)(2,1)S(1)} %collective-permute-done.8.fourth, ...), custom_call_target="tpu_custom_call" | custom-call | flops 4294967296 | bytes 65536 | tf_op jit(solution)/shard_map/early/pallas_call | solution.py:216
  45.5 4.0 %early.3 = (f32[256,512]{1,0:T(8,128)S(1)}, f32[256,512]{1,0:T(8,128)S(1)}) custom-call(s32[2]{0:T(128)S(1)} %pad_add_fusion.here_ref, bf16[4,256,384]{2,1,0:T(8,128)(2,1)S(1)} %collective-permute-done.4.held, bf16[4,256,384]{2,1,0:T(8,128)(2,1)S(1)} %collective-permute-done.5.third, bf16[4,256,384]{2,1,0:T(8,128)(2,1)S(1)} %collective-permute-done.9.fourth, ...), custom_call_target="tpu_custom_call" | custom-call | flops 1048576 | bytes 65536 | tf_op jit(solution)/shard_map/early/pallas_call | solution.py:216
  50.9 4.1 %middle.1 = (bf16[256,512]{1,0:T(8,128)(2,1)S(1)}, bf16[256,512]{1,0:T(8,128)(2,1)S(1)}, bf16[4,256,384]{2,1,0:T(8,128)(2,1)S(1)}, bf16[4,256,384]{2,1,0:T(8,128)(2,1)S(1)}) custom-call(s32[2]{0:T(128)S(1)} %pad_add_fusion.here_ref, bf16[4,256,384]{2,1,0:T(8,128)(2,1)S(1)} %collective-permute-done.6.la, bf16[4,256,384]{2,1,0:T(8,128)(2,1)S(1)} %collective-permute-done.7.lb, ...), custom_call_target="tpu_custom_call" | custom-call | flops 4294967296 | bytes 65536 | tf_op jit(solution)/shard_map/middle/pallas_call | solution.py:216
  57.0 4.0 %late.1 = (bf16[4,256,384]{2,1,0:T(8,128)(2,1)S(1)}, bf16[4,256,384]{2,1,0:T(8,128)(2,1)S(1)}, f32[4,256,384]{2,1,0:T(8,128)S(1)}, f32[4,256,384]{2,1,0:T(8,128)...) custom-call(s32[2]{0:T(128)S(1)} %pad_add_fusion.here_ref, ...), custom_call_target="tpu_custom_call" | custom-call | flops 1048576 | bytes 65536 | tf_op jit(solution)/shard_map/late/pallas_call | solution.py:216
  62.9 3.2 %collective-permute-done.12 = bf16[4,256,384]{2,1,0:T(8,128)(2,1)S(1)} collective-permute-done((bf16[4,256,384]{2,1,0:T(8,128)(2,1)S(1)}, bf16[4,256,384]{2,1,0:T(8,128)(2,1)S(1)}, u32[]{:S(2)}, u32[]{:S(2)}) %collective-permute-start.12) | collective-permute-done | bytes 786464 | tf_op jit(solution)/shard_map/ppermute | solution.py:39
  66.2 1.7 %collective-permute-done.13 = bf16[4,256,384]{2,1,0:T(8,128)(2,1)S(1)} collective-permute-done((bf16[4,256,384]{2,1,0:T(8,128)(2,1)S(1)}, bf16[4,256,384]{2,1,0:T(8,128)(2,1)S(1)}, u32[]{:S(2)}, u32[]{:S(2)}) %collective-permute-start.13) | collective-permute-done | bytes 786464 | tf_op jit(solution)/shard_map/ppermute | solution.py:39
  68.3 5.1 %collective-permute-start.15 = (bf16[4,256,384]{2,1,0:T(8,128)(2,1)S(1)}, bf16[4,256,384]{2,1,0:T(8,128)(2,1)S(1)}, u32[]{:S(2)}, u32[]{:S(2)}) collective-permute-start(bf16[4,256,384]{2,1,0:T(8,128)(2,1)S(1)} %add_convert_fusion.2), channel_id=1, source_target_pairs={{0,17},{1,16},{2,19},{3,18},{4,21},{5,20},{6,23},{7,22},{8,25},{9,... | collective-permute-start | bytes 2359304 | tf_op jit(solution)/shard_map/ppermute | solution.py:39
  73.4 2.4 %collective-permute-done.10 = bf16[4,256,384]{2,1,0:T(8,128)(2,1)S(1)} collective-permute-done((bf16[4,256,384]{2,1,0:T(8,128)(2,1)S(1)}, bf16[4,256,384]{2,1,0:T(8,128)(2,1)S(1)}, u32[]{:S(2)}, u32[]{:S(2)}) %collective-permute-start.10) | collective-permute-done | bytes 786464 | tf_op jit(solution)/shard_map/ppermute | solution.py:39
  75.8 2.5 %collective-permute-done.11 = bf16[4,256,384]{2,1,0:T(8,128)(2,1)S(1)} collective-permute-done((bf16[4,256,384]{2,1,0:T(8,128)(2,1)S(1)}, bf16[4,256,384]{2,1,0:T(8,128)(2,1)S(1)}, u32[]{:S(2)}, u32[]{:S(2)}) %collective-permute-start.11) | collective-permute-done | bytes 786464 | tf_op jit(solution)/shard_map/ppermute | solution.py:39
  78.5 5.6 %collective-permute-start.16 = (bf16[4,256,384]{2,1,0:T(8,128)(2,1)S(1)}, bf16[4,256,384]{2,1,0:T(8,128)(2,1)S(1)}, u32[]{:S(2)}, u32[]{:S(2)}) collective-permute-start(bf16[4,256,384]{2,1,0:T(8,128)(2,1)S(1)} %add_convert_fusion.1), channel_id=1, source_target_pairs={{0,16},{16,0},{1,17},{17,1},{2,18},{18,2},{3,19},{19,3},{4,20},{20... | collective-permute-start | bytes 2359304 | tf_op jit(solution)/shard_map/ppermute | solution.py:271
  86.7 2.0 %collective-permute-start.17 = (bf16[512,384]{1,0:T(8,128)(2,1)S(1)}, bf16[512,384]{1,0:T(8,128)(2,1)S(1)}, u32[]{:S(2)}, u32[]{:S(2)}) collective-permute-start(bf16[512,384]{1,0:T(8,128)(2,1)S(1)} %pad_maximum_fusion.2), channel_id=1, source_target_pairs={{0,1},{1,0},{2,3},{3,2},{4,5},{5,4},{6,7},{7,6},{8,9},{9,8},{10,11... | collective-permute-start | bytes 1179656 | tf_op jit(solution)/shard_map/ppermute | solution.py:39
  88.7 2.3 %collective-permute-start.18 = (bf16[512,384]{1,0:T(8,128)(2,1)S(1)}, bf16[512,384]{1,0:T(8,128)(2,1)S(1)}, u32[]{:S(2)}, u32[]{:S(2)}) collective-permute-start(bf16[512,384]{1,0:T(8,128)(2,1)S(1)} %pad_maximum_fusion.3), channel_id=1, source_target_pairs={{0,4},{1,5},{2,6},{3,7},{4,0},{5,1},{6,2},{7,3},{8,12},{9,13},{10,... | collective-permute-start | bytes 1179656 | tf_op jit(solution)/shard_map/ppermute | solution.py:39
  91.8 2.9 %collective-permute-done.17.na_ref = bf16[512,384]{1,0:T(8,128)(2,1)S(1)} collective-permute-done((bf16[512,384]{1,0:T(8,128)(2,1)S(1)}, bf16[512,384]{1,0:T(8,128)(2,1)S(1)}, u32[]{:S(2)}, u32[]{:S(2)}) %collective-permute-start.17) | collective-permute-done | bytes 393248 | tf_op jit(solution)/shard_map/ppermute | solution.py:39
  94.7 5.2 %collective-permute-done.18.nb_ref = bf16[512,384]{1,0:T(8,128)(2,1)S(1)} collective-permute-done((bf16[512,384]{1,0:T(8,128)(2,1)S(1)}, bf16[512,384]{1,0:T(8,128)(2,1)S(1)}, u32[]{:S(2)}, u32[]{:S(2)}) %collective-permute-start.18) | collective-permute-done | bytes 393248 | tf_op jit(solution)/shard_map/ppermute | solution.py:39
  (50 shorter events, 17.8 us)
Async XLA Ops:
  0.0 1.0 copy-start
  1.0 0.7 copy-start.1
  2.3 8.6 %collective-permute-start = (bf16[512,384]{1,0:T(8,128)(2,1)S(1)}, bf16[512,384]{1,0:T(8,128)(2,1)S(1)}, u32[]{:S(2)}, u32[]{:S(2)}) collective-permute-start(bf16[512,384]{1,0:T(8,128)(2,1)S(1)} %get-tuple-element.72), channel_id=1, source_target_pairs={{0,1},{1,0},{2,3},{3,2},{4,5},{5,4},{6,7},{7,6},{8,9},{9,8},{10,11... | collective-permute-start | bytes 1179656 | tf_op jit(solution)/shard_map/ppermute | solution.py:39
  5.7 11.7 %collective-permute-start.1 = (bf16[512,384]{1,0:T(8,128)(2,1)S(1)}, bf16[512,384]{1,0:T(8,128)(2,1)S(1)}, u32[]{:S(2)}, u32[]{:S(2)}) collective-permute-start(bf16[512,384]{1,0:T(8,128)(2,1)S(1)} %get-tuple-element.72), channel_id=1, source_target_pairs={{0,4},{1,5},{2,6},{3,7},{4,0},{5,1},{6,2},{7,3},{8,12},{9,13},{10,... | collective-permute-start | bytes 1179656 | tf_op jit(solution)/shard_map/ppermute | solution.py:39
  8.4 9.9 %collective-permute-start.2 = (bf16[512,384]{1,0:T(8,128)(2,1)S(1)}, bf16[512,384]{1,0:T(8,128)(2,1)S(1)}, u32[]{:S(2)}, u32[]{:S(2)}) collective-permute-start(bf16[512,384]{1,0:T(8,128)(2,1)S(1)} %get-tuple-element.72), channel_id=1, source_target_pairs={{0,5},{1,4},{2,7},{3,6},{4,1},{5,0},{6,3},{7,2},{8,13},{9,12},{10,... | collective-permute-start | bytes 1179656 | tf_op jit(solution)/shard_map/ppermute | solution.py:39
  18.7 2.4 %collective-permute-start.4 = (bf16[4,256,384]{2,1,0:T(8,128)(2,1)S(1)}, bf16[4,256,384]{2,1,0:T(8,128)(2,1)S(1)}, u32[]{:S(2)}, u32[]{:S(2)}) collective-permute-start(bf16[4,256,384]{2,1,0:T(8,128)(2,1)S(1)} %pad_maximum_fusion.1), channel_id=1, source_target_pairs={{0,16},{16,0},{1,17},{17,1},{2,18},{18,2},{3,19},{19,3},{4,20},{20... | collective-permute-start | bytes 2359304 | tf_op jit(solution)/shard_map/ppermute | solution.py:245
  18.9 13.3 %collective-permute-start.3 = (bf16[4,256,384]{2,1,0:T(8,128)(2,1)S(1)}, bf16[4,256,384]{2,1,0:T(8,128)(2,1)S(1)}, u32[]{:S(2)}, u32[]{:S(2)}) collective-permute-start(bf16[4,256,384]{2,1,0:T(8,128)(2,1)S(1)} %pad_maximum_fusion.held), channel_id=1, source_target_pairs={{0,3},{1,2},{2,1},{3,0},{4,7},{5,6},{6,5},{7,4},{8,11},{9,10},{10,... | collective-permute-start | bytes 2359304 | tf_op jit(solution)/shard_map/ppermute | solution.py:39
  21.1 12.1 %collective-permute-start.5 = (bf16[4,256,384]{2,1,0:T(8,128)(2,1)S(1)}, bf16[4,256,384]{2,1,0:T(8,128)(2,1)S(1)}, u32[]{:S(2)}, u32[]{:S(2)}) collective-permute-start(bf16[4,256,384]{2,1,0:T(8,128)(2,1)S(1)} %collective-permute-done.4.held), channel_id=1, source_target_pairs={{0,1},{1,0},{2,3},{3,2},{4,5},{5,4},{6,7},{7,6},{8,9},{9,8},{10,11... | collective-permute-start | bytes 2359304 | tf_op jit(solution)/shard_map/ppermute | solution.py:39
  23.2 12.7 %copy-start.2 = (s32[512,2]{0,1:T(2,128)S(1)}, s32[512,2]{0,1:T(2,128)}, u32[]{:S(2)}) copy-start(s32[512,2]{0,1:T(2,128)} %param.7) | copy-start | bytes 12292
  23.2 12.7 %copy-start.3 = (f32[512,2]{0,1:T(2,128)S(1)}, f32[512,2]{0,1:T(2,128)}, u32[]{:S(2)}) copy-start(f32[512,2]{0,1:T(2,128)} %param.8) | copy-start | bytes 12292
  30.2 11.4 %collective-permute-start.8 = (bf16[4,256,384]{2,1,0:T(8,128)(2,1)S(1)}, bf16[4,256,384]{2,1,0:T(8,128)(2,1)S(1)}, u32[]{:S(2)}, u32[]{:S(2)}) collective-permute-start(bf16[4,256,384]{2,1,0:T(8,128)(2,1)S(1)} %pad_maximum_fusion.held), channel_id=1, source_target_pairs={{0,12},{1,13},{2,14},{3,15},{4,8},{5,9},{6,10},{7,11},{8,4},{9,5},... | collective-permute-start | bytes 2359304 | tf_op jit(solution)/shard_map/ppermute | solution.py:39
  30.3 15.2 %collective-permute-start.9 = (bf16[4,256,384]{2,1,0:T(8,128)(2,1)S(1)}, bf16[4,256,384]{2,1,0:T(8,128)(2,1)S(1)}, u32[]{:S(2)}, u32[]{:S(2)}) collective-permute-start(bf16[4,256,384]{2,1,0:T(8,128)(2,1)S(1)} %collective-permute-done.4.held), channel_id=1, source_target_pairs={{0,4},{1,5},{2,6},{3,7},{4,0},{5,1},{6,2},{7,3},{8,12},{9,13},{10,... | collective-permute-start | bytes 2359304 | tf_op jit(solution)/shard_map/ppermute | solution.py:39
  33.2 16.8 %collective-permute-start.6 = (bf16[4,256,384]{2,1,0:T(8,128)(2,1)S(1)}, bf16[4,256,384]{2,1,0:T(8,128)(2,1)S(1)}, u32[]{:S(2)}, u32[]{:S(2)}) collective-permute-start(bf16[4,256,384]{2,1,0:T(8,128)(2,1)S(1)} %collective-permute-done.3.third), channel_id=1, source_target_pairs={{0,12},{1,13},{2,14},{3,15},{4,8},{5,9},{6,10},{7,11},{8,4},{9,5},... | collective-permute-start | bytes 2359304 | tf_op jit(solution)/shard_map/ppermute | solution.py:39
  33.8 17.1 %collective-permute-start.7 = (bf16[4,256,384]{2,1,0:T(8,128)(2,1)S(1)}, bf16[4,256,384]{2,1,0:T(8,128)(2,1)S(1)}, u32[]{:S(2)}, u32[]{:S(2)}) collective-permute-start(bf16[4,256,384]{2,1,0:T(8,128)(2,1)S(1)} %collective-permute-done.5.third), channel_id=1, source_target_pairs={{0,4},{1,5},{2,6},{3,7},{4,0},{5,1},{6,2},{7,3},{8,12},{9,13},{10,... | collective-permute-start | bytes 2359304 | tf_op jit(solution)/shard_map/ppermute | solution.py:39
  54.9 11.2 %collective-permute-start.12 = (bf16[4,256,384]{2,1,0:T(8,128)(2,1)S(1)}, bf16[4,256,384]{2,1,0:T(8,128)(2,1)S(1)}, u32[]{:S(2)}, u32[]{:S(2)}) collective-permute-start(bf16[4,256,384]{2,1,0:T(8,128)(2,1)S(1)} %get-tuple-element.120), channel_id=1, source_target_pairs={{0,12},{1,13},{2,14},{3,15},{4,8},{5,9},{6,10},{7,11},{8,4},{9,5},... | collective-permute-start | bytes 2359304 | tf_op jit(solution)/shard_map/ppermute | solution.py:39
  55.5 12.3 %collective-permute-start.13 = (bf16[4,256,384]{2,1,0:T(8,128)(2,1)S(1)}, bf16[4,256,384]{2,1,0:T(8,128)(2,1)S(1)}, u32[]{:S(2)}, u32[]{:S(2)}) collective-permute-start(bf16[4,256,384]{2,1,0:T(8,128)(2,1)S(1)} %get-tuple-element.121), channel_id=1, source_target_pairs={{0,4},{1,5},{2,6},{3,7},{4,0},{5,1},{6,2},{7,3},{8,12},{9,13},{10,... | collective-permute-start | bytes 2359304 | tf_op jit(solution)/shard_map/ppermute | solution.py:39
  61.0 14.8 %collective-permute-start.10 = (bf16[4,256,384]{2,1,0:T(8,128)(2,1)S(1)}, bf16[4,256,384]{2,1,0:T(8,128)(2,1)S(1)}, u32[]{:S(2)}, u32[]{:S(2)}) collective-permute-start(bf16[4,256,384]{2,1,0:T(8,128)(2,1)S(1)} %get-tuple-element.114), channel_id=1, source_target_pairs={{0,12},{1,13},{2,14},{3,15},{4,8},{5,9},{6,10},{7,11},{8,4},{9,5},... | collective-permute-start | bytes 2359304 | tf_op jit(solution)/shard_map/ppermute | solution.py:39
  62.1 16.2 %collective-permute-start.11 = (bf16[4,256,384]{2,1,0:T(8,128)(2,1)S(1)}, bf16[4,256,384]{2,1,0:T(8,128)(2,1)S(1)}, u32[]{:S(2)}, u32[]{:S(2)}) collective-permute-start(bf16[4,256,384]{2,1,0:T(8,128)(2,1)S(1)} %get-tuple-element.115), channel_id=1, source_target_pairs={{0,4},{1,5},{2,6},{3,7},{4,0},{5,1},{6,2},{7,3},{8,12},{9,13},{10,... | collective-permute-start | bytes 2359304 | tf_op jit(solution)/shard_map/ppermute | solution.py:39
  68.2 17.2 %collective-permute-start.14 = (bf16[4,256,384]{2,1,0:T(8,128)(2,1)S(1)}, bf16[4,256,384]{2,1,0:T(8,128)(2,1)S(1)}, u32[]{:S(2)}, u32[]{:S(2)}) collective-permute-start(bf16[4,256,384]{2,1,0:T(8,128)(2,1)S(1)} %add_convert_fusion.3), channel_id=1, source_target_pairs={{0,3},{1,2},{2,1},{3,0},{4,7},{5,6},{6,5},{7,4},{8,11},{9,10},{10,... | collective-permute-start | bytes 2359304 | tf_op jit(solution)/shard_map/ppermute | solution.py:39
  68.3 17.1 %collective-permute-start.15 = (bf16[4,256,384]{2,1,0:T(8,128)(2,1)S(1)}, bf16[4,256,384]{2,1,0:T(8,128)(2,1)S(1)}, u32[]{:S(2)}, u32[]{:S(2)}) collective-permute-start(bf16[4,256,384]{2,1,0:T(8,128)(2,1)S(1)} %add_convert_fusion.2), channel_id=1, source_target_pairs={{0,17},{1,16},{2,19},{3,18},{4,21},{5,20},{6,23},{7,22},{8,25},{9,... | collective-permute-start | bytes 2359304 | tf_op jit(solution)/shard_map/ppermute | solution.py:39
  78.5 7.6 %collective-permute-start.16 = (bf16[4,256,384]{2,1,0:T(8,128)(2,1)S(1)}, bf16[4,256,384]{2,1,0:T(8,128)(2,1)S(1)}, u32[]{:S(2)}, u32[]{:S(2)}) collective-permute-start(bf16[4,256,384]{2,1,0:T(8,128)(2,1)S(1)} %add_convert_fusion.1), channel_id=1, source_target_pairs={{0,16},{16,0},{1,17},{17,1},{2,18},{18,2},{3,19},{19,3},{4,20},{20... | collective-permute-start | bytes 2359304 | tf_op jit(solution)/shard_map/ppermute | solution.py:271
  86.7 8.1 %collective-permute-start.17 = (bf16[512,384]{1,0:T(8,128)(2,1)S(1)}, bf16[512,384]{1,0:T(8,128)(2,1)S(1)}, u32[]{:S(2)}, u32[]{:S(2)}) collective-permute-start(bf16[512,384]{1,0:T(8,128)(2,1)S(1)} %pad_maximum_fusion.2), channel_id=1, source_target_pairs={{0,1},{1,0},{2,3},{3,2},{4,5},{5,4},{6,7},{7,6},{8,9},{9,8},{10,11... | collective-permute-start | bytes 1179656 | tf_op jit(solution)/shard_map/ppermute | solution.py:39
  88.7 11.2 %collective-permute-start.18 = (bf16[512,384]{1,0:T(8,128)(2,1)S(1)}, bf16[512,384]{1,0:T(8,128)(2,1)S(1)}, u32[]{:S(2)}, u32[]{:S(2)}) collective-permute-start(bf16[512,384]{1,0:T(8,128)(2,1)S(1)} %pad_maximum_fusion.3), channel_id=1, source_target_pairs={{0,4},{1,5},{2,6},{3,7},{4,0},{5,1},{6,2},{7,3},{8,12},{9,13},{10,... | collective-permute-start | bytes 1179656 | tf_op jit(solution)/shard_map/ppermute | solution.py:39
  91.0 9.9 %collective-permute-start.19 = (bf16[512,384]{1,0:T(8,128)(2,1)S(1)}, bf16[512,384]{1,0:T(8,128)(2,1)S(1)}, u32[]{:S(2)}, u32[]{:S(2)}) collective-permute-start(bf16[512,384]{1,0:T(8,128)(2,1)S(1)} %pad_maximum_fusion.4), channel_id=1, source_target_pairs={{0,5},{1,4},{2,7},{3,6},{4,1},{5,0},{6,3},{7,2},{8,13},{9,12},{10,... | collective-permute-start | bytes 1179656 | tf_op jit(solution)/shard_map/ppermute | solution.py:39

commit v7 on v6

--- a/solution.py
+++ b/solution.py
@@ -47,7 +47,11 @@
     return together([exchange(values[i], i, bits, cross and i == 1) for i in range(2)])
 
 
-def dispatch_kernel(core_ref, ids_ref, tok_ref, out_ref, slot_ref):
+def dispatch_kernel(core_ref, ids_hbm, tok_hbm, out_ref, slot_ref, ids_ref, tok_ref, sem):
+    ids_copy = pltpu.make_async_copy(ids_hbm, ids_ref, sem.at[0])
+    tok_copy = pltpu.make_async_copy(tok_hbm, tok_ref, sem.at[1])
+    ids_copy.start()
+    tok_copy.start()
     rows = tok_ref.shape[0]
     cap = out_ref.shape[0] // 2
     core = core_ref[0]
@@ -57,11 +61,13 @@
     ).astype(jnp.bfloat16)
     kind = lax.broadcasted_iota(jnp.int32, (kinds, rows), 0)
     wanted = jnp.where(kind == 0, core, jnp.where(kind == 1, 1 - core, -1))
+    ids_copy.wait()
     match = ((ids_ref[0:1, :] == wanted) | (ids_ref[1:2, :] == wanted)).astype(jnp.bfloat16)
     earlier = jnp.dot(match, tri, preferred_element_type=jnp.float32).astype(jnp.int32)
     slot = jnp.where(match > 0, earlier, -1)
     slot_ref[...] = slot
     slots = lax.broadcasted_iota(jnp.int32, (cap, rows), 0)
+    tok_copy.wait()
     for k in range(2):
         onehot = (slot[k : k + 1, :] == slots).astype(jnp.bfloat16)
         picked = jnp.dot(onehot, tok_ref[...], preferred_element_type=jnp.float32)
@@ -71,15 +77,20 @@
 def dispatch(core, ids, tokens):
     rows, width = tokens.shape
     vmem = pl.BlockSpec(memory_space=pltpu.VMEM)
+    hbm = pl.BlockSpec(memory_space=pl.ANY)
     return pl.pallas_call(
         dispatch_kernel,
-        in_specs=[pl.BlockSpec(memory_space=pltpu.SMEM), vmem, vmem],
+        in_specs=[pl.BlockSpec(memory_space=pltpu.SMEM), hbm, hbm],
         out_specs=[vmem, vmem],
         out_shape=[
             jax.ShapeDtypeStruct((rows, width), jnp.bfloat16),
             jax.ShapeDtypeStruct((16, rows), jnp.int32),
         ],
-        compiler_params=pltpu.CompilerParams(vmem_limit_bytes=VMEM_LIMIT),
+        scratch_shapes=[
+            pltpu.VMEM(ids.shape, ids.dtype),
+            pltpu.VMEM(tokens.shape, tokens.dtype),
+            pltpu.SemaphoreType.DMA((2,)),
+        ],
         name="dispatch",
     )(core, ids, tokens)
 

time: 102 us -> 103 us (level)
  Pallas kernels: 25.2 us -> 26.8 us
    unnamed x8 -> x6, local copies, waits for them, and re-layouts: 1.69 us -> 0.01 us
    pallas_call x1, Pallas kernels: 0.57 us -> 2.22 us  [dispatch(): pl.pallas_call(dispatch_kernel, in_specs=[pl.BlockSpec(memory_space=pltpu...]
    another operation x3, local copies, waits for them, and re-layouts: 0.16 us -> 1.19 us  [body(): jnp.stack([x[i * cap:(i + 1) * cap] for x in (mine, *near)])]
  transfers between devices with their start and end apart: 20 -> 20, of which waited for: 17 -> 17; matrix products, arithmetic and copies ran while one was open for 1% -> 2% of each run, Pallas kernels for 19% -> 19%
where the time goes in v7:
time: 103 us; the launch traced here: 102 us
  waiting for transfers between devices  38.9 us (38%)
  starting transfers between devices  33.5 us (33%)
  Pallas kernels  26.8 us (26%)
  other arithmetic  1.61 us (2%)
  local copies, waits for them, and re-layouts  1.37 us (1%)
    ppermute x18, waiting for transfers between devices, exchange(): return lax.ppermute(value, ('expert', 'tensor'), pairs)  36.7 us
    ppermute x18, starting transfers between devices, exchange(): return lax.ppermute(value, ('expert', 'tensor'), pairs)  27.7 us
    pallas_call x4, Pallas kernels, local_kernel(): pl.pallas_call(kernel, in_specs=[pl.BlockSpec(memory_space=pltpu.SMEM)] +...  16 us
    pallas_call x1, Pallas kernels, load(): pl.pallas_call(load_kernel, in_specs=[pl.BlockSpec(memory_space=pltpu.SME...  6.96 us
    ppermute x1, starting transfers between devices, body(): back = lax.ppermute(oth.astype(bf16), 'expert', SWAP)  5.64 us
    pallas_call x1, Pallas kernels, dispatch(): pl.pallas_call(dispatch_kernel, in_specs=[pl.BlockSpec(memory_space=pltpu...  2.22 us
  transfers between devices with their start and end apart: 20, of which 17 were waited for; matrix products, arithmetic and copies ran while one was open for 2% of the time, Pallas kernels for 19%

profile of v7, /device:TPU:1, one launch (start us, length us, event | category | flops | bytes accessed | tf_op | source)
XLA Modules:
  0.0 102.4 jit_solution(15953177406691277335)
XLA Ops:
  0.0 2.2 %dispatch.1 = (bf16[512,384]{1,0:T(8,128)(2,1)}, s32[16,512]{1,0:T(8,128)}) custom-call(s32[1]{0:T(128)} %bitcast.core_ref, s32[2,512]{1,0:T(2,128)} %bitcast.35, bf16[512,384]{1,0:T(8,128)(2,1)} %tok_hbm.1), custom_call_target="tpu_custom_call" | custom-call | tf_op jit(solution)/shard_map/dispatch/pallas_call | solution.py:81
  2.2 3.4 %collective-permute-start = (bf16[512,384]{1,0:T(8,128)(2,1)}, bf16[512,384]{1,0:T(8,128)(2,1)S(1)}, u32[]{:S(2)}, u32[]{:S(2)}) collective-permute-start(bf16[512,384]{1,0:T(8,128)(2,1)} %get-tuple-element.72), channel_id=1, source_target_pairs={{0,1},{1,0},{2,3},{3,2},{4,5},{5,4},{6,7},{7,6},{8,9},{9,8},{10,11... | collective-permute-start | bytes 1179656 | tf_op jit(solution)/shard_map/ppermute | solution.py:39
  5.6 2.7 %collective-permute-start.1 = (bf16[512,384]{1,0:T(8,128)(2,1)}, bf16[512,384]{1,0:T(8,128)(2,1)S(1)}, u32[]{:S(2)}, u32[]{:S(2)}) collective-permute-start(bf16[512,384]{1,0:T(8,128)(2,1)} %get-tuple-element.72), channel_id=1, source_target_pairs={{0,4},{1,5},{2,6},{3,7},{4,0},{5,1},{6,2},{7,3},{8,12},{9,13},{10,... | collective-permute-start | bytes 1179656 | tf_op jit(solution)/shard_map/ppermute | solution.py:39
  11.0 6.6 %collective-permute-done.1 = bf16[512,384]{1,0:T(8,128)(2,1)S(1)} collective-permute-done((bf16[512,384]{1,0:T(8,128)(2,1)}, bf16[512,384]{1,0:T(8,128)(2,1)S(1)}, u32[]{:S(2)}, u32[]{:S(2)}) %collective-permute-start.1) | collective-permute-done | bytes 393248 | tf_op jit(solution)/shard_map/ppermute | solution.py:39
  19.5 1.8 %collective-permute-done.4.held = bf16[4,256,384]{2,1,0:T(8,128)(2,1)S(1)} collective-permute-done((bf16[4,256,384]{2,1,0:T(8,128)(2,1)S(1)}, bf16[4,256,384]{2,1,0:T(8,128)(2,1)S(1)}, u32[]{:S(2)}, u32[]{:S(2)}) %collective-permute-start.4) | collective-permute-done | bytes 786464 | tf_op jit(solution)/shard_map/ppermute | solution.py:256
  21.3 2.1 %collective-permute-start.5 = (bf16[4,256,384]{2,1,0:T(8,128)(2,1)S(1)}, bf16[4,256,384]{2,1,0:T(8,128)(2,1)S(1)}, u32[]{:S(2)}, u32[]{:S(2)}) collective-permute-start(bf16[4,256,384]{2,1,0:T(8,128)(2,1)S(1)} %collective-permute-done.4.held), channel_id=1, source_target_pairs={{0,1},{1,0},{2,3},{3,2},{4,5},{5,4},{6,7},{7,6},{8,9},{9,8},{10,11... | collective-permute-start | bytes 2359304 | tf_op jit(solution)/shard_map/ppermute | solution.py:39
  23.4 7.0 %load.1 = (bf16[6144,512]{1,0:T(8,128)(2,1)S(1)}, bf16[6144,512]{1,0:T(8,128)(2,1)S(1)}, bf16[512,6144]{1,0:T(8,128)(2,1)S(1)}) custom-call(s32[2]{0:T(128)S(1)} %pad_add_fusion.here_ref, bf16[6144,512]{1,0:T(8,128)(2,1)} %bitcast.38, bf16[6144,512]{1,0:T(8,128)(2,1)} %bitcast.39, bf16[512,6144]{1,0:T(8,128)(2,1)} %bitcast.40), custom_call_target="tpu_custom_call" | custom-call | flops 8589934592 | bytes 65536 | tf_op jit(solution)/shard_map/load/pallas_call | solution.py:167
  30.5 2.0 %collective-permute-start.9 = (bf16[4,256,384]{2,1,0:T(8,128)(2,1)S(1)}, bf16[4,256,384]{2,1,0:T(8,128)(2,1)S(1)}, u32[]{:S(2)}, u32[]{:S(2)}) collective-permute-start(bf16[4,256,384]{2,1,0:T(8,128)(2,1)S(1)} %collective-permute-done.4.held), channel_id=1, source_target_pairs={{0,4},{1,5},{2,6},{3,7},{4,0},{5,1},{6,2},{7,3},{8,12},{9,13},{10,... | collective-permute-start | bytes 2359304 | tf_op jit(solution)/shard_map/ppermute | solution.py:39
  34.0 2.2 %collective-permute-start.7 = (bf16[4,256,384]{2,1,0:T(8,128)(2,1)S(1)}, bf16[4,256,384]{2,1,0:T(8,128)(2,1)S(1)}, u32[]{:S(2)}, u32[]{:S(2)}) collective-permute-start(bf16[4,256,384]{2,1,0:T(8,128)(2,1)S(1)} %collective-permute-done.5.third), channel_id=1, source_target_pairs={{0,4},{1,5},{2,6},{3,7},{4,0},{5,1},{6,2},{7,3},{8,12},{9,13},{10,... | collective-permute-start | bytes 2359304 | tf_op jit(solution)/shard_map/ppermute | solution.py:39
  36.5 5.2 %collective-permute-done.8.fourth = bf16[4,256,384]{2,1,0:T(8,128)(2,1)S(1)} collective-permute-done((bf16[4,256,384]{2,1,0:T(8,128)(2,1)S(1)}, bf16[4,256,384]{2,1,0:T(8,128)(2,1)S(1)}, u32[]{:S(2)}, u32[]{:S(2)}) %collective-permute-start.8) | collective-permute-done | bytes 786464 | tf_op jit(solution)/shard_map/ppermute | solution.py:39
  41.7 4.0 %early.2 = (f32[256,512]{1,0:T(8,128)S(1)}, f32[256,512]{1,0:T(8,128)S(1)}) custom-call(s32[2]{0:T(128)S(1)} %pad_add_fusion.here_ref, bf16[4,256,384]{2,1,0:T(8,128)(2,1)S(1)} %pad_maximum_fusion.held, bf16[4,256,384]{2,1,0:T(8,128)(2,1)S(1)} %collective-permute-done.3.third, bf16[4,256,384]{2,1,0:T(8,128)(2,1)S(1)} %collective-permute-done.8.fourth, ...), custom_call_target="tpu_custom_call" | custom-call | flops 4294967296 | bytes 65536 | tf_op jit(solution)/shard_map/early/pallas_call | solution.py:227
  45.7 4.0 %early.3 = (f32[256,512]{1,0:T(8,128)S(1)}, f32[256,512]{1,0:T(8,128)S(1)}) custom-call(s32[2]{0:T(128)S(1)} %pad_add_fusion.here_ref, bf16[4,256,384]{2,1,0:T(8,128)(2,1)S(1)} %collective-permute-done.4.held, bf16[4,256,384]{2,1,0:T(8,128)(2,1)S(1)} %collective-permute-done.5.third, bf16[4,256,384]{2,1,0:T(8,128)(2,1)S(1)} %collective-permute-done.9.fourth, ...), custom_call_target="tpu_custom_call" | custom-call | flops 1048576 | bytes 65536 | tf_op jit(solution)/shard_map/early/pallas_call | solution.py:227
  51.0 4.1 %middle.1 = (bf16[256,512]{1,0:T(8,128)(2,1)S(1)}, bf16[256,512]{1,0:T(8,128)(2,1)S(1)}, bf16[4,256,384]{2,1,0:T(8,128)(2,1)S(1)}, bf16[4,256,384]{2,1,0:T(8,128)(2,1)S(1)}) custom-call(s32[2]{0:T(128)S(1)} %pad_add_fusion.here_ref, bf16[4,256,384]{2,1,0:T(8,128)(2,1)S(1)} %collective-permute-done.6.la, bf16[4,256,384]{2,1,0:T(8,128)(2,1)S(1)} %collective-permute-done.7.lb, ...), custom_call_target="tpu_custom_call" | custom-call | flops 4294967296 | bytes 65536 | tf_op jit(solution)/shard_map/middle/pallas_call | solution.py:227
  57.2 4.0 %late.1 = (bf16[4,256,384]{2,1,0:T(8,128)(2,1)S(1)}, bf16[4,256,384]{2,1,0:T(8,128)(2,1)S(1)}, f32[4,256,384]{2,1,0:T(8,128)S(1)}, f32[4,256,384]{2,1,0:T(8,128)...) custom-call(s32[2]{0:T(128)S(1)} %pad_add_fusion.here_ref, ...), custom_call_target="tpu_custom_call" | custom-call | flops 1048576 | bytes 65536 | tf_op jit(solution)/shard_map/late/pallas_call | solution.py:227
  63.1 3.2 %collective-permute-done.12 = bf16[4,256,384]{2,1,0:T(8,128)(2,1)S(1)} collective-permute-done((bf16[4,256,384]{2,1,0:T(8,128)(2,1)S(1)}, bf16[4,256,384]{2,1,0:T(8,128)(2,1)S(1)}, u32[]{:S(2)}, u32[]{:S(2)}) %collective-permute-start.12) | collective-permute-done | bytes 786464 | tf_op jit(solution)/shard_map/ppermute | solution.py:39
  66.3 1.7 %collective-permute-done.13 = bf16[4,256,384]{2,1,0:T(8,128)(2,1)S(1)} collective-permute-done((bf16[4,256,384]{2,1,0:T(8,128)(2,1)S(1)}, bf16[4,256,384]{2,1,0:T(8,128)(2,1)S(1)}, u32[]{:S(2)}, u32[]{:S(2)}) %collective-permute-start.13) | collective-permute-done | bytes 786464 | tf_op jit(solution)/shard_map/ppermute | solution.py:39
  68.5 5.1 %collective-permute-start.15 = (bf16[4,256,384]{2,1,0:T(8,128)(2,1)S(1)}, bf16[4,256,384]{2,1,0:T(8,128)(2,1)S(1)}, u32[]{:S(2)}, u32[]{:S(2)}) collective-permute-start(bf16[4,256,384]{2,1,0:T(8,128)(2,1)S(1)} %add_convert_fusion.2), channel_id=1, source_target_pairs={{0,17},{1,16},{2,19},{3,18},{4,21},{5,20},{6,23},{7,22},{8,25},{9,... | collective-permute-start | bytes 2359304 | tf_op jit(solution)/shard_map/ppermute | solution.py:39
  73.6 2.4 %collective-permute-done.10 = bf16[4,256,384]{2,1,0:T(8,128)(2,1)S(1)} collective-permute-done((bf16[4,256,384]{2,1,0:T(8,128)(2,1)S(1)}, bf16[4,256,384]{2,1,0:T(8,128)(2,1)S(1)}, u32[]{:S(2)}, u32[]{:S(2)}) %collective-permute-start.10) | collective-permute-done | bytes 786464 | tf_op jit(solution)/shard_map/ppermute | solution.py:39
  76.0 2.5 %collective-permute-done.11 = bf16[4,256,384]{2,1,0:T(8,128)(2,1)S(1)} collective-permute-done((bf16[4,256,384]{2,1,0:T(8,128)(2,1)S(1)}, bf16[4,256,384]{2,1,0:T(8,128)(2,1)S(1)}, u32[]{:S(2)}, u32[]{:S(2)}) %collective-permute-start.11) | collective-permute-done | bytes 786464 | tf_op jit(solution)/shard_map/ppermute | solution.py:39
  78.7 5.6 %collective-permute-start.16 = (bf16[4,256,384]{2,1,0:T(8,128)(2,1)S(1)}, bf16[4,256,384]{2,1,0:T(8,128)(2,1)S(1)}, u32[]{:S(2)}, u32[]{:S(2)}) collective-permute-start(bf16[4,256,384]{2,1,0:T(8,128)(2,1)S(1)} %add_convert_fusion.1), channel_id=1, source_target_pairs={{0,16},{16,0},{1,17},{17,1},{2,18},{18,2},{3,19},{19,3},{4,20},{20... | collective-permute-start | bytes 2359304 | tf_op jit(solution)/shard_map/ppermute | solution.py:282
  86.8 2.0 %collective-permute-start.17 = (bf16[512,384]{1,0:T(8,128)(2,1)S(1)}, bf16[512,384]{1,0:T(8,128)(2,1)S(1)}, u32[]{:S(2)}, u32[]{:S(2)}) collective-permute-start(bf16[512,384]{1,0:T(8,128)(2,1)S(1)} %pad_maximum_fusion.2), channel_id=1, source_target_pairs={{0,1},{1,0},{2,3},{3,2},{4,5},{5,4},{6,7},{7,6},{8,9},{9,8},{10,11... | collective-permute-start | bytes 1179656 | tf_op jit(solution)/shard_map/ppermute | solution.py:39
  88.9 2.3 %collective-permute-start.18 = (bf16[512,384]{1,0:T(8,128)(2,1)S(1)}, bf16[512,384]{1,0:T(8,128)(2,1)S(1)}, u32[]{:S(2)}, u32[]{:S(2)}) collective-permute-start(bf16[512,384]{1,0:T(8,128)(2,1)S(1)} %pad_maximum_fusion.3), channel_id=1, source_target_pairs={{0,4},{1,5},{2,6},{3,7},{4,0},{5,1},{6,2},{7,3},{8,12},{9,13},{10,... | collective-permute-start | bytes 1179656 | tf_op jit(solution)/shard_map/ppermute | solution.py:39
  92.0 2.9 %collective-permute-done.17.na_ref = bf16[512,384]{1,0:T(8,128)(2,1)S(1)} collective-permute-done((bf16[512,384]{1,0:T(8,128)(2,1)S(1)}, bf16[512,384]{1,0:T(8,128)(2,1)S(1)}, u32[]{:S(2)}, u32[]{:S(2)}) %collective-permute-start.17) | collective-permute-done | bytes 393248 | tf_op jit(solution)/shard_map/ppermute | solution.py:39
  94.9 5.2 %collective-permute-done.18.nb_ref = bf16[512,384]{1,0:T(8,128)(2,1)S(1)} collective-permute-done((bf16[512,384]{1,0:T(8,128)(2,1)S(1)}, bf16[512,384]{1,0:T(8,128)(2,1)S(1)}, u32[]{:S(2)}, u32[]{:S(2)}) %collective-permute-start.18) | collective-permute-done | bytes 393248 | tf_op jit(solution)/shard_map/ppermute | solution.py:39
  (48 shorter events, 18.1 us)
Async XLA Ops:
  2.2 8.8 %collective-permute-start = (bf16[512,384]{1,0:T(8,128)(2,1)}, bf16[512,384]{1,0:T(8,128)(2,1)S(1)}, u32[]{:S(2)}, u32[]{:S(2)}) collective-permute-start(bf16[512,384]{1,0:T(8,128)(2,1)} %get-tuple-element.72), channel_id=1, source_target_pairs={{0,1},{1,0},{2,3},{3,2},{4,5},{5,4},{6,7},{7,6},{8,9},{9,8},{10,11... | collective-permute-start | bytes 1179656 | tf_op jit(solution)/shard_map/ppermute | solution.py:39
  5.6 12.0 %collective-permute-start.1 = (bf16[512,384]{1,0:T(8,128)(2,1)}, bf16[512,384]{1,0:T(8,128)(2,1)S(1)}, u32[]{:S(2)}, u32[]{:S(2)}) collective-permute-start(bf16[512,384]{1,0:T(8,128)(2,1)} %get-tuple-element.72), channel_id=1, source_target_pairs={{0,4},{1,5},{2,6},{3,7},{4,0},{5,1},{6,2},{7,3},{8,12},{9,13},{10,... | collective-permute-start | bytes 1179656 | tf_op jit(solution)/shard_map/ppermute | solution.py:39
  8.4 10.2 %collective-permute-start.2 = (bf16[512,384]{1,0:T(8,128)(2,1)}, bf16[512,384]{1,0:T(8,128)(2,1)S(1)}, u32[]{:S(2)}, u32[]{:S(2)}) collective-permute-start(bf16[512,384]{1,0:T(8,128)(2,1)} %get-tuple-element.72), channel_id=1, source_target_pairs={{0,5},{1,4},{2,7},{3,6},{4,1},{5,0},{6,3},{7,2},{8,13},{9,12},{10,... | collective-permute-start | bytes 1179656 | tf_op jit(solution)/shard_map/ppermute | solution.py:39
  18.9 2.4 %collective-permute-start.4 = (bf16[4,256,384]{2,1,0:T(8,128)(2,1)S(1)}, bf16[4,256,384]{2,1,0:T(8,128)(2,1)S(1)}, u32[]{:S(2)}, u32[]{:S(2)}) collective-permute-start(bf16[4,256,384]{2,1,0:T(8,128)(2,1)S(1)} %pad_maximum_fusion.1), channel_id=1, source_target_pairs={{0,16},{16,0},{1,17},{17,1},{2,18},{18,2},{3,19},{19,3},{4,20},{20... | collective-permute-start | bytes 2359304 | tf_op jit(solution)/shard_map/ppermute | solution.py:256
  19.1 13.3 %collective-permute-start.3 = (bf16[4,256,384]{2,1,0:T(8,128)(2,1)S(1)}, bf16[4,256,384]{2,1,0:T(8,128)(2,1)S(1)}, u32[]{:S(2)}, u32[]{:S(2)}) collective-permute-start(bf16[4,256,384]{2,1,0:T(8,128)(2,1)S(1)} %pad_maximum_fusion.held), channel_id=1, source_target_pairs={{0,3},{1,2},{2,1},{3,0},{4,7},{5,6},{6,5},{7,4},{8,11},{9,10},{10,... | collective-permute-start | bytes 2359304 | tf_op jit(solution)/shard_map/ppermute | solution.py:39
  21.3 12.1 %collective-permute-start.5 = (bf16[4,256,384]{2,1,0:T(8,128)(2,1)S(1)}, bf16[4,256,384]{2,1,0:T(8,128)(2,1)S(1)}, u32[]{:S(2)}, u32[]{:S(2)}) collective-permute-start(bf16[4,256,384]{2,1,0:T(8,128)(2,1)S(1)} %collective-permute-done.4.held), channel_id=1, source_target_pairs={{0,1},{1,0},{2,3},{3,2},{4,5},{5,4},{6,7},{7,6},{8,9},{9,8},{10,11... | collective-permute-start | bytes 2359304 | tf_op jit(solution)/shard_map/ppermute | solution.py:39
  23.4 12.7 %copy-start = (s32[512,2]{0,1:T(2,128)S(1)}, s32[512,2]{0,1:T(2,128)}, u32[]{:S(2)}) copy-start(s32[512,2]{0,1:T(2,128)} %param.7) | copy-start | bytes 12292
  23.4 12.7 %copy-start.1 = (s32[16,512]{1,0:T(8,128)S(1)}, s32[16,512]{1,0:T(8,128)}, u32[]{:S(2)}) copy-start(s32[16,512]{1,0:T(8,128)} %get-tuple-element.81.slot_ref) | copy-start | bytes 98308
  23.4 12.7 %copy-start.2 = (f32[512,2]{0,1:T(2,128)S(1)}, f32[512,2]{0,1:T(2,128)}, u32[]{:S(2)}) copy-start(f32[512,2]{0,1:T(2,128)} %param.8) | copy-start | bytes 12292
  30.4 11.4 %collective-permute-start.8 = (bf16[4,256,384]{2,1,0:T(8,128)(2,1)S(1)}, bf16[4,256,384]{2,1,0:T(8,128)(2,1)S(1)}, u32[]{:S(2)}, u32[]{:S(2)}) collective-permute-start(bf16[4,256,384]{2,1,0:T(8,128)(2,1)S(1)} %pad_maximum_fusion.held), channel_id=1, source_target_pairs={{0,12},{1,13},{2,14},{3,15},{4,8},{5,9},{6,10},{7,11},{8,4},{9,5},... | collective-permute-start | bytes 2359304 | tf_op jit(solution)/shard_map/ppermute | solution.py:39
  30.5 15.2 %collective-permute-start.9 = (bf16[4,256,384]{2,1,0:T(8,128)(2,1)S(1)}, bf16[4,256,384]{2,1,0:T(8,128)(2,1)S(1)}, u32[]{:S(2)}, u32[]{:S(2)}) collective-permute-start(bf16[4,256,384]{2,1,0:T(8,128)(2,1)S(1)} %collective-permute-done.4.held), channel_id=1, source_target_pairs={{0,4},{1,5},{2,6},{3,7},{4,0},{5,1},{6,2},{7,3},{8,12},{9,13},{10,... | collective-permute-start | bytes 2359304 | tf_op jit(solution)/shard_map/ppermute | solution.py:39
  33.3 16.8 %collective-permute-start.6 = (bf16[4,256,384]{2,1,0:T(8,128)(2,1)S(1)}, bf16[4,256,384]{2,1,0:T(8,128)(2,1)S(1)}, u32[]{:S(2)}, u32[]{:S(2)}) collective-permute-start(bf16[4,256,384]{2,1,0:T(8,128)(2,1)S(1)} %collective-permute-done.3.third), channel_id=1, source_target_pairs={{0,12},{1,13},{2,14},{3,15},{4,8},{5,9},{6,10},{7,11},{8,4},{9,5},... | collective-permute-start | bytes 2359304 | tf_op jit(solution)/shard_map/ppermute | solution.py:39
  34.0 17.1 %collective-permute-start.7 = (bf16[4,256,384]{2,1,0:T(8,128)(2,1)S(1)}, bf16[4,256,384]{2,1,0:T(8,128)(2,1)S(1)}, u32[]{:S(2)}, u32[]{:S(2)}) collective-permute-start(bf16[4,256,384]{2,1,0:T(8,128)(2,1)S(1)} %collective-permute-done.5.third), channel_id=1, source_target_pairs={{0,4},{1,5},{2,6},{3,7},{4,0},{5,1},{6,2},{7,3},{8,12},{9,13},{10,... | collective-permute-start | bytes 2359304 | tf_op jit(solution)/shard_map/ppermute | solution.py:39
  55.1 11.2 %collective-permute-start.12 = (bf16[4,256,384]{2,1,0:T(8,128)(2,1)S(1)}, bf16[4,256,384]{2,1,0:T(8,128)(2,1)S(1)}, u32[]{:S(2)}, u32[]{:S(2)}) collective-permute-start(bf16[4,256,384]{2,1,0:T(8,128)(2,1)S(1)} %get-tuple-element.120), channel_id=1, source_target_pairs={{0,12},{1,13},{2,14},{3,15},{4,8},{5,9},{6,10},{7,11},{8,4},{9,5},... | collective-permute-start | bytes 2359304 | tf_op jit(solution)/shard_map/ppermute | solution.py:39
  55.7 12.3 %collective-permute-start.13 = (bf16[4,256,384]{2,1,0:T(8,128)(2,1)S(1)}, bf16[4,256,384]{2,1,0:T(8,128)(2,1)S(1)}, u32[]{:S(2)}, u32[]{:S(2)}) collective-permute-start(bf16[4,256,384]{2,1,0:T(8,128)(2,1)S(1)} %get-tuple-element.121), channel_id=1, source_target_pairs={{0,4},{1,5},{2,6},{3,7},{4,0},{5,1},{6,2},{7,3},{8,12},{9,13},{10,... | collective-permute-start | bytes 2359304 | tf_op jit(solution)/shard_map/ppermute | solution.py:39
  61.2 14.8 %collective-permute-start.10 = (bf16[4,256,384]{2,1,0:T(8,128)(2,1)S(1)}, bf16[4,256,384]{2,1,0:T(8,128)(2,1)S(1)}, u32[]{:S(2)}, u32[]{:S(2)}) collective-permute-start(bf16[4,256,384]{2,1,0:T(8,128)(2,1)S(1)} %get-tuple-element.114), channel_id=1, source_target_pairs={{0,12},{1,13},{2,14},{3,15},{4,8},{5,9},{6,10},{7,11},{8,4},{9,5},... | collective-permute-start | bytes 2359304 | tf_op jit(solution)/shard_map/ppermute | solution.py:39
  62.3 16.2 %collective-permute-start.11 = (bf16[4,256,384]{2,1,0:T(8,128)(2,1)S(1)}, bf16[4,256,384]{2,1,0:T(8,128)(2,1)S(1)}, u32[]{:S(2)}, u32[]{:S(2)}) collective-permute-start(bf16[4,256,384]{2,1,0:T(8,128)(2,1)S(1)} %get-tuple-element.115), channel_id=1, source_target_pairs={{0,4},{1,5},{2,6},{3,7},{4,0},{5,1},{6,2},{7,3},{8,12},{9,13},{10,... | collective-permute-start | bytes 2359304 | tf_op jit(solution)/shard_map/ppermute | solution.py:39
  68.4 17.2 %collective-permute-start.14 = (bf16[4,256,384]{2,1,0:T(8,128)(2,1)S(1)}, bf16[4,256,384]{2,1,0:T(8,128)(2,1)S(1)}, u32[]{:S(2)}, u32[]{:S(2)}) collective-permute-start(bf16[4,256,384]{2,1,0:T(8,128)(2,1)S(1)} %add_convert_fusion.3), channel_id=1, source_target_pairs={{0,3},{1,2},{2,1},{3,0},{4,7},{5,6},{6,5},{7,4},{8,11},{9,10},{10,... | collective-permute-start | bytes 2359304 | tf_op jit(solution)/shard_map/ppermute | solution.py:39
  68.5 17.1 %collective-permute-start.15 = (bf16[4,256,384]{2,1,0:T(8,128)(2,1)S(1)}, bf16[4,256,384]{2,1,0:T(8,128)(2,1)S(1)}, u32[]{:S(2)}, u32[]{:S(2)}) collective-permute-start(bf16[4,256,384]{2,1,0:T(8,128)(2,1)S(1)} %add_convert_fusion.2), channel_id=1, source_target_pairs={{0,17},{1,16},{2,19},{3,18},{4,21},{5,20},{6,23},{7,22},{8,25},{9,... | collective-permute-start | bytes 2359304 | tf_op jit(solution)/shard_map/ppermute | solution.py:39
  78.7 7.6 %collective-permute-start.16 = (bf16[4,256,384]{2,1,0:T(8,128)(2,1)S(1)}, bf16[4,256,384]{2,1,0:T(8,128)(2,1)S(1)}, u32[]{:S(2)}, u32[]{:S(2)}) collective-permute-start(bf16[4,256,384]{2,1,0:T(8,128)(2,1)S(1)} %add_convert_fusion.1), channel_id=1, source_target_pairs={{0,16},{16,0},{1,17},{17,1},{2,18},{18,2},{3,19},{19,3},{4,20},{20... | collective-permute-start | bytes 2359304 | tf_op jit(solution)/shard_map/ppermute | solution.py:282
  86.8 8.1 %collective-permute-start.17 = (bf16[512,384]{1,0:T(8,128)(2,1)S(1)}, bf16[512,384]{1,0:T(8,128)(2,1)S(1)}, u32[]{:S(2)}, u32[]{:S(2)}) collective-permute-start(bf16[512,384]{1,0:T(8,128)(2,1)S(1)} %pad_maximum_fusion.2), channel_id=1, source_target_pairs={{0,1},{1,0},{2,3},{3,2},{4,5},{5,4},{6,7},{7,6},{8,9},{9,8},{10,11... | collective-permute-start | bytes 1179656 | tf_op jit(solution)/shard_map/ppermute | solution.py:39
  88.9 11.2 %collective-permute-start.18 = (bf16[512,384]{1,0:T(8,128)(2,1)S(1)}, bf16[512,384]{1,0:T(8,128)(2,1)S(1)}, u32[]{:S(2)}, u32[]{:S(2)}) collective-permute-start(bf16[512,384]{1,0:T(8,128)(2,1)S(1)} %pad_maximum_fusion.3), channel_id=1, source_target_pairs={{0,4},{1,5},{2,6},{3,7},{4,0},{5,1},{6,2},{7,3},{8,12},{9,13},{10,... | collective-permute-start | bytes 1179656 | tf_op jit(solution)/shard_map/ppermute | solution.py:39
  91.2 9.9 %collective-permute-start.19 = (bf16[512,384]{1,0:T(8,128)(2,1)S(1)}, bf16[512,384]{1,0:T(8,128)(2,1)S(1)}, u32[]{:S(2)}, u32[]{:S(2)}) collective-permute-start(bf16[512,384]{1,0:T(8,128)(2,1)S(1)} %pad_maximum_fusion.4), channel_id=1, source_target_pairs={{0,5},{1,4},{2,7},{3,6},{4,1},{5,0},{6,3},{7,2},{8,13},{9,12},{10,... | collective-permute-start | bytes 1179656 | tf_op jit(solution)/shard_map/ppermute | solution.py:39
